TPU v7x, 32 devices: a whole 2x2x4 slice. The times are simulated.
32 devices in a mesh: dp: 8 (over z, y), tensor: 4 (over x, core).
Axes of the slice: x: 2, y: 2, z: 4, core: 2. Of those that a mesh axis runs over, the one named last changes fastest.
Arguments:
- block_input: bfloat16 [8192, 1024], P('dp'), may hold values from -6 to 6
- output_grad: bfloat16 [8192, 1024], P('dp'), may hold values from -6 to 6
- seq_lengths: int32 [4], replicated, may hold values from 1024 to 4096, as said below
- ln1_gain: float32 [1024], replicated, may hold values from 0.5 to 1.5
- ln1_bias: float32 [1024], replicated, may hold values from -3 to 3
- w_qkv: bfloat16 [3, 1024, 1024], P(None, None, 'tensor'), may hold values from -2 to 2
- b_qv: float32 [2, 1024], P(None, 'tensor'), may hold values from -3 to 3
- w_out: bfloat16 [1024, 1024], P('tensor'), may hold values from -4 to 4
- b_out: float32 [1024], replicated, may hold values from -3 to 3
- ln2_gain: float32 [1024], replicated, may hold values from 0.5 to 1.5
- ln2_bias: float32 [1024], replicated, may hold values from -3 to 3
- w_fc: bfloat16 [1024, 4096], P(None, 'tensor'), may hold values from -0.1875 to 0.1875
- b_fc: float32 [4096], P('tensor'), may hold values from -3 to 3
- w_proj: bfloat16 [4096, 1024], P('tensor'), may hold values from -0.09375 to 0.09375
- b_proj: float32 [1024], replicated, may hold values from -3 to 3
Outputs:
- block_output: bfloat16 [8192, 1024], P('dp')
- input_grad: bfloat16 [8192, 1024], P('dp')
- grad_ln1_gain: float32 [1024], replicated
- grad_ln1_bias: float32 [1024], replicated
- grad_w_qkv: float32 [3, 1024, 1024], P(None, None, 'tensor')
- grad_b_qv: float32 [2, 1024], P(None, 'tensor')
- grad_w_out: float32 [1024, 1024], P('tensor')
- grad_b_out: float32 [1024], replicated
- grad_ln2_gain: float32 [1024], replicated
- grad_ln2_bias: float32 [1024], replicated
- grad_w_fc: float32 [1024, 4096], P(None, 'tensor')
- grad_b_fc: float32 [4096], P('tensor')
- grad_w_proj: float32 [4096, 1024], P('tensor')
- grad_b_proj: float32 [1024], replicated
Inputs may be any that keep to these rules, and one draw needn't show every extreme that they name: `seq_lengths`: the 4 sequences lie one after another and fill all 8192 tokens; each has 1024 to 4096 tokens and one has exactly 4096.
All inputs are finite; a program needn't handle non-finite values.
Results may differ from a plain program's by a relative error of at most 0.012.
Values may be sent and summed in bfloat16 or wider, within the bound.
No kernel may reach another device: no remote copies, remote signals or barrier semaphores. Data moves between devices by JAX's collectives and lax.ppermute only.
A program may use at most 256 MiB of HBM per device.

v0:
```python
import jax
import jax.numpy as jnp
from jax import lax
from jax.sharding import PartitionSpec as P

HEAD_DIM = 64
MAXLEN = 4096
QBLOCK = 512
WINDOW = 4608
REACH = 4


def from_behind(value, axis, steps):
    count = lax.axis_size(axis)
    first, last = (max(0, -steps), min(count, count - steps))
    return lax.ppermute(value, axis, [(source, source + steps) for source in range(first, last)])


def norm_rows(values, weight_row, shift_row):
    centred = values - jnp.mean(values, axis=-1, keepdims=True)
    spread = jnp.mean(centred * centred, axis=-1, keepdims=True)
    return centred * lax.rsqrt(spread + 1e-05) * weight_row + shift_row


def gelu_tanh(values):
    return jax.nn.gelu(values, approximate=True)


def segment_of(places, seq_ends):
    return jnp.sum((places[:, None] >= seq_ends[None, :]).astype(jnp.int32), axis=1)


def shift_keys(key_rows, value_rows):
    key_list = [key_rows]
    value_list = [value_rows]
    for offset in range(1, REACH + 1):
        arrived = from_behind((key_rows, value_rows), "dp", offset)
        key_list.insert(0, arrived[0])
        value_list.insert(0, arrived[1])
    return (jnp.concatenate(key_list, 0), jnp.concatenate(value_list, 0))


def per_device(
    block_input,
    output_grad,
    seq_lengths,
    ln1_gain,
    ln1_bias,
    w_qkv,
    b_qv,
    w_out,
    b_out,
    ln2_gain,
    ln2_bias,
    w_fc,
    b_fc,
    w_proj,
    b_proj,
):
    row_count = block_input.shape[0]
    local_width = w_qkv.shape[2]
    head_count = local_width // HEAD_DIM
    block_count = row_count // QBLOCK
    share = row_count // lax.axis_size("tensor")
    share_start = lax.axis_index("tensor") * share
    key_base = REACH * row_count - MAXLEN
    seq_ends = jnp.cumsum(seq_lengths)
    first_row = lax.axis_index("dp") * row_count
    own_place = first_row + jnp.arange(row_count, dtype=jnp.int32)
    key_place = first_row - REACH * row_count + jnp.arange((REACH + 1) * row_count, dtype=jnp.int32)
    own_group = segment_of(own_place, seq_ends)
    key_group = jnp.where(key_place >= 0, segment_of(key_place, seq_ends), -1)

    def allowed_at(query_start, key_start):
        query_place = lax.dynamic_slice_in_dim(own_place, query_start, QBLOCK, 0)
        query_group = lax.dynamic_slice_in_dim(own_group, query_start, QBLOCK, 0)
        window_place = lax.dynamic_slice_in_dim(key_place, key_start, WINDOW, 0)
        window_group = lax.dynamic_slice_in_dim(key_group, key_start, WINDOW, 0)
        return (
            (window_group[None, :] == query_group[:, None])
            & (window_place[None, :] <= query_place[:, None])
            & (window_place[None, :] >= 0)
        )

    x_float = block_input.astype(jnp.float32)
    first_norm = norm_rows(x_float, ln1_gain, ln1_bias)
    first_low = first_norm.astype(jnp.bfloat16)
    query_rows = (
        jnp.dot(first_low, w_qkv[0], preferred_element_type=jnp.float32) + b_qv[0]
    ).astype(jnp.bfloat16)
    key_rows = jnp.dot(first_low, w_qkv[1], preferred_element_type=jnp.float32).astype(jnp.bfloat16)
    value_rows = (
        jnp.dot(first_low, w_qkv[2], preferred_element_type=jnp.float32) + b_qv[1]
    ).astype(jnp.bfloat16)
    all_keys, all_values = shift_keys(key_rows, value_rows)
    query3 = query_rows.reshape(row_count, head_count, HEAD_DIM)
    keys3 = all_keys.reshape((REACH + 1) * row_count, head_count, HEAD_DIM)
    values3 = all_values.reshape((REACH + 1) * row_count, head_count, HEAD_DIM)

    def forward_block(block_id):
        query_start = block_id * QBLOCK
        key_start = key_base + query_start
        query_block = lax.dynamic_slice_in_dim(query3, query_start, QBLOCK, 0)
        key_window = lax.dynamic_slice_in_dim(keys3, key_start, WINDOW, 0)
        value_window = lax.dynamic_slice_in_dim(values3, key_start, WINDOW, 0)
        allowed = allowed_at(query_start, key_start)
        scores = (
            jnp.einsum("qhd,khd->hqk", query_block, key_window, preferred_element_type=jnp.float32)
            * 0.125
        )
        scores = jnp.where(allowed[None], scores, -1e30)
        highest_score = jnp.max(scores, axis=-1, keepdims=True)
        exp_scores = jnp.exp(scores - highest_score)
        totals = jnp.sum(exp_scores, axis=-1, keepdims=True)
        probs = (exp_scores / totals).astype(jnp.bfloat16)
        mixed = jnp.einsum("hqk,khd->qhd", probs, value_window, preferred_element_type=jnp.float32)
        return (mixed, (highest_score + jnp.log(totals))[..., 0])

    heads_out, log_totals = lax.map(forward_block, jnp.arange(block_count, dtype=jnp.int32))
    heads_low = heads_out.reshape(row_count, local_width).astype(jnp.bfloat16)
    attn_share = lax.psum_scatter(
        jnp.dot(heads_low, w_out, preferred_element_type=jnp.float32),
        "tensor",
        scatter_dimension=0,
        tiled=True,
    )
    middle_share = lax.dynamic_slice_in_dim(x_float, share_start, share, 0) + attn_share + b_out
    second_share, second_back = jax.vjp(norm_rows, middle_share, ln2_gain, ln2_bias)
    second_low = lax.all_gather(second_share.astype(jnp.bfloat16), "tensor", axis=0, tiled=True)
    hidden = jnp.dot(second_low, w_fc, preferred_element_type=jnp.float32) + b_fc
    active, gelu_back = jax.vjp(gelu_tanh, hidden)
    active_low = active.astype(jnp.bfloat16)
    feed_share = (
        lax.psum_scatter(
            jnp.dot(active_low, w_proj, preferred_element_type=jnp.float32),
            "tensor",
            scatter_dimension=0,
            tiled=True,
        )
        + b_proj
    )
    output_share = (middle_share + feed_share).astype(jnp.bfloat16)
    feed_grad = output_grad.astype(jnp.float32)
    grad_b_proj = jnp.sum(feed_grad, axis=0)
    grad_w_proj = jnp.einsum(
        "tf,td->fd", active_low, output_grad, preferred_element_type=jnp.float32
    )
    active_grad = jnp.einsum("td,fd->tf", output_grad, w_proj, preferred_element_type=jnp.float32)
    hidden_grad = gelu_back(active_grad)[0].astype(jnp.bfloat16)
    grad_b_fc = jnp.sum(hidden_grad.astype(jnp.float32), axis=0)
    grad_w_fc = jnp.einsum("tc,tf->cf", second_low, hidden_grad, preferred_element_type=jnp.float32)
    second_grad = lax.psum_scatter(
        jnp.einsum("tf,cf->tc", hidden_grad, w_fc, preferred_element_type=jnp.float32),
        "tensor",
        scatter_dimension=0,
        tiled=True,
    )
    middle_part, grad_ln2_gain, grad_ln2_bias = second_back(second_grad)
    middle_grad = lax.dynamic_slice_in_dim(feed_grad, share_start, share, 0) + middle_part
    block_output, branch_grad = (
        lax.all_gather(output_share, "tensor", axis=0, tiled=True),
        lax.all_gather(middle_grad.astype(jnp.bfloat16), "tensor", axis=0, tiled=True),
    )
    grad_b_out = jnp.sum(branch_grad.astype(jnp.float32), axis=0)
    grad_w_out = jnp.einsum("tl,td->ld", heads_low, branch_grad, preferred_element_type=jnp.float32)
    heads_grad = jnp.einsum(
        "td,ld->tl", branch_grad, w_out, preferred_element_type=jnp.float32
    ).astype(jnp.bfloat16)
    heads_grad3 = heads_grad.reshape(row_count, head_count, HEAD_DIM)

    def backward_block(block_id, totals_in):
        query_acc, key_acc, value_acc = totals_in
        query_start = block_id * QBLOCK
        key_start = key_base + query_start
        query_block = lax.dynamic_slice_in_dim(query3, query_start, QBLOCK, 0)
        key_window = lax.dynamic_slice_in_dim(keys3, key_start, WINDOW, 0)
        value_window = lax.dynamic_slice_in_dim(values3, key_start, WINDOW, 0)
        grad_block = lax.dynamic_slice_in_dim(heads_grad3, query_start, QBLOCK, 0)
        allowed = allowed_at(query_start, key_start)
        scores = (
            jnp.einsum("qhd,khd->hqk", query_block, key_window, preferred_element_type=jnp.float32)
            * 0.125
        )
        probs = jnp.where(allowed[None], jnp.exp(scores - log_totals[block_id][..., None]), 0.0)
        probs_low = probs.astype(jnp.bfloat16)
        prob_grad = jnp.einsum(
            "qhd,khd->hqk", grad_block, value_window, preferred_element_type=jnp.float32
        )
        row_dot = jnp.sum(probs * prob_grad, axis=-1, keepdims=True)
        score_grad = (probs * (prob_grad - row_dot)).astype(jnp.bfloat16)
        query_part = (
            jnp.einsum("hqk,khd->qhd", score_grad, key_window, preferred_element_type=jnp.float32)
            * 0.125
        )
        key_part = (
            jnp.einsum("hqk,qhd->khd", score_grad, query_block, preferred_element_type=jnp.float32)
            * 0.125
        )
        value_part = jnp.einsum(
            "hqk,qhd->khd", probs_low, grad_block, preferred_element_type=jnp.float32
        )
        query_acc = lax.dynamic_update_slice_in_dim(query_acc, query_part, query_start, 0)
        key_acc = lax.dynamic_update_slice_in_dim(
            key_acc,
            lax.dynamic_slice_in_dim(key_acc, key_start, WINDOW, 0) + key_part,
            key_start,
            0,
        )
        value_acc = lax.dynamic_update_slice_in_dim(
            value_acc,
            lax.dynamic_slice_in_dim(value_acc, key_start, WINDOW, 0) + value_part,
            key_start,
            0,
        )
        return (query_acc, key_acc, value_acc)

    start_totals = (
        jnp.zeros((row_count, head_count, HEAD_DIM), jnp.float32),
        jnp.zeros(((REACH + 1) * row_count, head_count, HEAD_DIM), jnp.float32),
        jnp.zeros(((REACH + 1) * row_count, head_count, HEAD_DIM), jnp.float32),
    )
    query_acc, key_acc, value_acc = lax.fori_loop(0, block_count, backward_block, start_totals)
    key_acc = key_acc.reshape((REACH + 1) * row_count, local_width)
    value_acc = value_acc.reshape((REACH + 1) * row_count, local_width)
    key_grad = key_acc[REACH * row_count :]
    value_grad = value_acc[REACH * row_count :]
    for offset in range(1, REACH + 1):
        lower_row = (REACH - offset) * row_count
        returned = from_behind(
            (
                key_acc[lower_row : lower_row + row_count],
                value_acc[lower_row : lower_row + row_count],
            ),
            "dp",
            -offset,
        )
        key_grad = key_grad + returned[0]
        value_grad = value_grad + returned[1]
    query_low = query_acc.reshape(row_count, local_width).astype(jnp.bfloat16)
    key_low = key_grad.astype(jnp.bfloat16)
    value_low = value_grad.astype(jnp.bfloat16)
    grad_b_qv = jnp.stack(
        [
            jnp.sum(query_low.astype(jnp.float32), axis=0),
            jnp.sum(value_low.astype(jnp.float32), axis=0),
        ]
    )
    grad_w_qkv = jnp.stack(
        [
            jnp.einsum("tc,tl->cl", first_low, query_low, preferred_element_type=jnp.float32),
            jnp.einsum("tc,tl->cl", first_low, key_low, preferred_element_type=jnp.float32),
            jnp.einsum("tc,tl->cl", first_low, value_low, preferred_element_type=jnp.float32),
        ]
    )
    query_part = query_low
    key_part = key_low
    value_part = value_low
    first_grad = lax.psum_scatter(
        jnp.einsum("tl,cl->tc", query_part, w_qkv[0], preferred_element_type=jnp.float32)
        + jnp.einsum("tl,cl->tc", key_part, w_qkv[1], preferred_element_type=jnp.float32)
        + jnp.einsum("tl,cl->tc", value_part, w_qkv[2], preferred_element_type=jnp.float32),
        "tensor",
        scatter_dimension=0,
        tiled=True,
    )
    first_share_back = jax.vjp(
        norm_rows, lax.dynamic_slice_in_dim(x_float, share_start, share, 0), ln1_gain, ln1_bias
    )[1]
    input_part, gain_share, bias_share = first_share_back(first_grad)
    input_grad = lax.all_gather(
        (middle_grad + input_part).astype(jnp.bfloat16), "tensor", axis=0, tiled=True
    )
    grad_ln1_gain, grad_ln1_bias, grad_ln2_gain, grad_ln2_bias = lax.psum(
        (gain_share, bias_share, grad_ln2_gain, grad_ln2_bias), "tensor"
    )
    (
        grad_ln1_gain,
        grad_ln1_bias,
        grad_w_qkv,
        grad_b_qv,
        grad_w_out,
        grad_b_out,
        grad_ln2_gain,
        grad_ln2_bias,
        grad_w_fc,
        grad_b_fc,
        grad_w_proj,
        grad_b_proj,
    ) = lax.psum(
        (
            grad_ln1_gain,
            grad_ln1_bias,
            grad_w_qkv,
            grad_b_qv,
            grad_w_out,
            grad_b_out,
            grad_ln2_gain,
            grad_ln2_bias,
            grad_w_fc,
            grad_b_fc,
            grad_w_proj,
            grad_b_proj,
        ),
        "dp",
    )
    return (
        block_output,
        input_grad,
        grad_ln1_gain,
        grad_ln1_bias,
        grad_w_qkv,
        grad_b_qv,
        grad_w_out,
        grad_b_out,
        grad_ln2_gain,
        grad_ln2_bias,
        grad_w_fc,
        grad_b_fc,
        grad_w_proj,
        grad_b_proj,
    )


def solution(mesh):
    placed = (
        P("dp", None),
        P("dp", None),
        P(),
        P(),
        P(),
        P(None, None, "tensor"),
        P(None, "tensor"),
        P("tensor", None),
        P(),
        P(),
        P(),
        P(None, "tensor"),
        P("tensor"),
        P("tensor", None),
        P(),
    )
    return jax.shard_map(
        per_device,
        mesh=mesh,
        in_specs=placed,
        out_specs=(
            P("dp", None),
            P("dp", None),
            P(),
            P(),
            P(None, None, "tensor"),
            P(None, "tensor"),
            P("tensor", None),
            P(),
            P(),
            P(),
            P(None, "tensor"),
            P("tensor"),
            P("tensor", None),
            P(),
        ),
        check_vma=False,
    )
```

profile of v0, /device:TPU:0, one launch (start us, length us, event | category | flops | bytes accessed | tf_op | source)
XLA Modules:
  0.0 1547.3 jit_solution(17745022627665904959)
XLA Ops:
  37.2 22.2 %collective-permute-start.5 = (bf16[1024,256]{1,0:T(8,128)(2,1)S(1)}, bf16[1024,256]{1,0:T(8,128)(2,1)}, u32[]{:S(2)}, u32[]{:S(2)}) collective-permute-start(bf16[1024,256]{1,0:T(8,128)(2,1)S(1)} %convolution_convert_fusion.1), channel_id=1, source_target_pairs={{0,12},{4,16},{8,20},{12,24},{16,28},{1,13},{5,17},{9,21},{13,25},... | collective-permute-start | bytes 1572872 | tf_op jit(solution)/shard_map/ppermute | solution.py:16
  99.7 111.2 %while.29 = (s32[]{:T(128)}, bf16[2,512,4,64]{1,3,2,0:T(8,128)(2,1)}, f32[2,4,512]{2,1,0:T(4,128)S(1)}, s32[2]{0:T(128)S(1)}, bf16[5120,4,64]{0,2,1:T(8,128)(2,1...) while((s32[]{:T(128)}, ...), condition=%wide.region_8.9_spmd, body=%wide.region_5.8_spmd.sunk | while | flops 2538605056 | bytes 138872624 | solution.py:119
  103.8 17.6 %fusion.155 = (f32[4,512]{1,0:T(4,128)S(1)}, f32[4,512,4608]{2,1,0:T(8,128)}) fusion(pred[512,4608]{1,0:T(8,128)(4,1)S(1)} %and_and_fusion.4, bf16[5120,4,64]{0,2,1:T(8,128)(2,1)} %get-tuple-element.628, s32[]{:T(128)S(6)} %select_n.105, bf16[1024,4,64]{0,2,1:T(8,128)(2,1)S(1)} %get-tuple-element.627, s32[]{:T(128)S(6)} %select_n.106), kind=kOutput, calls=%fused_computation.3.clone.1 | convolution fusion | flops 1236269056 | bytes 42737672 | tf_op jit(solution)/shard_map/while/body/eval_jaxpr/qhd,khd->hqk/dot_general | solution.py:108
  121.4 17.2 %fusion.156 = f32[4,512]{1,0:T(4,128)S(1)} fusion(f32[4,512,4608]{2,1,0:T(8,128)} %get-tuple-element.567, f32[4,512]{1,0:T(4,128)S(1)} %get-tuple-element.568, pred[512,4608]{1,0:T(8,128)(4,1)S(1)} %and_and_fusion.4), kind=kLoop, calls=%fused_computation.4.clone.1 | loop fusion | flops 37746688 | bytes 40124416 | tf_op jit(solution)/shard_map/while/body/eval_jaxpr/reduce_sum | solution.py:114
  159.4 17.6 %fusion.155 = (f32[4,512]{1,0:T(4,128)S(1)}, f32[4,512,4608]{2,1,0:T(8,128)}) fusion(pred[512,4608]{1,0:T(8,128)(4,1)S(1)} %and_and_fusion.4, bf16[5120,4,64]{0,2,1:T(8,128)(2,1)} %get-tuple-element.628, s32[]{:T(128)S(6)} %select_n.105, bf16[1024,4,64]{0,2,1:T(8,128)(2,1)S(1)} %get-tuple-element.627, s32[]{:T(128)S(6)} %select_n.106), kind=kOutput, calls=%fused_computation.3.clone.1 | convolution fusion | flops 1236269056 | bytes 42737672 | tf_op jit(solution)/shard_map/while/body/eval_jaxpr/qhd,khd->hqk/dot_general | solution.py:108
  223.4 102.4 %reduce-scatter.5.cloned.1.call-done = f32[256,1024]{1,0:T(8,128)} async-done(((f32[1024,1024]{1,0:T(8,128)}), f32[256,1024]{1,0:T(8,128)}) %reduce-scatter.5.cloned.1.call-update) | async-done | bytes 1048592 | tf_op jit(solution)/shard_map/reduce_scatter | solution.py:121
  329.7 22.7 %all-gather.5.cloned.1.call-done = bf16[1024,1024]{1,0:T(8,128)(2,1)} async-done(((bf16[256,1024]{1,0:T(8,128)(2,1)}), bf16[1024,1024]{1,0:T(8,128)(2,1)}) %all-gather.5.cloned.1.call-update) | async-done | bytes 2097168 | tf_op jit(solution)/shard_map/all_gather | solution.py:129
  380.1 33.2 %reduce-scatter.9.cloned.1.call-done = f32[256,1024]{1,0:T(8,128)} async-done(((f32[1024,1024]{1,0:T(8,128)}), f32[256,1024]{1,0:T(8,128)}) %reduce-scatter.9.cloned.1.call-update) | async-done | bytes 1048592 | tf_op jit(solution)/shard_map/reduce_scatter | solution.py:152
  415.5 44.8 %reduce-scatter.7.cloned.1.call-done = f32[256,1024]{1,0:T(8,128)} async-done(((f32[1024,1024]{1,0:T(8,128)}), f32[256,1024]{1,0:T(8,128)}) %reduce-scatter.7.cloned.1.call-update) | async-done | bytes 1048592 | tf_op jit(solution)/shard_map/reduce_scatter | solution.py:134
  465.6 22.7 %all-gather.9.cloned.1.call-done = bf16[1024,1024]{1,0:T(8,128)(2,1)} async-done(((bf16[256,1024]{1,0:T(8,128)(2,1)}), bf16[1024,1024]{1,0:T(8,128)(2,1)}) %all-gather.9.cloned.1.call-update) | async-done | bytes 2097168 | tf_op jit(solution)/shard_map/all_gather | solution.py:162
  496.6 248.7 %while.30 = (s32[]{:T(128)}, bf16[1024,4,64]{0,2,1:T(8,128)(2,1)S(1)}, f32[5120,4,64]{0,2,1:T(8,128)}, f32[5120,4,64]{0,2,1:T(8,128)}, bf16[5120,4,64]{0,2,1:T(8...) while((s32[]{:T(128)}, ...), condition=%wide.region_18.19_spmd, body=%wide.region_16.18_spmd.sunk | while | flops 6194465280 | bytes 340190528 | solution.py:222
  517.2 28.6 %multiply_reduce_fusion.9 = (f32[4,512]{1,0:T(4,128)S(1)}, f32[4,512,4608]{2,1,0:T(8,128)}) fusion(f32[4,512,4608]{2,1,0:T(8,128)} %fusion.166, f32[4,512]{1,0:T(4,128)S(1)} %dynamic-slice_bitcast_fusion.2, pred[512,4608]{1,0:T(8,128)(4,1)} %and_and_fusion.5, bf16[5120,4,64]{0,2,1:T(8,128)(2,1)} %get-tuple-element.682, s32[]{:T(128)S(6)} %select_n.111, ...), kind=kOutput, calls=%fused_computation.20.clone.1 | convolution fusion | flops 1255143424 | bytes 80494600 | tf_op jit(solution)/shard_map/while/body/eval_jaxpr/qhd,khd->hqk/dot_general | solution.py:186
  545.8 32.6 %multiply_convert_fusion.5 = bf16[4,512,4608]{2,1,0:T(8,128)(2,1)} fusion(f32[4,512,4608]{2,1,0:T(8,128)} %get-tuple-element.584, f32[4,512,4608]{2,1,0:T(8,128)} %fusion.166, f32[4,512]{1,0:T(4,128)S(1)} %get-tuple-element.585, f32[4,512]{1,0:T(4,128)S(1)} %dynamic-slice_bitcast_fusion.2, pred[512,4608]{1,0:T(8,128)(4,1)} %and_and_fusion.5), kind=kLoop, calls=%fused_computation.19.clone.1 | loop fusion | flops 56623104 | bytes 96747520 | tf_op jit(solution)/shard_map/while/body/eval_jaxpr/convert_element_type | solution.py:190
  601.7 19.3 %fusion.169 = f32[5120,4,64]{0,2,1:T(8,128)} fusion(f32[5120,4,64]{0,2,1:T(8,128)} %get-tuple-element.655, s32[]{:T(128)S(6)} %select_n.111, f32[4,512,4608]{2,1,0:T(8,128)} %fusion.166, f32[4,512]{1,0:T(4,128)S(1)} %dynamic-slice_bitcast_fusion.2, pred[512,4608]{1,0:T(8,128)(4,1)S(1)} %copy-done.2, ...), kind=kOutput, calls=%fused_computation.28.clone.1 | convolution fusion | flops 1246887936 | bytes 49815560 | tf_op jit(solution)/shard_map/while/body/eval_jaxpr/hqk,qhd->khd/dot_general | solution.py:199
  641.3 28.6 %multiply_reduce_fusion.9 = (f32[4,512]{1,0:T(4,128)S(1)}, f32[4,512,4608]{2,1,0:T(8,128)}) fusion(f32[4,512,4608]{2,1,0:T(8,128)} %fusion.166, f32[4,512]{1,0:T(4,128)S(1)} %dynamic-slice_bitcast_fusion.2, pred[512,4608]{1,0:T(8,128)(4,1)} %and_and_fusion.5, bf16[5120,4,64]{0,2,1:T(8,128)(2,1)} %get-tuple-element.682, s32[]{:T(128)S(6)} %select_n.111, ...), kind=kOutput, calls=%fused_computation.20.clone.1 | convolution fusion | flops 1255143424 | bytes 80494600 | tf_op jit(solution)/shard_map/while/body/eval_jaxpr/qhd,khd->hqk/dot_general | solution.py:186
  669.9 32.6 %multiply_convert_fusion.5 = bf16[4,512,4608]{2,1,0:T(8,128)(2,1)} fusion(f32[4,512,4608]{2,1,0:T(8,128)} %get-tuple-element.584, f32[4,512,4608]{2,1,0:T(8,128)} %fusion.166, f32[4,512]{1,0:T(4,128)S(1)} %get-tuple-element.585, f32[4,512]{1,0:T(4,128)S(1)} %dynamic-slice_bitcast_fusion.2, pred[512,4608]{1,0:T(8,128)(4,1)} %and_and_fusion.5), kind=kLoop, calls=%fused_computation.19.clone.1 | loop fusion | flops 56623104 | bytes 96747520 | tf_op jit(solution)/shard_map/while/body/eval_jaxpr/convert_element_type | solution.py:190
  725.9 19.3 %fusion.169 = f32[5120,4,64]{0,2,1:T(8,128)} fusion(f32[5120,4,64]{0,2,1:T(8,128)} %get-tuple-element.655, s32[]{:T(128)S(6)} %select_n.111, f32[4,512,4608]{2,1,0:T(8,128)} %fusion.166, f32[4,512]{1,0:T(4,128)S(1)} %dynamic-slice_bitcast_fusion.2, pred[512,4608]{1,0:T(8,128)(4,1)S(1)} %copy-done.2, ...), kind=kOutput, calls=%fused_computation.28.clone.1 | convolution fusion | flops 1246887936 | bytes 49815560 | tf_op jit(solution)/shard_map/while/body/eval_jaxpr/hqk,qhd->khd/dot_general | solution.py:199
  757.3 22.8 %collective-permute-done.10 = f32[1024,256]{0,1:T(8,128)S(1)} collective-permute-done((f32[1024,256]{0,1:T(8,128)S(1)}, f32[1024,256]{0,1:T(8,128)S(1)}, u32[]{:S(2)}, u32[]{:S(2)}) %collective-permute-start.10) | collective-permute-done | bytes 1048608 | tf_op jit(solution)/shard_map/ppermute | solution.py:16
  781.4 66.6 %collective-permute-done.11 = f32[1024,256]{0,1:T(8,128)S(1)} collective-permute-done((f32[1024,256]{0,1:T(8,128)S(1)}, f32[1024,256]{0,1:T(8,128)S(1)}, u32[]{:S(2)}, u32[]{:S(2)}) %collective-permute-start.11) | collective-permute-done | bytes 1048608 | tf_op jit(solution)/shard_map/ppermute | solution.py:16
  852.7 40.1 %collective-permute-done.13 = f32[1024,256]{0,1:T(8,128)S(1)} collective-permute-done((f32[1024,256]{0,1:T(8,128)S(1)}, f32[1024,256]{0,1:T(8,128)S(1)}, u32[]{:S(2)}, u32[]{:S(2)}) %collective-permute-start.13) | collective-permute-done | bytes 1048608 | tf_op jit(solution)/shard_map/ppermute | solution.py:16
  892.9 134.2 %collective-permute-done.15 = f32[1024,256]{0,1:T(8,128)S(1)} collective-permute-done((f32[1024,256]{0,1:T(8,128)S(1)}, f32[1024,256]{0,1:T(8,128)S(1)}, u32[]{:S(2)}, u32[]{:S(2)}) %collective-permute-start.15) | collective-permute-done | bytes 1048608 | tf_op jit(solution)/shard_map/ppermute | solution.py:16
  1031.1 40.2 %reduce-scatter.11.cloned.1.call-done = f32[256,1024]{1,0:T(8,128)} async-done(((f32[1024,1024]{1,0:T(8,128)}), f32[256,1024]{1,0:T(8,128)}) %reduce-scatter.11.cloned.1.call-update) | async-done | bytes 1048592 | tf_op jit(solution)/shard_map/reduce_scatter | solution.py:258
  1109.7 38.2 %all-reduce = (f32[1024]{0:T(1024)}, f32[1024]{0:T(1024)}, f32[2,256]{1,0:T(2,128)}, f32[1024]{0:T(1024)}, f32[1024]{0:T(1024)}, /*index=5*/f32[1024]{0:T(1024)}, f32[1024]{0:T(1024)}, f32[1024]{0:T(1024)}) all-reduce(f32[1024]{0:T(1024)S(1)} %get-tuple-element.383, ...), channel_id=1, replica_groups=mesh['dp'=8,'tensor'=4] {'dp'}, use_global_device_ids=true, to_apply=%region_26.27 | all-reduce | flops 7680 | bytes 61440 | tf_op jit(solution)/shard_map/psum | solution.py:289
  1147.9 378.4 %all-reduce.5.cloned.1.call-done = (f32[3,1024,256]{2,1,0:T(8,128)}, f32[256,1024]{1,0:T(8,128)}, f32[1024,1024]{1,0:T(8,128)}, f32[1024,1024]{1,0:T(8,128)}) async-done(((f32[3,1024,256]{2,1,0:T(8,128)}, f32[256,1024]{1,0:T(8,128)}, f32[1024,1024]{1,0:T(8,128)}, f32[1024,1024]{1,0:T(8,128)}), (f32[3,1024,256]{2,1,0:T(8,128)}, f32[256,1024]{1,0:T(8,128)}, f32[1024,1024]{1,0:T(8,128)}, ...) | async-done | bytes 12582928 | tf_op jit(solution)/shard_map/psum | solution.py:289
  (276 shorter events, 348.8 us)
Async XLA Ops:
  7.2 318.6 %reduce-scatter.5.cloned.1.call-start = ((), (), s32[]{:S(2)}) async-start(), calls=%async_computation.4 | async-start | bytes 5242880 | tf_op jit(solution)/shard_map/reduce_scatter | solution.py:121
  21.0 40.3 %collective-permute-start.1 = (bf16[1024,256]{1,0:T(8,128)(2,1)}, bf16[1024,256]{1,0:T(8,128)(2,1)}, u32[]{:S(2)}, u32[]{:S(2)}) collective-permute-start(bf16[1024,256]{1,0:T(8,128)(2,1)} %fusion.66), channel_id=1, source_target_pairs={{0,12},{4,16},{8,20},{12,24},{16,28},{1,13},{5,17},{9,21},{13,25},... | collective-permute-start | bytes 1572872 | tf_op jit(solution)/shard_map/ppermute | solution.py:16
  26.3 39.0 %collective-permute-start.2 = (bf16[1024,256]{1,0:T(8,128)(2,1)}, bf16[1024,256]{1,0:T(8,128)(2,1)}, u32[]{:S(2)}, u32[]{:S(2)}) collective-permute-start(bf16[1024,256]{1,0:T(8,128)(2,1)} %fusion.66), channel_id=1, source_target_pairs={{0,8},{4,12},{8,16},{12,20},{16,24},{20,28},{1,9},{5,13},{9,17},{1... | collective-permute-start | bytes 1572872 | tf_op jit(solution)/shard_map/ppermute | solution.py:16
  28.4 50.4 %collective-permute-start.3 = (bf16[1024,256]{1,0:T(8,128)(2,1)}, bf16[1024,256]{1,0:T(8,128)(2,1)}, u32[]{:S(2)}, u32[]{:S(2)}) collective-permute-start(bf16[1024,256]{1,0:T(8,128)(2,1)} %fusion.66), channel_id=1, source_target_pairs={{0,4},{4,8},{8,12},{12,16},{16,20},{20,24},{24,28},{1,5},{5,9},{9,... | collective-permute-start | bytes 1572872 | tf_op jit(solution)/shard_map/ppermute | solution.py:16
  32.2 54.8 %collective-permute-start.4 = (bf16[1024,256]{1,0:T(8,128)(2,1)S(1)}, bf16[1024,256]{1,0:T(8,128)(2,1)}, u32[]{:S(2)}, u32[]{:S(2)}) collective-permute-start(bf16[1024,256]{1,0:T(8,128)(2,1)S(1)} %convolution_convert_fusion.1), channel_id=1, source_target_pairs={{0,16},{4,20},{8,24},{12,28},{1,17},{5,21},{9,25},{13,29},{2,18},{... | collective-permute-start | bytes 1572872 | tf_op jit(solution)/shard_map/ppermute | solution.py:16
  37.2 51.6 %collective-permute-start.5 = (bf16[1024,256]{1,0:T(8,128)(2,1)S(1)}, bf16[1024,256]{1,0:T(8,128)(2,1)}, u32[]{:S(2)}, u32[]{:S(2)}) collective-permute-start(bf16[1024,256]{1,0:T(8,128)(2,1)S(1)} %convolution_convert_fusion.1), channel_id=1, source_target_pairs={{0,12},{4,16},{8,20},{12,24},{16,28},{1,13},{5,17},{9,21},{13,25},... | collective-permute-start | bytes 1572872 | tf_op jit(solution)/shard_map/ppermute | solution.py:16
  61.3 29.4 %collective-permute-start.6 = (bf16[1024,256]{1,0:T(8,128)(2,1)S(1)}, bf16[1024,256]{1,0:T(8,128)(2,1)}, u32[]{:S(2)}, u32[]{:S(2)}) collective-permute-start(bf16[1024,256]{1,0:T(8,128)(2,1)S(1)} %convolution_convert_fusion.1), channel_id=1, source_target_pairs={{0,8},{4,12},{8,16},{12,20},{16,24},{20,28},{1,9},{5,13},{9,17},{1... | collective-permute-start | bytes 1572872 | tf_op jit(solution)/shard_map/ppermute | solution.py:16
  65.3 27.3 %collective-permute-start.7 = (bf16[1024,256]{1,0:T(8,128)(2,1)S(1)}, bf16[1024,256]{1,0:T(8,128)(2,1)}, u32[]{:S(2)}, u32[]{:S(2)}) collective-permute-start(bf16[1024,256]{1,0:T(8,128)(2,1)S(1)} %convolution_convert_fusion.1), channel_id=1, source_target_pairs={{0,4},{4,8},{8,12},{12,16},{16,20},{20,24},{24,28},{1,5},{5,9},{9,... | collective-permute-start | bytes 1572872 | tf_op jit(solution)/shard_map/ppermute | solution.py:16
  217.4 134.9 %all-gather.5.cloned.1.call-start = ((), (), s32[]{:S(2)}) async-start(), calls=%async_computation.5 | async-start | bytes 2621440 | tf_op jit(solution)/shard_map/all_gather | solution.py:129
  329.6 83.6 %reduce-scatter.9.cloned.1.call-start = ((), (), s32[]{:S(2)}) async-start(), calls=%async_computation.8 | async-start | bytes 5242880 | tf_op jit(solution)/shard_map/reduce_scatter | solution.py:152
  368.6 91.6 %reduce-scatter.7.cloned.1.call-start = ((), (), s32[]{:S(2)}) async-start(), calls=%async_computation.6 | async-start | bytes 5242880 | tf_op jit(solution)/shard_map/reduce_scatter | solution.py:134
  375.6 112.7 %all-gather.9.cloned.1.call-start = ((), (), s32[]{:S(2)}) async-start(), calls=%async_computation.9 | async-start | bytes 2621440 | tf_op jit(solution)/shard_map/all_gather | solution.py:162
  465.5 605.7 %reduce-scatter.11.cloned.1.call-start = ((), (), s32[]{:S(2)}) async-start(), calls=%async_computation.10 | async-start | bytes 5242880 | tf_op jit(solution)/shard_map/reduce_scatter | solution.py:258
  750.8 29.3 %collective-permute-start.10 = (f32[1024,256]{0,1:T(8,128)S(1)}, f32[1024,256]{0,1:T(8,128)S(1)}, u32[]{:S(2)}, u32[]{:S(2)}) collective-permute-start(f32[1024,256]{0,1:T(8,128)S(1)} %bitcast.156), channel_id=1, source_target_pairs={{12,0},{16,4},{20,8},{24,12},{28,16},{13,1},{17,5},{21,9},{25,13},... | collective-permute-start | bytes 3145736 | tf_op jit(solution)/shard_map/ppermute | solution.py:16
  752.1 95.9 %collective-permute-start.11 = (f32[1024,256]{0,1:T(8,128)S(1)}, f32[1024,256]{0,1:T(8,128)S(1)}, u32[]{:S(2)}, u32[]{:S(2)}) collective-permute-start(f32[1024,256]{0,1:T(8,128)S(1)} %bitcast.155), channel_id=1, source_target_pairs={{16,0},{20,4},{24,8},{28,12},{17,1},{21,5},{25,9},{29,13},{18,2},{... | collective-permute-start | bytes 3145736 | tf_op jit(solution)/shard_map/ppermute | solution.py:16
  753.4 95.9 %collective-permute-start.8 = (f32[1024,256]{0,1:T(8,128)S(1)}, f32[1024,256]{0,1:T(8,128)S(1)}, u32[]{:S(2)}, u32[]{:S(2)}) collective-permute-start(f32[1024,256]{0,1:T(8,128)S(1)} %bitcast.154), channel_id=1, source_target_pairs={{4,0},{8,4},{12,8},{16,12},{20,16},{24,20},{28,24},{5,1},{9,5},{13... | collective-permute-start | bytes 3145736 | tf_op jit(solution)/shard_map/ppermute | solution.py:16
  754.7 96.6 %collective-permute-start.9 = (f32[1024,256]{0,1:T(8,128)S(1)}, f32[1024,256]{0,1:T(8,128)S(1)}, u32[]{:S(2)}, u32[]{:S(2)}) collective-permute-start(f32[1024,256]{0,1:T(8,128)S(1)} %bitcast.153), channel_id=1, source_target_pairs={{8,0},{12,4},{16,8},{20,12},{24,16},{28,20},{9,1},{13,5},{17,9},{2... | collective-permute-start | bytes 3145736 | tf_op jit(solution)/shard_map/ppermute | solution.py:16
  756.0 96.7 %collective-permute-start.12 = (f32[1024,256]{0,1:T(8,128)S(1)}, f32[1024,256]{0,1:T(8,128)S(1)}, u32[]{:S(2)}, u32[]{:S(2)}) collective-permute-start(f32[1024,256]{0,1:T(8,128)S(1)} %bitcast.152), channel_id=1, source_target_pairs={{4,0},{8,4},{12,8},{16,12},{20,16},{24,20},{28,24},{5,1},{9,5},{13... | collective-permute-start | bytes 3145736 | tf_op jit(solution)/shard_map/ppermute | solution.py:16
  780.1 112.8 %collective-permute-start.13 = (f32[1024,256]{0,1:T(8,128)S(1)}, f32[1024,256]{0,1:T(8,128)S(1)}, u32[]{:S(2)}, u32[]{:S(2)}) collective-permute-start(f32[1024,256]{0,1:T(8,128)S(1)} %bitcast.151), channel_id=1, source_target_pairs={{8,0},{12,4},{16,8},{20,12},{24,16},{28,20},{9,1},{13,5},{17,9},{2... | collective-permute-start | bytes 3145736 | tf_op jit(solution)/shard_map/ppermute | solution.py:16
  848.0 44.9 %collective-permute-start.14 = (f32[1024,256]{0,1:T(8,128)S(1)}, f32[1024,256]{0,1:T(8,128)S(1)}, u32[]{:S(2)}, u32[]{:S(2)}) collective-permute-start(f32[1024,256]{0,1:T(8,128)S(1)} %bitcast.150), channel_id=1, source_target_pairs={{12,0},{16,4},{20,8},{24,12},{28,16},{13,1},{17,5},{21,9},{25,13},... | collective-permute-start | bytes 3145736 | tf_op jit(solution)/shard_map/ppermute | solution.py:16
  849.3 177.8 %collective-permute-start.15 = (f32[1024,256]{0,1:T(8,128)S(1)}, f32[1024,256]{0,1:T(8,128)S(1)}, u32[]{:S(2)}, u32[]{:S(2)}) collective-permute-start(f32[1024,256]{0,1:T(8,128)S(1)} %bitcast.149), channel_id=1, source_target_pairs={{16,0},{20,4},{24,8},{28,12},{17,1},{21,5},{25,9},{29,13},{18,2},{... | collective-permute-start | bytes 3145736 | tf_op jit(solution)/shard_map/ppermute | solution.py:16
  1030.3 66.9 %all-gather.7.cloned.1.call-start = ((), (), s32[]{:S(2)}) async-start(), calls=%async_computation.7 | async-start | bytes 2621440 | tf_op jit(solution)/shard_map/all_gather | solution.py:161
  1031.0 116.9 %all-gather.11.cloned.1.call-start = ((), (), s32[]{:S(2)}) async-start(), calls=%async_computation.11 | async-start | bytes 2621440 | tf_op jit(solution)/shard_map/all_gather | solution.py:270
  1077.5 448.8 %all-reduce.5.cloned.1.call-start = ((), (), s32[]{:S(2)}) async-start(), calls=%async_computation.12 | async-start | bytes 25165824 | tf_op jit(solution)/shard_map/psum | solution.py:289
  (55 other events, 1927.4 us)
Sparse Core Ops, SparseCore 0:
  217.5 108.2 reduce-scatter.4
  329.7 22.5 all-gather.4
  368.7 44.5 reduce-scatter.8
  415.6 44.5 reduce-scatter.6
  465.6 22.5 all-gather.8
  1030.4 40.8 reduce-scatter.10
  1072.8 22.5 all-gather.6
  1097.0 22.6 all-gather.10
  1125.6 400.6 all-reduce.4
where the time goes:
time: 1550 us
  waiting for transfers between devices  909 us (59%)
  matrix products  297 us (19%)
  other arithmetic  148 us (10%)
  starting transfers between devices  66.6 us (4%)
  local copies, waits for them, and re-layouts  61.3 us (4%)
  blocking collectives  48.8 us (3%)
    psum x1, waiting for transfers between devices, per_device(): lax.psum((grad_ln1_gain, grad_ln1_bias, grad_w_qkv, grad_b_qv, grad_w_out...  378 us
    ppermute x16, waiting for transfers between devices, from_behind(): lax.ppermute(value, axis, [(source, source + steps) for source in range(f...  264 us
    reduce_scatter x1, waiting for transfers between devices, per_device(): lax.psum_scatter(jnp.dot(heads_low, w_out, preferred_element_type=jnp.flo...  102 us
    ppermute x16, starting transfers between devices, from_behind(): lax.ppermute(value, axis, [(source, source + steps) for source in range(f...  65.7 us
    convert_element_type x2, other arithmetic, backward_block(): score_grad = (probs * (prob_grad - row_dot)).astype(jnp.bfloat16)  65.2 us
    dot_general x2, matrix products, backward_block(): jnp.einsum('qhd,khd->hqk', grad_block, value_window, preferred_element_ty...  57.2 us
    reduce_scatter x1, waiting for transfers between devices, per_device(): lax.psum_scatter(jnp.dot(active_low, w_proj, preferred_element_type=jnp.f...  44.8 us
    reduce_scatter x1, waiting for transfers between devices, per_device(): lax.psum_scatter(jnp.einsum('tl,cl->tc', query_part, w_qkv[0], preferred_...  40.2 us
  transfers between devices with their start and end apart: 25, of which 11 were waited for; matrix products, arithmetic and copies ran while one was open for 4% of the time, Pallas kernels for 0%

commit v1 on v0

v1 whole, which is shorter than its diff:
```python
import functools

import jax
import jax.numpy as jnp
from jax import lax
from jax.experimental import pallas as pl
from jax.experimental.pallas import tpu as pltpu
from jax.sharding import PartitionSpec as P

HEAD_DIM = 64
NEG = -1e30
TN = (((0,), (0,)), ((), ()))
NN = (((1,), (0,)), ((), ()))
NT = (((1,), (1,)), ((), ()))
LOW = jnp.bfloat16
F32 = jnp.float32


def dotf(a,b,dims): return lax.dot_general(a,b,dims,preferred_element_type=jnp.float32)

def seq_start(place, ends):
    start = jnp.zeros_like(place)
    for e in ends: start = jnp.where(place >= e, e, start)
    return start

def read_ends(seq_ref):
    ends=[]; total=jnp.int32(0)
    for s in range(seq_ref.shape[0]-1):
        total=total+seq_ref[s]; ends.append(total)
    return ends

def key_spot(kstart, meta_ref, J,S,T):
    b=kstart//T
    gg=lax.rem(b,S); kj=b//S
    e=lax.rem(meta_ref[1]-gg+S,S); s=lax.rem(meta_ref[0]-kj+J,J)
    return e*J+s, lax.rem(kstart,T)

def transpose_blocks(kv_ref, lo, dst, T):
    n=kv_ref.shape[0]*kv_ref.shape[1]
    J=kv_ref.shape[1]
    def one(i,_):
        dst[i]=kv_ref[i//J, lax.rem(i,J), lo:lo+HEAD_DIM, :].T
        return 0
    lax.fori_loop(0,n,one,0)

def fwd_kernel(bq,bk,meta_ref,seq_ref,q_ref,kv_ref,o_ref,lse_ref,kt_ref):
    S,J,_,T=kv_ref.shape
    ends=read_ends(seq_ref)
    transpose_blocks(kv_ref,0,kt_ref,T)
    per=T//bq
    rows=lax.broadcasted_iota(jnp.int32,(bk,bq),0)
    def q_tile(i,_):
        s=i//per; qo=pl.multiple_of(lax.rem(i,per)*bq,bq)
        jj=lax.rem(meta_ref[0]-s+J,J)
        q0=(jj*S+meta_ref[1])*T+qo
        q=q_ref[s,:,pl.ds(qo,bq)]
        place=q0+lax.broadcasted_iota(jnp.int32,(1,bq),1)
        start=seq_start(place,ends)
        lo_min=seq_start(q0,ends); lo_max=seq_start(q0+bq-1,ends)
        def tile(masked,kt,carry):
            m,l,acc=carry
            kstart=kt*bk
            spot,ko=key_spot(kstart,meta_ref,J,S,T)
            ko=pl.multiple_of(ko,bk)
            k=kt_ref[spot,pl.ds(ko,bk),:]
            v=kv_ref[spot//J,lax.rem(spot,J),HEAD_DIM:,pl.ds(ko,bk)]
            sc=dotf(k,q,NN)
            if masked:
                sc=jnp.where((rows>=start-kstart)&(rows<=place-kstart),sc,NEG)
            m2=jnp.maximum(m,jnp.max(sc,axis=0,keepdims=True))
            p=jnp.exp(sc-m2)
            a=jnp.exp(m-m2)
            l=l*a+jnp.sum(p,axis=0,keepdims=True)
            acc=acc*a+dotf(v,p.astype(jnp.bfloat16),NN)
            return m2,l,acc
        t0=lo_min//bk; t3=(q0+bq+bk-1)//bk
        t2=jnp.maximum(q0//bk,t0); t1=jnp.minimum((lo_max+bk-1)//bk,t2)
        t1=jnp.maximum(t1,t0)
        c=(jnp.full((1,bq),NEG,jnp.float32),jnp.zeros((1,bq),jnp.float32),jnp.zeros((HEAD_DIM,bq),jnp.float32))
        c=lax.fori_loop(t2,t3,functools.partial(tile,True),c)
        c=lax.fori_loop(t0,t1,functools.partial(tile,True),c)
        c=lax.fori_loop(t1,t2,functools.partial(tile,False),c)
        m,l,acc=c
        o_ref[s,:,pl.ds(qo,bq)]=(acc/l).astype(o_ref.dtype)
        lse_ref[s,:,pl.ds(qo,bq)]=m+jnp.log(l)
        return 0
    lax.fori_loop(0,J*per,q_tile,0)

def bwd_kernel(bq,bk,nt,meta_ref,seq_ref,q_ref,kv_ref,o_ref,lse_ref,do_ref,dq_ref,dkv_ref,kt_ref,vt_ref,dk_acc,dv_acc):
    S,J,_,T=kv_ref.shape
    ends=read_ends(seq_ref)
    transpose_blocks(kv_ref,0,kt_ref,T)
    transpose_blocks(kv_ref,HEAD_DIM,vt_ref,T)
    dk_acc[...]=jnp.zeros_like(dk_acc)
    dv_acc[...]=jnp.zeros_like(dv_acc)
    per=T//bq
    rows=lax.broadcasted_iota(jnp.int32,(bk,bq),0)
    def q_tile(i,_):
        s=i//per; qo=pl.multiple_of(lax.rem(i,per)*bq,bq)
        jj=lax.rem(meta_ref[0]-s+J,J)
        q0=(jj*S+meta_ref[1])*T+qo
        q=q_ref[s,:,pl.ds(qo,bq)]
        do=do_ref[s,:,pl.ds(qo,bq)]
        lse=lse_ref[s,:,pl.ds(qo,bq)]
        delta=jnp.sum(do.astype(jnp.float32)*o_ref[s,:,pl.ds(qo,bq)].astype(jnp.float32),axis=0,keepdims=True)
        if not nt:
            q_t=q.T; do_t=do.T
        place=q0+lax.broadcasted_iota(jnp.int32,(1,bq),1)
        start=seq_start(place,ends)
        lo_min=seq_start(q0,ends); lo_max=seq_start(q0+bq-1,ends)
        def tile(masked,kt,dq):
            kstart=kt*bk
            spot,ko=key_spot(kstart,meta_ref,J,S,T)
            ko=pl.multiple_of(ko,bk)
            k=kt_ref[spot,pl.ds(ko,bk),:]
            v=vt_ref[spot,pl.ds(ko,bk),:]
            k_flat=kv_ref[spot//J,lax.rem(spot,J),:HEAD_DIM,pl.ds(ko,bk)]
            sc=dotf(k,q,NN)
            p=jnp.exp(sc-lse)
            if masked:
                p=jnp.where((rows>=start-kstart)&(rows<=place-kstart),p,0.0)
            dp=dotf(v,do,NN)
            ds=(p*(dp-delta)).astype(jnp.bfloat16)
            pb=p.astype(jnp.bfloat16)
            if nt:
                dv_acc[spot,:,pl.ds(ko,bk)]+=dotf(do,pb,NT)
                dk_acc[spot,:,pl.ds(ko,bk)]+=dotf(q,ds,NT)
            else:
                dv_acc[spot,pl.ds(ko,bk),:]+=dotf(pb,do_t,NN)
                dk_acc[spot,pl.ds(ko,bk),:]+=dotf(ds,q_t,NN)
            return dq+dotf(k_flat,ds,NN)
        t0=lo_min//bk; t3=(q0+bq+bk-1)//bk
        t2=jnp.maximum(q0//bk,t0); t1=jnp.minimum((lo_max+bk-1)//bk,t2)
        t1=jnp.maximum(t1,t0)
        dq=jnp.zeros((HEAD_DIM,bq),jnp.float32)
        dq=lax.fori_loop(t2,t3,functools.partial(tile,True),dq)
        dq=lax.fori_loop(t0,t1,functools.partial(tile,True),dq)
        dq=lax.fori_loop(t1,t2,functools.partial(tile,False),dq)
        dq_ref[s,:,pl.ds(qo,bq)]=(dq*0.125).astype(dq_ref.dtype)
        return 0
    lax.fori_loop(0,J*per,q_tile,0)
    def out(i,_):
        a=dk_acc[i]; b=dv_acc[i]
        if not nt: a=a.T; b=b.T
        dkv_ref[i//J,lax.rem(i,J),:HEAD_DIM,:]=a.astype(dkv_ref.dtype)
        dkv_ref[i//J,lax.rem(i,J),HEAD_DIM:,:]=b.astype(dkv_ref.dtype)
        return 0
    lax.fori_loop(0,S*J,out,0)

V=pl.BlockSpec(memory_space=pltpu.VMEM); M=pl.BlockSpec(memory_space=pltpu.SMEM)
MIB = 2**20


def vmem_for(keys):
    return (60 if keys > 8192 else 40) * MIB


def attn_fwd(meta,seq,q,kv,bq=512,bk=512):
    S,J,_,T=kv.shape
    return pl.pallas_call(functools.partial(fwd_kernel,bq,bk),
        out_shape=(jax.ShapeDtypeStruct((J,HEAD_DIM,T),jnp.bfloat16),jax.ShapeDtypeStruct((J,1,T),jnp.float32)),
        in_specs=[M,M,V,V],out_specs=(V,V),
        scratch_shapes=[pltpu.VMEM((S*J,T,HEAD_DIM),jnp.bfloat16)],
        compiler_params=pltpu.CompilerParams(vmem_limit_bytes=vmem_for(S*J*T)),name="attn_fwd")(meta,seq,q,kv)
def attn_bwd(meta,seq,q,kv,o,lse,do,bq=512,bk=512,nt=True):
    S,J,_,T=kv.shape
    acc=(S*J,HEAD_DIM,T) if nt else (S*J,T,HEAD_DIM)
    return pl.pallas_call(functools.partial(bwd_kernel,bq,bk,nt),
        out_shape=(jax.ShapeDtypeStruct((J,HEAD_DIM,T),jnp.bfloat16),jax.ShapeDtypeStruct((S,J,2*HEAD_DIM,T),jnp.bfloat16)),
        in_specs=[M,M,V,V,V,V,V],out_specs=(V,V),
        scratch_shapes=[pltpu.VMEM((S*J,T,HEAD_DIM),jnp.bfloat16)]*2+[pltpu.VMEM(acc,jnp.float32)]*2,
        compiler_params=pltpu.CompilerParams(vmem_limit_bytes=vmem_for(S*J*T)),name="attn_bwd")(meta,seq,q,kv,o,lse,do)


def norm_rows(values, weight_row, shift_row):
    centred = values - jnp.mean(values, axis=-1, keepdims=True)
    spread = jnp.mean(centred * centred, axis=-1, keepdims=True)
    return centred * lax.rsqrt(spread + 1e-05) * weight_row + shift_row


def gelu_tanh(values):
    return jax.nn.gelu(values, approximate=True)


def shift_dp(value, steps):
    count = lax.axis_size("dp")
    return lax.ppermute(value, "dp", [(i, (i + steps) % count) for i in range(count)])


def swap_core(value):
    return lax.ppermute(value, "tensor", [(i, i ^ 1) for i in range(lax.axis_size("tensor"))])


def swap_x(value):
    return lax.ppermute(value, "tensor", [(i, i ^ 2) for i in range(lax.axis_size("tensor"))])


def shift_group(value, steps, S):
    count = lax.axis_size("dp")
    return lax.ppermute(
        value, "dp", [(i, i // S * S + (i % S + steps) % S) for i in range(count)]
    )


def reduce_blocks(blocks, j, g):
    J, S = blocks.shape[:2]
    kept = None
    arrived = []
    for s in range(J):
        row = pick(blocks, (j + s) % J)
        total = pick(row, g).astype(F32)
        for e in range(1, S):
            total = total + shift_group(pick(row, (g + e) % S), e, S).astype(F32)
        if s:
            arrived.append(shift_dp(total.astype(LOW), s * S))
        else:
            kept = total
    for part in arrived:
        kept = kept + part.astype(F32)
    return kept


def gather_blocks(block, j, g, J, S):
    found = []
    for s in range(J):
        part = shift_dp(block, s * S) if s else block
        found.append(((j - s) % J, g, part))
        for e in range(1, S):
            found.append(((j - s) % J, (g - e) % S, shift_group(part, e, S)))
    return found


def rows_at(value, start, count):
    return lax.dynamic_slice_in_dim(value, start, count, 0)


def pick(value, index):
    return lax.dynamic_index_in_dim(value, index, 0, keepdims=False)


def in_order(first, own, other):
    return jnp.where(first, jnp.concatenate([own, other], 0), jnp.concatenate([other, own], 0))


def sum_rows(partial, core, side):
    half = partial.shape[0] // 2
    own = rows_at(partial, core * half, half)
    own = own + swap_core(rows_at(partial, (1 - core) * half, half).astype(LOW)).astype(F32)
    quarter = half // 2
    kept = rows_at(own, side * quarter, quarter)
    return kept + swap_x(rows_at(own, (1 - side) * quarter, quarter).astype(LOW)).astype(F32)


def all_rows(quarter, core, side):
    half = in_order(side == 0, quarter, swap_x(quarter))
    return in_order(core == 0, half, swap_core(half))


def per_device(
    block_input,
    output_grad,
    seq_lengths,
    ln1_gain,
    ln1_bias,
    w_qkv,
    b_qv,
    w_out,
    b_out,
    ln2_gain,
    ln2_bias,
    w_fc,
    b_fc,
    w_proj,
    b_proj,
):
    T, D = block_input.shape
    local = w_qkv.shape[2]
    J = local // HEAD_DIM
    count = lax.axis_size("dp")
    S = count // J
    place = lax.axis_index("dp")
    j, g = place // S, place % S
    tensor = lax.axis_index("tensor")
    core, side = tensor % 2, tensor // 2
    share = T // lax.axis_size("tensor")
    share_start = core * (T // 2) + side * share
    meta = jnp.stack([j, g]).astype(jnp.int32)

    x_float = block_input.astype(F32)
    first_low = norm_rows(x_float, ln1_gain, ln1_bias).astype(LOW)

    b_v = b_qv[1].reshape(J, HEAD_DIM, 1)
    b_q = b_qv[0].reshape(J, HEAD_DIM, 1)

    def project(weight):
        return jnp.einsum("cl,tc->lt", weight, first_low, preferred_element_type=F32).reshape(
            J, HEAD_DIM, T
        )

    keys = project(w_qkv[1]).astype(LOW)
    values = (project(w_qkv[2]) + b_v).astype(LOW)
    both = jnp.concatenate([keys, values], 1)
    kv_parts = []
    for s in range(J):
        piece = pick(both, (j + s) % J)
        kv_parts.append(shift_dp(piece, s * S) if s else piece)
    queries = ((project(w_qkv[0]) + b_q).astype(LOW) * 0.125).astype(LOW)
    q_parts = []
    for s in range(J):
        piece = pick(queries, (j + s) % J)
        q_parts.append(shift_dp(piece, s * S) if s else piece)
    kv_all = [jnp.stack(kv_parts)]
    for e in range(1, S):
        kv_all.append(jnp.stack([shift_group(part, e, S) for part in kv_parts]))
    kv_all = jnp.stack(kv_all)
    q_all = jnp.stack(q_parts)

    o_all, lse = attn_fwd(meta, seq_lengths, q_all, kv_all)

    def home(parts):
        out = jnp.zeros((J, *parts[0].shape), parts[0].dtype)
        for s in range(J):
            got = shift_dp(parts[s], -s * S) if s else parts[s]
            out = lax.dynamic_update_slice_in_dim(out, got[None], (j + s) % J, 0)
        return out

    o_home = home([o_all[s] for s in range(J)]).reshape(local, T)

    def gather_tensor(value):
        across = swap_x(value)
        return jnp.concatenate([value, swap_core(value), across, swap_core(across)], 0)

    w_out_all = gather_tensor(w_out)
    o_gathered = gather_tensor(o_home)
    attn = jnp.einsum("lt,ld->td", o_gathered, w_out_all, preferred_element_type=F32)
    middle = x_float + attn + b_out
    second_low = norm_rows(middle, ln2_gain, ln2_bias).astype(LOW)
    hidden = jnp.dot(second_low, w_fc, preferred_element_type=F32) + b_fc
    active, gelu_back = jax.vjp(gelu_tanh, hidden)
    active_low = active.astype(LOW)
    active_grad = jnp.einsum("td,fd->tf", output_grad, w_proj, preferred_element_type=F32)
    hidden_grad = gelu_back(active_grad)[0].astype(LOW)
    second_part = jnp.einsum("tf,cf->tc", hidden_grad, w_fc, preferred_element_type=F32)
    second_grad = sum_rows(second_part, core, side)
    middle_share = rows_at(middle, share_start, share)
    _, second_back = jax.vjp(norm_rows, middle_share, ln2_gain, ln2_bias)
    middle_part, grad_ln2_gain, grad_ln2_bias = second_back(second_grad)
    feed_share = rows_at(output_grad, share_start, share).astype(F32)
    middle_grad = feed_share + middle_part
    branch_share = middle_grad.astype(LOW)
    branch_grad = all_rows(branch_share, core, side)

    heads_grad = jnp.einsum("ld,td->lt", w_out, branch_grad, preferred_element_type=F32)
    heads_grad = heads_grad.astype(LOW).reshape(J, HEAD_DIM, T)
    do_parts = []
    for s in range(J):
        piece = pick(heads_grad, (j + s) % J)
        do_parts.append(shift_dp(piece, s * S) if s else piece)
    do_all = jnp.stack(do_parts)

    grad_w_proj = jnp.einsum("tf,td->fd", active_low, output_grad, preferred_element_type=F32)
    grad_w_fc = jnp.einsum("tc,tf->cf", second_low, hidden_grad, preferred_element_type=F32)
    grad_w_out = jnp.einsum("lt,td->ld", o_home, branch_grad, preferred_element_type=F32)
    grad_w_proj, grad_w_fc, grad_w_out = lax.psum(
        (grad_w_proj.astype(LOW), grad_w_fc.astype(LOW), grad_w_out.astype(LOW)), "dp"
    )
    grad_b_fc = jnp.sum(hidden_grad.astype(F32), axis=0)
    width = grad_b_fc.shape[0] * lax.axis_size("tensor")
    wide = lax.dynamic_update_slice_in_dim(
        jnp.zeros((width,), F32), grad_b_fc, tensor * grad_b_fc.shape[0], 0
    ).reshape(-1, D)
    small = jnp.concatenate(
        [
            jnp.stack(
                [
                    jnp.sum(feed_share, axis=0),
                    jnp.sum(branch_share.astype(F32), axis=0),
                    grad_ln2_gain,
                    grad_ln2_bias,
                ]
            ),
            wide,
        ],
        0,
    )
    small = lax.psum(small, ("dp", "tensor"))
    grad_b_proj, grad_b_out, grad_ln2_gain, grad_ln2_bias = small[0], small[1], small[2], small[3]
    grad_b_fc = rows_at(small[4:].reshape(-1), tensor * grad_b_fc.shape[0], grad_b_fc.shape[0])

    feed_part = jnp.dot(active_low, w_proj, preferred_element_type=F32)
    output_share = (middle_share + (sum_rows(feed_part, core, side) + b_proj)).astype(LOW)
    block_output = all_rows(output_share, core, side)

    dq, dkv = attn_bwd(meta, seq_lengths, q_all, kv_all, o_all, lse, do_all)
    kv_total = [dkv[0, s].astype(F32) for s in range(J)]
    for e in range(1, S):
        for s in range(J):
            kv_total[s] = kv_total[s] + shift_group(dkv[e, s], -e, S).astype(F32)
    q_home = home([dq[s] for s in range(J)]).reshape(local, T)
    kv_home = home([part.astype(LOW) for part in kv_total])
    k_home = kv_home[:, :HEAD_DIM].reshape(local, T)
    v_home = kv_home[:, HEAD_DIM:].reshape(local, T)

    first_part = sum(
        jnp.einsum("lt,cl->tc", part, w_qkv[i], preferred_element_type=F32)
        for i, part in enumerate((q_home, k_home, v_home))
    )
    first_grad = sum_rows(first_part, core, side)
    first_back = jax.vjp(norm_rows, rows_at(x_float, share_start, share), ln1_gain, ln1_bias)[1]
    input_part, gain_share, bias_share = first_back(first_grad)
    input_grad = all_rows((middle_grad + input_part).astype(LOW), core, side)

    slab = D // count
    grad_parts = jnp.stack(
        [
            jnp.einsum("tc,lt->cl", first_low, part, preferred_element_type=F32).astype(LOW)
            for part in (q_home, k_home, v_home)
        ]
    )
    blocks = grad_parts.reshape(3, J, S, slab, local).transpose(1, 2, 0, 3, 4)
    block = reduce_blocks(blocks, j, g).astype(LOW)
    grad_w_qkv = jnp.zeros((3, count, slab, local), F32)
    for jj, gg, part in gather_blocks(block, j, g, J, S):
        grad_w_qkv = lax.dynamic_update_slice(
            grad_w_qkv, part.astype(F32)[:, None], (0, jj * S + gg, 0, 0)
        )
    grad_w_qkv = grad_w_qkv.reshape(3, D, local)
    bias_qv = jnp.stack([jnp.sum(q_home.astype(F32), axis=1), jnp.sum(v_home.astype(F32), axis=1)])
    wide = lax.dynamic_update_slice_in_dim(jnp.zeros((2, D), F32), bias_qv, tensor * local, 1)
    late = jnp.concatenate([jnp.stack([gain_share, bias_share]), wide], 0)
    late = late + swap_core(late)
    late = late + swap_x(late)
    step = 1
    while step < count:
        late = late + lax.ppermute(late, "dp", [(i, i ^ step) for i in range(count)])
        step *= 2
    grad_b_qv = lax.dynamic_slice_in_dim(late[2:], tensor * local, local, 1)
    return (
        block_output,
        input_grad,
        late[0],
        late[1],
        grad_w_qkv,
        grad_b_qv,
        grad_w_out.astype(F32),
        grad_b_out,
        grad_ln2_gain,
        grad_ln2_bias,
        grad_w_fc.astype(F32),
        grad_b_fc,
        grad_w_proj.astype(F32),
        grad_b_proj,
    )


def solution(mesh):
    placed = (
        P("dp", None),
        P("dp", None),
        P(),
        P(),
        P(),
        P(None, None, "tensor"),
        P(None, "tensor"),
        P("tensor", None),
        P(),
        P(),
        P(),
        P(None, "tensor"),
        P("tensor"),
        P("tensor", None),
        P(),
    )
    return jax.shard_map(
        per_device,
        mesh=mesh,
        in_specs=placed,
        out_specs=(
            P("dp", None),
            P("dp", None),
            P(),
            P(),
            P(None, None, "tensor"),
            P(None, "tensor"),
            P("tensor", None),
            P(),
            P(),
            P(),
            P(None, "tensor"),
            P("tensor"),
            P("tensor", None),
            P(),
        ),
        check_vma=False,
    )
```

time: 1550 us -> 574 us (0.37)
  waiting for transfers between devices: 909 us -> 198 us
  matrix products: 297 us -> 44.4 us
  other arithmetic: 148 us -> 55.1 us
  starting transfers between devices: 66.6 us -> 126 us
  Pallas kernels: 0 us -> 47.9 us
  local copies, waits for them, and re-layouts: 61.3 us -> 26 us
    psum x1, waiting for transfers between devices: 378 us -> 0.01 us  [per_device(): lax.psum((grad_w_proj.astype(LOW), grad_w_fc.astype(LOW), grad_w_out.asty...]
    dot_general x32 -> x18, matrix products: 297 us -> 44.4 us  [the longest x1 6.89 us: per_device(): jnp.einsum('tc,tf->cf', second_low, hidden_grad, preferred_element_type=F32)]
    reduce_scatter x4 -> x0, waiting for transfers between devices: 221 us -> none  [the longest x1 102 us: per_device(): lax.psum_scatter(jnp.dot(heads_low, w_out, preferred_element_type=jnp.flo...]
    convert_element_type x9 -> x8, other arithmetic: 79 us -> 12.4 us  [the longest x1 4.22 us: per_device(): grad_w_fc.astype(F32)]
    ppermute x16 -> x63, waiting for transfers between devices: 264 us -> 198 us  [the longest x24 96.5 us: shift_dp(): lax.ppermute(value, 'dp', [(i, (i + steps) % count) for i in range(count)])]
    ppermute x16 -> x63, starting transfers between devices: 65.7 us -> 126 us  [the longest x24 60.7 us: shift_dp(): lax.ppermute(value, 'dp', [(i, (i + steps) % count) for i in range(count)])]
    pallas_call x0 -> x2, Pallas kernels: none -> 47.9 us  [the longest x1 26.5 us: attn_bwd(): pl.pallas_call(functools.partial(bwd_kernel, bq, bk, nt), out_shape=(jax....]
    all_gather x4 -> x0, waiting for transfers between devices: 45.4 us -> none  [the longest x1 22.7 us: per_device(): lax.all_gather(middle_grad.astype(jnp.bfloat16), 'tensor', axis=0, tiled=...]
  transfers between devices with their start and end apart: 25 -> 64, of which waited for: 11 -> 30; matrix products, arithmetic and copies ran while one was open for 4% -> 14% of each run, Pallas kernels for 0% -> 5%
where the time goes in v1:
time: 574 us; the launch traced here: 569 us
  waiting for transfers between devices  198 us (34%)
  starting transfers between devices  126 us (22%)
  other arithmetic  55.1 us (10%)
  blocking collectives  54.8 us (10%)
  Pallas kernels  47.9 us (8%)
  matrix products  44.4 us (8%)
  local copies, waits for them, and re-layouts  26 us (5%)
  between operations  15.6 us (3%)
    ppermute x24, waiting for transfers between devices, shift_dp(): lax.ppermute(value, 'dp', [(i, (i + steps) % count) for i in range(count)])  96.5 us
    ppermute x9, waiting for transfers between devices, swap_x(): lax.ppermute(value, 'tensor', [(i, i ^ 2) for i in range(lax.axis_size('t...  60.8 us
    ppermute x24, starting transfers between devices, shift_dp(): lax.ppermute(value, 'dp', [(i, (i + steps) % count) for i in range(count)])  60.7 us
    psum x1, blocking collectives, per_device(): small = lax.psum(small, ('dp', 'tensor'))  54.8 us
    ppermute x16, starting transfers between devices, shift_group(): lax.ppermute(value, 'dp', [(i, i // S * S + (i % S + steps) % S) for i in...  46.3 us
    ppermute x16, waiting for transfers between devices, shift_group(): lax.ppermute(value, 'dp', [(i, i // S * S + (i % S + steps) % S) for i in...  36.2 us
    pallas_call x1, Pallas kernels, attn_bwd(): pl.pallas_call(functools.partial(bwd_kernel, bq, bk, nt), out_shape=(jax....  26.5 us
    pallas_call x1, Pallas kernels, attn_fwd(): pl.pallas_call(functools.partial(fwd_kernel, bq, bk), out_shape=(jax.Shap...  21.3 us
  transfers between devices with their start and end apart: 64, of which 30 were waited for; matrix products, arithmetic and copies ran while one was open for 14% of the time, Pallas kernels for 5%

profile of v1, /device:TPU:0, one launch (start us, length us, event | category | flops | bytes accessed | tf_op | source)
XLA Modules:
  0.0 568.7 jit_solution(13805351451581080459)
XLA Ops:
  27.1 15.2 %collective-permute-done.2 = bf16[64,1024]{1,0:T(8,128)(2,1)S(1)} collective-permute-done((bf16[64,1024]{1,0:T(8,128)(2,1)S(1)}, bf16[64,1024]{1,0:T(8,128)(2,1)S(1)}, u32[]{:S(2)}, u32[]{:S(2)}) %collective-permute-start.2) | collective-permute-done | bytes 131104 | tf_op jit(solution)/shard_map/ppermute | solution.py:187
  42.3 7.3 %collective-permute-start.1 = (bf16[64,1024]{1,0:T(8,128)(2,1)S(1)}, bf16[64,1024]{1,0:T(8,128)(2,1)S(1)}, u32[]{:S(2)}, u32[]{:S(2)}) collective-permute-start(bf16[64,1024]{1,0:T(8,128)(2,1)S(1)} %get-tuple-element.80), channel_id=1, source_target_pairs={{0,16},{4,20},{8,24},{12,28},{16,0},{20,4},{24,8},{28,12},{1,17},{... | collective-permute-start | bytes 393224 | tf_op jit(solution)/shard_map/ppermute | solution.py:187
  64.6 5.6 collective-permute-done.8
  75.2 21.3 %attn_fwd.1 = (bf16[4,64,1024]{2,1,0:T(8,128)(2,1)S(1)}, f32[4,1,1024]{2,1,0:T(1,128)S(1)}) custom-call(s32[2]{0:T(128)S(1)} %pad_add_fusion.meta_ref, s32[4]{0:T(128)S(1)} %copy-done.4, bf16[4,64,1024]{2,1,0:T(8,128)(2,1)S(1)} %pad_maximum_fusion.2.q_ref, bf16[2,4,128,1024]{3,2,1,0:T(8,128)(2,1)S(1)} %pad_maximum_fusion.kv_ref), custom_call_target="tpu_custom_call" | custom-call | tf_op jit(solution)/shard_map/attn_fwd/pallas_call | solution.py:160
  107.4 6.1 %collective-permute-done.11 = bf16[64,1024]{1,0:T(8,128)(2,1)S(1)} collective-permute-done((bf16[64,1024]{1,0:T(8,128)(2,1)S(1)}, bf16[64,1024]{1,0:T(8,128)(2,1)S(1)}, u32[]{:S(2)}, u32[]{:S(2)}) %collective-permute-start.11) | collective-permute-done | bytes 131104 | tf_op jit(solution)/shard_map/ppermute | solution.py:187
  116.9 11.7 %collective-permute-done.14 = bf16[256,1024]{1,0:T(8,128)(2,1)} collective-permute-done((bf16[256,1024]{1,0:T(8,128)(2,1)}, bf16[256,1024]{1,0:T(8,128)(2,1)}, u32[]{:S(2)}, u32[]{:S(2)}) %collective-permute-start.14) | collective-permute-done | bytes 524320 | tf_op jit(solution)/shard_map/ppermute | solution.py:195
  130.9 5.7 %fusion.85 = (f32[1024]{0:T(1024)S(1)}, f32[1024,1024]{1,0:T(8,128)S(1)}) fusion(f32[1024]{0:T(1024)S(1)} %copy-done.35, bf16[256,1024]{1,0:T(8,128)(2,1)} %collective-permute-done.18, bf16[256,1024]{1,0:T(8,128)(2,1)} %collective-permute-done.17, bf16[256,1024]{1,0:T(8,128)(2,1)} %collective-permute-done.16, bf16[256,1024]{1,0:T(8,128)(2,1)} %param.22, ...), kind=kOutput, calls=%fused_computation.216 | convolution fusion | flops 2168454144 | bytes 10493952 | tf_op jit(solution)/shard_map/lt,ld->td/dot_general | solution.py:335
  172.6 10.6 %collective-permute-done.24 = bf16[256,1024]{1,0:T(8,128)(2,1)S(1)} collective-permute-done((bf16[256,1024]{1,0:T(8,128)(2,1)S(1)}, bf16[256,1024]{1,0:T(8,128)(2,1)S(1)}, u32[]{:S(2)}, u32[]{:S(2)}) %collective-permute-start.24) | collective-permute-done | bytes 524320 | tf_op jit(solution)/shard_map/ppermute | solution.py:195
  183.7 10.2 %collective-permute-done.20 = bf16[256,1024]{1,0:T(8,128)(2,1)S(1)} collective-permute-done((bf16[256,1024]{1,0:T(8,128)(2,1)S(1)}, bf16[256,1024]{1,0:T(8,128)(2,1)S(1)}, u32[]{:S(2)}, u32[]{:S(2)}) %collective-permute-start.20) | collective-permute-done | bytes 524320 | tf_op jit(solution)/shard_map/ppermute | solution.py:195
  197.7 10.6 %collective-permute-done.25 = bf16[256,1024]{1,0:T(8,128)(2,1)S(1)} collective-permute-done((bf16[256,1024]{1,0:T(8,128)(2,1)S(1)}, bf16[256,1024]{1,0:T(8,128)(2,1)S(1)}, u32[]{:S(2)}, u32[]{:S(2)}) %collective-permute-start.25) | collective-permute-done | bytes 524320 | tf_op jit(solution)/shard_map/ppermute | solution.py:195
  215.0 6.9 %convolution_convert_fusion.1 = bf16[1024,1024]{1,0:T(8,128)(2,1)} fusion(bf16[1024,1024]{1,0:T(8,128)(2,1)} %copy-done.40, f32[1024,1024]{1,0:T(8,128)} %copy-done.11, f32[1024]{0:T(1024)S(1)} %copy-done.37, f32[1024]{0:T(1024)S(1)} %copy-done.30, f32[1024]{0:T(1024)S(1)} %add_rsqrt_fusion, f32[1024]{0:T(1024)S(1)} %broadcast_multiply_fusion), kind=kOutput, calls=%fused_computation.44 | convolution fusion | flops 2153775104 | bytes 8404992 | tf_op jit(solution)/shard_map/tc,tf->cf/dot_general | solution.py:362
  221.9 6.3 %collective-permute-done.21 = bf16[256,1024]{1,0:T(8,128)(2,1)S(1)} collective-permute-done((bf16[256,1024]{1,0:T(8,128)(2,1)S(1)}, bf16[256,1024]{1,0:T(8,128)(2,1)S(1)}, u32[]{:S(2)}, u32[]{:S(2)}) %collective-permute-start.21) | collective-permute-done | bytes 524320 | tf_op jit(solution)/shard_map/ppermute | solution.py:195
  247.7 26.5 %attn_bwd.1 = (bf16[4,64,1024]{2,1,0:T(8,128)(2,1)S(1)}, bf16[2,4,128,1024]{3,2,1,0:T(8,128)(2,1)S(1)}) custom-call(s32[2]{0:T(128)S(1)} %pad_add_fusion.meta_ref, s32[4]{0:T(128)S(1)} %copy-done.4, bf16[4,64,1024]{2,1,0:T(8,128)(2,1)S(1)} %pad_maximum_fusion.2.q_ref, bf16[2,4,128,1024]{3,2,1,0:T(8,128)(2,1)S(1)} %copy-done.3, ...), custom_call_target="tpu_custom_call" | custom-call | tf_op jit(solution)/shard_map/attn_bwd/pallas_call | solution.py:168
  278.9 28.1 %collective-permute-start.34 = (bf16[128,1024]{1,0:T(8,128)(2,1)S(1)}, bf16[128,1024]{1,0:T(8,128)(2,1)S(1)}, u32[]{:S(2)}, u32[]{:S(2)}) collective-permute-start(bf16[128,1024]{1,0:T(8,128)(2,1)S(1)} %get-tuple-element.51), channel_id=1, source_target_pairs={{0,4},{4,0},{8,12},{12,8},{16,20},{20,16},{24,28},{28,24},{1,5},{5... | collective-permute-start | bytes 786440 | tf_op jit(solution)/shard_map/ppermute | solution.py:200
  309.1 7.5 %collective-permute-done.31 = bf16[64,1024]{1,0:T(8,128)(2,1)S(1)} collective-permute-done((bf16[64,1024]{1,0:T(8,128)(2,1)S(1)}, bf16[64,1024]{1,0:T(8,128)(2,1)S(1)}, u32[]{:S(2)}, u32[]{:S(2)}) %collective-permute-start.31) | collective-permute-done | bytes 131104 | tf_op jit(solution)/shard_map/ppermute | solution.py:187
  316.6 6.7 %collective-permute-done.32 = bf16[64,1024]{1,0:T(8,128)(2,1)S(1)} collective-permute-done((bf16[64,1024]{1,0:T(8,128)(2,1)S(1)}, bf16[64,1024]{1,0:T(8,128)(2,1)S(1)}, u32[]{:S(2)}, u32[]{:S(2)}) %collective-permute-start.32) | collective-permute-done | bytes 131104 | tf_op jit(solution)/shard_map/ppermute | solution.py:187
  340.2 19.1 %collective-permute-done.37 = bf16[128,1024]{1,0:T(8,128)(2,1)S(1)} collective-permute-done((bf16[128,1024]{1,0:T(8,128)(2,1)S(1)}, bf16[128,1024]{1,0:T(8,128)(2,1)S(1)}, u32[]{:S(2)}, u32[]{:S(2)}) %collective-permute-start.37) | collective-permute-done | bytes 262176 | tf_op jit(solution)/shard_map/ppermute | solution.py:187
  376.2 6.2 %collective-permute-done.52 = bf16[3,128,256]{2,1,0:T(8,128)(2,1)S(1)} collective-permute-done((bf16[3,128,256]{2,1,0:T(8,128)(2,1)S(1)}, bf16[3,128,256]{2,1,0:T(8,128)(2,1)S(1)}, u32[]{:S(2)}, u32[]{:S(2)}) %collective-permute-start.52) | collective-permute-done | bytes 196640 | tf_op jit(solution)/shard_map/ppermute | solution.py:200
  397.4 13.1 %collective-permute-done.53 = bf16[3,128,256]{2,1,0:T(8,128)(2,1)S(1)} collective-permute-done((bf16[3,128,256]{2,1,0:T(8,128)(2,1)}, bf16[3,128,256]{2,1,0:T(8,128)(2,1)S(1)}, u32[]{:S(2)}, u32[]{:S(2)}) %collective-permute-start.53) | collective-permute-done | bytes 196640 | tf_op jit(solution)/shard_map/ppermute | solution.py:187
  415.8 16.8 %collective-permute-start.57 = (bf16[3,128,256]{2,1,0:T(8,128)(2,1)S(1)}, bf16[3,128,256]{2,1,0:T(8,128)(2,1)S(1)}, u32[]{:S(2)}, u32[]{:S(2)}) collective-permute-start(bf16[3,128,256]{2,1,0:T(8,128)(2,1)S(1)} %get-tuple-element.38), channel_id=1, source_target_pairs={{0,8},{4,12},{8,16},{12,20},{16,24},{20,28},{24,0},{28,4},{1,9},{5... | collective-permute-start | bytes 589832 | tf_op jit(solution)/shard_map/ppermute | solution.py:187
  435.2 7.8 %collective-permute-done.57 = bf16[3,128,256]{2,1,0:T(8,128)(2,1)S(1)} collective-permute-done((bf16[3,128,256]{2,1,0:T(8,128)(2,1)S(1)}, bf16[3,128,256]{2,1,0:T(8,128)(2,1)S(1)}, u32[]{:S(2)}, u32[]{:S(2)}) %collective-permute-start.57) | collective-permute-done | bytes 196640 | tf_op jit(solution)/shard_map/ppermute | solution.py:187
  444.4 12.0 %collective-permute-done.59 = bf16[3,128,256]{2,1,0:T(8,128)(2,1)S(1)} collective-permute-done((bf16[3,128,256]{2,1,0:T(8,128)(2,1)S(1)}, bf16[3,128,256]{2,1,0:T(8,128)(2,1)S(1)}, u32[]{:S(2)}, u32[]{:S(2)}) %collective-permute-start.59) | collective-permute-done | bytes 196640 | tf_op jit(solution)/shard_map/ppermute | solution.py:187
  478.3 6.0 %collective-permute-done.42 = bf16[256,1024]{1,0:T(8,128)(2,1)S(1)} collective-permute-done((bf16[256,1024]{1,0:T(8,128)(2,1)S(1)}, bf16[256,1024]{1,0:T(8,128)(2,1)S(1)}, u32[]{:S(2)}, u32[]{:S(2)}) %collective-permute-start.42) | collective-permute-done | bytes 524320 | tf_op jit(solution)/shard_map/ppermute | solution.py:195
  486.6 54.8 %psum.29 = f32[8,1024]{1,0:T(8,128)S(1)} all-reduce(f32[8,1024]{1,0:T(8,128)S(1)} %concatenate.68), channel_id=1, replica_groups=mesh['dp'=8,'tensor'=4] {'dp','tensor'}, use_global_device_ids=true, to_apply=%region_22.23 | all-reduce | flops 8192 | bytes 65536 | tf_op jit(solution)/shard_map/psum | solution.py:386
  (319 shorter events, 230.9 us)
Async XLA Ops:
  7.2 546.3 %all-reduce.3.cloned.1.call-start = ((), (), s32[]{:S(2)}) async-start(), calls=%async_computation | async-start | bytes 9437184 | tf_op jit(solution)/shard_map/psum | solution.py:364
  16.0 35.3 %collective-permute-start.3 = (bf16[128,1024]{1,0:T(8,128)(2,1)}, bf16[128,1024]{1,0:T(8,128)(2,1)}, u32[]{:S(2)}, u32[]{:S(2)}) collective-permute-start(bf16[128,1024]{1,0:T(8,128)(2,1)} %get-tuple-element.63), channel_id=1, source_target_pairs={{0,8},{4,12},{8,16},{12,20},{16,24},{20,28},{24,0},{28,4},{1,9},{5... | collective-permute-start | bytes 786440 | tf_op jit(solution)/shard_map/ppermute | solution.py:187
  19.0 32.8 %collective-permute-start.4 = (bf16[128,1024]{1,0:T(8,128)(2,1)}, bf16[128,1024]{1,0:T(8,128)(2,1)}, u32[]{:S(2)}, u32[]{:S(2)}) collective-permute-start(bf16[128,1024]{1,0:T(8,128)(2,1)} %get-tuple-element.64), channel_id=1, source_target_pairs={{0,16},{4,20},{8,24},{12,28},{16,0},{20,4},{24,8},{28,12},{1,17},{... | collective-permute-start | bytes 786440 | tf_op jit(solution)/shard_map/ppermute | solution.py:187
  21.6 31.7 %collective-permute-start.5 = (bf16[128,1024]{1,0:T(8,128)(2,1)}, bf16[128,1024]{1,0:T(8,128)(2,1)}, u32[]{:S(2)}, u32[]{:S(2)}) collective-permute-start(bf16[128,1024]{1,0:T(8,128)(2,1)} %get-tuple-element.65), channel_id=1, source_target_pairs={{0,24},{4,28},{8,0},{12,4},{16,8},{20,12},{24,16},{28,20},{1,25},{... | collective-permute-start | bytes 786440 | tf_op jit(solution)/shard_map/ppermute | solution.py:187
  25.5 24.2 %collective-permute-start = (bf16[64,1024]{1,0:T(8,128)(2,1)S(1)}, bf16[64,1024]{1,0:T(8,128)(2,1)S(1)}, u32[]{:S(2)}, u32[]{:S(2)}) collective-permute-start(bf16[64,1024]{1,0:T(8,128)(2,1)S(1)} %get-tuple-element.81), channel_id=1, source_target_pairs={{0,8},{4,12},{8,16},{12,20},{16,24},{20,28},{24,0},{28,4},{1,9},{5... | collective-permute-start | bytes 393224 | tf_op jit(solution)/shard_map/ppermute | solution.py:187
  53.3 21.2 %collective-permute-start.9 = (bf16[128,1024]{1,0:T(8,128)(2,1)}, bf16[128,1024]{1,0:T(8,128)(2,1)S(1)}, u32[]{:S(2)}, u32[]{:S(2)}) collective-permute-start(bf16[128,1024]{1,0:T(8,128)(2,1)} %collective-permute-done.5), channel_id=1, source_target_pairs={{0,4},{4,0},{8,12},{12,8},{16,20},{20,16},{24,28},{28,24},{1,5},{5... | collective-permute-start | bytes 786440 | tf_op jit(solution)/shard_map/ppermute | solution.py:200
  171.5 22.5 %collective-permute-start.20 = (bf16[256,1024]{1,0:T(8,128)(2,1)S(1)}, bf16[256,1024]{1,0:T(8,128)(2,1)S(1)}, u32[]{:S(2)}, u32[]{:S(2)}) collective-permute-start(bf16[256,1024]{1,0:T(8,128)(2,1)S(1)} %dynamic-slice_convert_fusion.5), channel_id=1, source_target_pairs={{0,2},{1,3},{2,0},{3,1},{4,6},{5,7},{6,4},{7,5},{8,10},{9,11},{10,... | collective-permute-start | bytes 1572872 | tf_op jit(solution)/shard_map/ppermute | solution.py:195
  229.6 159.9 %collective-permute-start.22 = (bf16[512,1024]{1,0:T(8,128)(2,1)}, bf16[512,1024]{1,0:T(8,128)(2,1)}, u32[]{:S(2)}, u32[]{:S(2)}) collective-permute-start(bf16[512,1024]{1,0:T(8,128)(2,1)} %maximum_select_fusion.3), channel_id=1, source_target_pairs={{0,1},{1,0},{2,3},{3,2},{4,5},{5,4},{6,7},{7,6},{8,9},{9,8},{10,11... | collective-permute-start | bytes 3145736 | tf_op jit(solution)/shard_map/ppermute | solution.py:191
  274.3 34.7 %collective-permute-start.30 = (bf16[64,1024]{1,0:T(8,128)(2,1)S(1)}, bf16[64,1024]{1,0:T(8,128)(2,1)S(1)}, u32[]{:S(2)}, u32[]{:S(2)}) collective-permute-start(bf16[64,1024]{1,0:T(8,128)(2,1)S(1)} %get-tuple-element.68), channel_id=1, source_target_pairs={{0,24},{4,28},{8,0},{12,4},{16,8},{20,12},{24,16},{28,20},{1,25},{... | collective-permute-start | bytes 393224 | tf_op jit(solution)/shard_map/ppermute | solution.py:187
  278.9 47.6 %collective-permute-start.34 = (bf16[128,1024]{1,0:T(8,128)(2,1)S(1)}, bf16[128,1024]{1,0:T(8,128)(2,1)S(1)}, u32[]{:S(2)}, u32[]{:S(2)}) collective-permute-start(bf16[128,1024]{1,0:T(8,128)(2,1)S(1)} %get-tuple-element.51), channel_id=1, source_target_pairs={{0,4},{4,0},{8,12},{12,8},{16,20},{20,16},{24,28},{28,24},{1,5},{5... | collective-permute-start | bytes 786440 | tf_op jit(solution)/shard_map/ppermute | solution.py:200
  332.1 27.2 %collective-permute-start.37 = (bf16[128,1024]{1,0:T(8,128)(2,1)S(1)}, bf16[128,1024]{1,0:T(8,128)(2,1)S(1)}, u32[]{:S(2)}, u32[]{:S(2)}) collective-permute-start(bf16[128,1024]{1,0:T(8,128)(2,1)S(1)} %get-tuple-element.47), channel_id=1, source_target_pairs={{0,16},{4,20},{8,24},{12,28},{16,0},{20,4},{24,8},{28,12},{1,17},{... | collective-permute-start | bytes 786440 | tf_op jit(solution)/shard_map/ppermute | solution.py:187
  332.1 27.2 %collective-permute-start.39 = (bf16[128,1024]{1,0:T(8,128)(2,1)S(1)}, bf16[128,1024]{1,0:T(8,128)(2,1)S(1)}, u32[]{:S(2)}, u32[]{:S(2)}) collective-permute-start(bf16[128,1024]{1,0:T(8,128)(2,1)S(1)} %get-tuple-element.46), channel_id=1, source_target_pairs={{0,8},{4,12},{8,16},{12,20},{16,24},{20,28},{24,0},{28,4},{1,9},{5... | collective-permute-start | bytes 786440 | tf_op jit(solution)/shard_map/ppermute | solution.py:187
  364.8 21.8 %collective-permute-start.54 = (bf16[3,128,256]{2,1,0:T(8,128)(2,1)S(1)}, bf16[3,128,256]{2,1,0:T(8,128)(2,1)S(1)}, u32[]{:S(2)}, u32[]{:S(2)}) collective-permute-start(bf16[3,128,256]{2,1,0:T(8,128)(2,1)S(1)} %get-tuple-element.56), channel_id=1, source_target_pairs={{0,4},{4,0},{8,12},{12,8},{16,20},{20,16},{24,28},{28,24},{1,5},{5... | collective-permute-start | bytes 589832 | tf_op jit(solution)/shard_map/ppermute | solution.py:200
  370.2 89.0 %collective-permute-start.40 = (bf16[512,1024]{1,0:T(8,128)(2,1)}, bf16[512,1024]{1,0:T(8,128)(2,1)}, u32[]{:S(2)}, u32[]{:S(2)}) collective-permute-start(bf16[512,1024]{1,0:T(8,128)(2,1)} %dynamic-slice_convert_fusion), channel_id=1, source_target_pairs={{0,1},{1,0},{2,3},{3,2},{4,5},{5,4},{6,7},{7,6},{8,9},{9,8},{10,11... | collective-permute-start | bytes 3145736 | tf_op jit(solution)/shard_map/ppermute | solution.py:191
  374.3 23.2 %collective-permute-start.49 = (bf16[3,128,256]{2,1,0:T(8,128)(2,1)}, bf16[3,128,256]{2,1,0:T(8,128)(2,1)S(1)}, u32[]{:S(2)}, u32[]{:S(2)}) collective-permute-start(bf16[3,128,256]{2,1,0:T(8,128)(2,1)} %get-tuple-element.53), channel_id=1, source_target_pairs={{0,4},{4,0},{8,12},{12,8},{16,20},{20,16},{24,28},{28,24},{1,5},{5... | collective-permute-start | bytes 589832 | tf_op jit(solution)/shard_map/ppermute | solution.py:200
  387.6 22.9 %collective-permute-start.53 = (bf16[3,128,256]{2,1,0:T(8,128)(2,1)}, bf16[3,128,256]{2,1,0:T(8,128)(2,1)S(1)}, u32[]{:S(2)}, u32[]{:S(2)}) collective-permute-start(bf16[3,128,256]{2,1,0:T(8,128)(2,1)} %get-tuple-element.59), channel_id=1, source_target_pairs={{0,16},{4,20},{8,24},{12,28},{16,0},{20,4},{24,8},{28,12},{1,17},{... | collective-permute-start | bytes 589832 | tf_op jit(solution)/shard_map/ppermute | solution.py:187
  415.0 43.5 %collective-permute-start.56 = (bf16[3,128,256]{2,1,0:T(8,128)(2,1)S(1)}, bf16[3,128,256]{2,1,0:T(8,128)(2,1)S(1)}, u32[]{:S(2)}, u32[]{:S(2)}) collective-permute-start(bf16[3,128,256]{2,1,0:T(8,128)(2,1)S(1)} %get-tuple-element.38), channel_id=1, source_target_pairs={{0,4},{4,0},{8,12},{12,8},{16,20},{20,16},{24,28},{28,24},{1,5},{5... | collective-permute-start | bytes 589832 | tf_op jit(solution)/shard_map/ppermute | solution.py:200
  415.8 27.2 %collective-permute-start.57 = (bf16[3,128,256]{2,1,0:T(8,128)(2,1)S(1)}, bf16[3,128,256]{2,1,0:T(8,128)(2,1)S(1)}, u32[]{:S(2)}, u32[]{:S(2)}) collective-permute-start(bf16[3,128,256]{2,1,0:T(8,128)(2,1)S(1)} %get-tuple-element.38), channel_id=1, source_target_pairs={{0,8},{4,12},{8,16},{12,20},{16,24},{20,28},{24,0},{28,4},{1,9},{5... | collective-permute-start | bytes 589832 | tf_op jit(solution)/shard_map/ppermute | solution.py:187
  432.6 23.8 %collective-permute-start.59 = (bf16[3,128,256]{2,1,0:T(8,128)(2,1)S(1)}, bf16[3,128,256]{2,1,0:T(8,128)(2,1)S(1)}, u32[]{:S(2)}, u32[]{:S(2)}) collective-permute-start(bf16[3,128,256]{2,1,0:T(8,128)(2,1)S(1)} %get-tuple-element.38), channel_id=1, source_target_pairs={{0,16},{4,20},{8,24},{12,28},{16,0},{20,4},{24,8},{28,12},{1,17},{... | collective-permute-start | bytes 589832 | tf_op jit(solution)/shard_map/ppermute | solution.py:187
  433.6 23.9 %collective-permute-start.61 = (bf16[3,128,256]{2,1,0:T(8,128)(2,1)S(1)}, bf16[3,128,256]{2,1,0:T(8,128)(2,1)S(1)}, u32[]{:S(2)}, u32[]{:S(2)}) collective-permute-start(bf16[3,128,256]{2,1,0:T(8,128)(2,1)S(1)} %get-tuple-element.38), channel_id=1, source_target_pairs={{0,24},{4,28},{8,0},{12,4},{16,8},{20,12},{24,16},{28,20},{1,25},{... | collective-permute-start | bytes 589832 | tf_op jit(solution)/shard_map/ppermute | solution.py:187
  443.0 22.2 %collective-permute-start.58 = (bf16[3,128,256]{2,1,0:T(8,128)(2,1)S(1)}, bf16[3,128,256]{2,1,0:T(8,128)(2,1)S(1)}, u32[]{:S(2)}, u32[]{:S(2)}) collective-permute-start(bf16[3,128,256]{2,1,0:T(8,128)(2,1)S(1)} %collective-permute-done.57), channel_id=1, source_target_pairs={{0,4},{4,0},{8,12},{12,8},{16,20},{20,16},{24,28},{28,24},{1,5},{5... | collective-permute-start | bytes 589832 | tf_op jit(solution)/shard_map/ppermute | solution.py:200
  457.5 28.3 %collective-permute-start.62 = (bf16[3,128,256]{2,1,0:T(8,128)(2,1)S(1)}, bf16[3,128,256]{2,1,0:T(8,128)(2,1)S(1)}, u32[]{:S(2)}, u32[]{:S(2)}) collective-permute-start(bf16[3,128,256]{2,1,0:T(8,128)(2,1)S(1)} %collective-permute-done.61), channel_id=1, source_target_pairs={{0,4},{4,0},{8,12},{12,8},{16,20},{20,16},{24,28},{28,24},{1,5},{5... | collective-permute-start | bytes 589832 | tf_op jit(solution)/shard_map/ppermute | solution.py:200
  484.8 66.4 %collective-permute-start.43 = (bf16[512,1024]{1,0:T(8,128)(2,1)S(1)}, bf16[512,1024]{1,0:T(8,128)(2,1)S(1)}, u32[]{:S(2)}, u32[]{:S(2)}) collective-permute-start(bf16[512,1024]{1,0:T(8,128)(2,1)S(1)} %maximum_select_fusion.5), channel_id=1, source_target_pairs={{0,1},{1,0},{2,3},{3,2},{4,5},{5,4},{6,7},{7,6},{8,9},{9,8},{10,11... | collective-permute-start | bytes 3145736 | tf_op jit(solution)/shard_map/ppermute | solution.py:191
  485.7 55.7 %collective-permute-start.46 = (f32[4,1024]{1,0:T(4,128)S(1)}, f32[4,1024]{1,0:T(4,128)S(1)}, u32[]{:S(2)}, u32[]{:S(2)}) collective-permute-start(f32[4,1024]{1,0:T(4,128)S(1)} %add.538), channel_id=1, source_target_pairs={{0,4},{4,0},{8,12},{12,8},{16,20},{20,16},{24,28},{28,24},{1,5},{5... | collective-permute-start | bytes 49160 | tf_op jit(solution)/shard_map/ppermute | solution.py:435
  (81 other events, 932.6 us)
Sparse Core Ops, SparseCore 0:
  241.8 233.6 all-reduce.2

commit v2 on v0

v2 whole, which is shorter than its diff:
```python
import functools
import math

import jax
import jax.numpy as jnp
from jax import lax
from jax.experimental import pallas as pl
from jax.experimental.pallas import tpu as pltpu
from jax.sharding import PartitionSpec as P

HEAD_DIM = 64
NEG = -1e30
EPS = 1e-05
NN = (((1,), (0,)), ((), ()))
NT = (((1,), (1,)), ((), ()))
TN = (((0,), (0,)), ((), ()))
LOW = jnp.bfloat16
F32 = jnp.float32
MIB = 2**20
LITTLE = 0
V = pl.BlockSpec(memory_space=pltpu.VMEM)
M = pl.BlockSpec(memory_space=pltpu.SMEM)


def dotf(a, b, dims):
    return lax.dot_general(a, b, dims, preferred_element_type=F32)


def norm_rows(values, weight_row, shift_row):
    centred = values - jnp.mean(values, axis=-1, keepdims=True)
    spread = jnp.mean(centred * centred, axis=-1, keepdims=True)
    return centred * lax.rsqrt(spread + EPS) * weight_row + shift_row


def cost(flops, moved):
    return pl.CostEstimate(flops=LITTLE * flops, bytes_accessed=LITTLE * moved, transcendentals=0)


def seq_start(place, ends):
    start = jnp.zeros_like(place)
    for end in ends:
        start = jnp.where(place >= end, end, start)
    return start


def read_ends(seq_ref):
    ends = []
    total = jnp.int32(0)
    for s in range(seq_ref.shape[0] - 1):
        total = total + seq_ref[s]
        ends.append(total)
    return ends


def key_spot(kstart, own, J, S, T):
    block = kstart // T
    distance = lax.rem(own - lax.rem(block, S) + S, S)
    return distance * J + block // S, lax.rem(kstart, T)


def tile_range(q0, bq, bk, ends):
    t0 = seq_start(q0, ends) // bk
    t3 = (q0 + bq + bk - 1) // bk
    t2 = jnp.maximum(q0 // bk, t0)
    t1 = jnp.minimum((seq_start(q0 + bq - 1, ends) + bk - 1) // bk, t2)
    return t0, jnp.maximum(t1, t0), t2, t3


def fill(refs, dst, flip):
    J = refs[0].shape[0]
    for e, ref in enumerate(refs):

        def one(i, _, e=e, ref=ref):
            dst[e * J + i] = ref[i].T if flip else ref[i]
            return 0

        lax.fori_loop(0, J, one, 0)


def fwd_kernel(bq, bk, S, meta_ref, seq_ref, q_ref, *refs):
    k_refs, v_refs = refs[:S], refs[S : 2 * S]
    o_ref, lse_ref, kt_ref, vf_ref = refs[2 * S :]
    J, _, T = q_ref.shape
    ends = read_ends(seq_ref)
    fill(k_refs, kt_ref, True)
    fill(v_refs, vf_ref, False)
    per = T // bq
    rows = lax.broadcasted_iota(jnp.int32, (bk, bq), 0)

    def q_tile(i, _):
        s = i // per
        qo = pl.multiple_of(lax.rem(i, per) * bq, bq)
        q0 = (s * S + meta_ref[0]) * T + qo
        q = q_ref[s, :, pl.ds(qo, bq)]
        place = q0 + lax.broadcasted_iota(jnp.int32, (1, bq), 1)
        start = seq_start(place, ends)

        def tile(masked, kt, carry):
            m, l, acc = carry
            kstart = kt * bk
            spot, ko = key_spot(kstart, meta_ref[0], J, S, T)
            ko = pl.multiple_of(ko, bk)
            k = kt_ref[spot, pl.ds(ko, bk), :]
            v = vf_ref[spot, :, pl.ds(ko, bk)]
            sc = dotf(k, q, NN)
            if masked:
                sc = jnp.where((rows >= start - kstart) & (rows <= place - kstart), sc, NEG)
            m2 = jnp.maximum(m, jnp.max(sc, axis=0, keepdims=True))
            p = jnp.exp(sc - m2)
            a = jnp.exp(m - m2)
            l = l * a + jnp.sum(p, axis=0, keepdims=True)
            acc = acc * a + dotf(v, p.astype(LOW), NN)
            return m2, l, acc

        t0, t1, t2, t3 = tile_range(q0, bq, bk, ends)
        c = (jnp.full((1, bq), NEG, F32), jnp.zeros((1, bq), F32), jnp.zeros((HEAD_DIM, bq), F32))
        c = lax.fori_loop(t2, t3, functools.partial(tile, True), c)
        c = lax.fori_loop(t0, t1, functools.partial(tile, True), c)
        m, l, acc = lax.fori_loop(t1, t2, functools.partial(tile, False), c)
        o_ref[s, :, pl.ds(qo, bq)] = (acc / l).astype(LOW)
        lse_ref[s, :, pl.ds(qo, bq)] = m + jnp.log(l)
        return 0

    lax.fori_loop(0, J * per, q_tile, 0)


def bwd_kernel(bq, bk, S, meta_ref, seq_ref, q_ref, *refs):
    k_refs, v_refs = refs[:S], refs[S : 2 * S]
    o_ref, lse_ref, do_ref, dq_ref = refs[2 * S : 2 * S + 4]
    dk_refs, dv_refs = refs[2 * S + 4 : 3 * S + 4], refs[3 * S + 4 : 4 * S + 4]
    kt_ref, kf_ref, vt_ref, dk_acc, dv_acc = refs[4 * S + 4 :]
    J, _, T = q_ref.shape
    ends = read_ends(seq_ref)
    fill(k_refs, kt_ref, True)
    fill(k_refs, kf_ref, False)
    fill(v_refs, vt_ref, True)
    dk_acc[...] = jnp.zeros_like(dk_acc)
    dv_acc[...] = jnp.zeros_like(dv_acc)
    per = T // bq
    rows = lax.broadcasted_iota(jnp.int32, (bk, bq), 0)

    def q_tile(i, _):
        s = i // per
        qo = pl.multiple_of(lax.rem(i, per) * bq, bq)
        q0 = (s * S + meta_ref[0]) * T + qo
        q = q_ref[s, :, pl.ds(qo, bq)]
        do = do_ref[s, :, pl.ds(qo, bq)]
        lse = lse_ref[s, :, pl.ds(qo, bq)]
        o = o_ref[s, :, pl.ds(qo, bq)].astype(F32)
        delta = jnp.sum(do.astype(F32) * o, axis=0, keepdims=True)
        place = q0 + lax.broadcasted_iota(jnp.int32, (1, bq), 1)
        start = seq_start(place, ends)

        def tile(masked, kt, dq):
            kstart = kt * bk
            spot, ko = key_spot(kstart, meta_ref[0], J, S, T)
            ko = pl.multiple_of(ko, bk)
            sc = dotf(kt_ref[spot, pl.ds(ko, bk), :], q, NN)
            p = jnp.exp(sc - lse)
            if masked:
                p = jnp.where((rows >= start - kstart) & (rows <= place - kstart), p, 0.0)
            dp = dotf(vt_ref[spot, pl.ds(ko, bk), :], do, NN)
            ds = (p * (dp - delta)).astype(LOW)
            dv_acc[spot, :, pl.ds(ko, bk)] += dotf(do, p.astype(LOW), NT)
            dk_acc[spot, :, pl.ds(ko, bk)] += dotf(q, ds, NT)
            return dq + dotf(kf_ref[spot, :, pl.ds(ko, bk)], ds, NN)

        t0, t1, t2, t3 = tile_range(q0, bq, bk, ends)
        dq = jnp.zeros((HEAD_DIM, bq), F32)
        dq = lax.fori_loop(t2, t3, functools.partial(tile, True), dq)
        dq = lax.fori_loop(t0, t1, functools.partial(tile, True), dq)
        dq = lax.fori_loop(t1, t2, functools.partial(tile, False), dq)
        dq_ref[s, :, pl.ds(qo, bq)] = (dq * 0.125).astype(LOW)
        return 0

    lax.fori_loop(0, J * per, q_tile, 0)
    for e in range(S):
        dk_refs[e][...] = dk_acc[e * J : (e + 1) * J].astype(LOW)
        dv_refs[e][...] = dv_acc[e * J : (e + 1) * J].astype(LOW)


def attn_params(keys):
    return pltpu.CompilerParams(vmem_limit_bytes=(58 if keys > 8192 else 40) * MIB)


def attn_fwd(meta, seq, q, ks, vs, bq=512, bk=512):
    J, _, T = q.shape
    S = len(ks)
    return pl.pallas_call(
        functools.partial(fwd_kernel, bq, bk, S),
        out_shape=(
            jax.ShapeDtypeStruct((J, HEAD_DIM, T), LOW),
            jax.ShapeDtypeStruct((J, 1, T), F32),
        ),
        in_specs=[M, M] + [V] * (1 + 2 * S),
        out_specs=(V, V),
        scratch_shapes=[
            pltpu.VMEM((S * J, T, HEAD_DIM), LOW),
            pltpu.VMEM((S * J, HEAD_DIM, T), LOW),
        ],
        compiler_params=attn_params(S * J * T),
        cost_estimate=cost(36 * 10**9, 4 * MIB),
        name="attn_fwd",
    )(meta, seq, q, *ks, *vs)


def attn_bwd(meta, seq, q, ks, vs, o, lse, do, bq=512, bk=512):
    J, _, T = q.shape
    S = len(ks)
    block = jax.ShapeDtypeStruct((J, HEAD_DIM, T), LOW)
    out = pl.pallas_call(
        functools.partial(bwd_kernel, bq, bk, S),
        out_shape=[block] * (1 + 2 * S),
        in_specs=[M, M] + [V] * (4 + 2 * S),
        out_specs=[V] * (1 + 2 * S),
        scratch_shapes=[
            pltpu.VMEM((S * J, T, HEAD_DIM), LOW),
            pltpu.VMEM((S * J, HEAD_DIM, T), LOW),
            pltpu.VMEM((S * J, T, HEAD_DIM), LOW),
            pltpu.VMEM((S * J, HEAD_DIM, T), F32),
            pltpu.VMEM((S * J, HEAD_DIM, T), F32),
        ],
        compiler_params=attn_params(S * J * T),
        cost_estimate=cost(10**6, 1000),
        name="attn_bwd",
    )(meta, seq, q, *ks, *vs, o, lse, do)
    return out[0], out[1 : 1 + S], out[1 + S :]


def qkv_kernel(x_ref, gain_ref, bias_ref, w_ref, b_ref, n_ref, q_ref, k_ref, v_ref):
    J = q_ref.shape[0]
    normed = norm_rows(x_ref[...].astype(F32), gain_ref[...], bias_ref[...]).astype(LOW)
    n_ref[...] = normed
    rows = normed.shape[0]
    for i, ref in ((1, k_ref), (2, v_ref), (0, q_ref)):
        made = dotf(normed, w_ref[i], NN)
        if i != 1:
            made = made + b_ref[i // 2][None]
        made = made.astype(LOW)
        if i == 0:
            made = (made * 0.125).astype(LOW)
        ref[...] = made.T.reshape(J, HEAD_DIM, rows)


def qkv(x, gain, bias, w, b):
    T, D = x.shape
    local = w.shape[2]
    J = local // HEAD_DIM
    rows = 256
    row_spec = pl.BlockSpec((rows, D), lambda i: (i, 0))
    head_spec = pl.BlockSpec((J, HEAD_DIM, rows), lambda i: (0, 0, i))
    heads = jax.ShapeDtypeStruct((J, HEAD_DIM, T), LOW)
    return pl.pallas_call(
        qkv_kernel,
        grid=(T // rows,),
        out_shape=(jax.ShapeDtypeStruct((T, D), LOW), heads, heads, heads),
        in_specs=[row_spec, V, V, V, V],
        out_specs=(row_spec, head_spec, head_spec, head_spec),
        compiler_params=pltpu.CompilerParams(vmem_limit_bytes=24 * MIB),
        cost_estimate=cost(6 * T * D * local, 8 * MIB),
        name="norm_qkv",
    )(x, gain[None], bias[None], w, b)


def out_kernel(pos_ref, o0, o1, o2, o3, w_ref, x_ref, b_ref, gain_ref, bias_ref, x1_ref, n2_ref, held):
    i = pl.program_id(0)
    rows = x1_ref.shape[0]

    @pl.when(i == 0)
    def _():
        for r, piece in enumerate((o0, o1, o2, o3)):
            held[pos_ref[r]] = piece[...]

    lanes = pl.ds(pl.multiple_of(i * rows, rows), rows)
    o = held[:, :, lanes].reshape(-1, rows)
    middle = x_ref[...].astype(F32) + dotf(o, w_ref[...], TN) + b_ref[...]
    x1_ref[...] = middle
    n2_ref[...] = norm_rows(middle, gain_ref[...], bias_ref[...]).astype(LOW)


def out_stage(pos, pieces, w, x, b, gain, bias):
    T, D = x.shape
    local = pieces[0].shape[0]
    rows = 256
    row_spec = pl.BlockSpec((rows, D), lambda i: (i, 0))
    return pl.pallas_call(
        out_kernel,
        grid=(T // rows,),
        out_shape=(jax.ShapeDtypeStruct((T, D), F32), jax.ShapeDtypeStruct((T, D), LOW)),
        in_specs=[M, V, V, V, V, V, row_spec, V, V, V],
        out_specs=(row_spec, row_spec),
        scratch_shapes=[pltpu.VMEM((4, local, T), LOW)],
        compiler_params=pltpu.CompilerParams(vmem_limit_bytes=32 * MIB),
        cost_estimate=cost(2 * T * D * 4 * local, 12 * MIB),
        name="out_norm",
    )(pos, *pieces, w, x, b[None], gain[None], bias[None])


def mlp_kernel(at_ref, n2_ref, dm_ref, wf_ref, wp_ref, b_ref, *refs):
    g_ref, dh_ref, dn2_ref, db_ref = refs[-4:]
    hidden = dotf(n2_ref[...], wf_ref[...], NN) + b_ref[...]
    back = dotf(dm_ref[...], wp_ref[...], NT)
    root = math.sqrt(2.0 / math.pi)
    square = hidden * hidden
    bent = jnp.tanh(root * hidden * (1.0 + 0.044715 * square))
    half = 0.5 * (1.0 + bent)
    g_ref[...] = (hidden * half).astype(LOW)
    slope = half + 0.5 * hidden * (1.0 - bent * bent) * (root * (1.0 + 3 * 0.044715 * square))
    dh = (back * slope).astype(LOW)
    dh_ref[...] = dh
    dn2_ref[...] = dotf(dh, wf_ref[...], NT).astype(LOW)

    @pl.when(pl.program_id(0) == 0)
    def _():
        db_ref[...] = jnp.zeros_like(db_ref)

    db_ref[...] += jnp.sum(dh.astype(F32), axis=0, keepdims=True)


def mlp_stage(at, n2, dm, w_fc, w_proj, b_fc, before=()):
    T, D = n2.shape
    F = w_fc.shape[1]
    rows = 256
    steps = T // 2 // rows
    row_spec = pl.BlockSpec((rows, D), lambda i, at: (at[0] * steps + i, 0))
    hid_spec = pl.BlockSpec((rows, F), lambda i, at: (at[0] * steps + i, 0))
    own_spec = pl.BlockSpec((rows, D), lambda i, at: (i, 0))
    whole = pl.BlockSpec(memory_space=pltpu.VMEM)
    return pl.pallas_call(
        mlp_kernel,
        grid_spec=pltpu.PrefetchScalarGridSpec(
            num_scalar_prefetch=1,
            grid=(steps,),
            in_specs=[row_spec, row_spec, whole, whole, whole]
            + [pl.BlockSpec(memory_space=pl.ANY)] * len(before),
            out_specs=(hid_spec, hid_spec, own_spec, whole),
        ),
        out_shape=(
            jax.ShapeDtypeStruct((T, F), LOW),
            jax.ShapeDtypeStruct((T, F), LOW),
            jax.ShapeDtypeStruct((T // 2, D), LOW),
            jax.ShapeDtypeStruct((1, F), F32),
        ),
        input_output_aliases={6 + i: i for i in range(len(before))},
        compiler_params=pltpu.CompilerParams(vmem_limit_bytes=40 * MIB),
        cost_estimate=cost(3 * T * D * F, 9 * MIB),
        name="feed",
    )(at, n2, dm, w_fc, w_proj, b_fc[None], *before)


def back_kernel(at_ref, own_ref, crossed_ref, x_ref, kept_ref, gain_ref, wide_ref, low_ref, sums_ref):
    grad = own_ref[...].astype(F32) + crossed_ref[...].astype(F32)
    values = x_ref[...].astype(F32)
    centred = values - jnp.mean(values, axis=-1, keepdims=True)
    factor = lax.rsqrt(jnp.mean(centred * centred, axis=-1, keepdims=True) + EPS)
    z = centred * factor
    u = grad * gain_ref[...]
    mean_u = jnp.mean(u, axis=-1, keepdims=True)
    mean_uz = jnp.mean(u * z, axis=-1, keepdims=True)
    made = kept_ref[...].astype(F32) + factor * (u - mean_u - z * mean_uz)
    wide_ref[...] = made
    low = made.astype(LOW)
    low_ref[...] = low

    @pl.when(pl.program_id(0) == 0)
    def _():
        sums_ref[...] = jnp.zeros_like(sums_ref)

    for i, part in enumerate((grad * z, grad, low.astype(F32), kept_ref[...].astype(F32))):
        sums_ref[i : i + 1, :] += jnp.sum(part, axis=0, keepdims=True)


def norm_back(at, own, crossed, x, kept, gain):
    half, D = own.shape
    rows = 256
    steps = half // rows
    spec = pl.BlockSpec((rows, D), lambda i, at: (i, 0))
    from_whole = pl.BlockSpec((rows, D), lambda i, at: (at[0] * steps + i, 0))
    whole = pl.BlockSpec(memory_space=pltpu.VMEM)
    return pl.pallas_call(
        back_kernel,
        grid_spec=pltpu.PrefetchScalarGridSpec(
            num_scalar_prefetch=1,
            grid=(steps,),
            in_specs=[spec, spec, from_whole, spec if kept.shape[0] == half else from_whole, whole],
            out_specs=(spec, spec, whole),
        ),
        out_shape=(
            jax.ShapeDtypeStruct((half, D), F32),
            jax.ShapeDtypeStruct((half, D), LOW),
            jax.ShapeDtypeStruct((4, D), F32),
        ),
        compiler_params=pltpu.CompilerParams(vmem_limit_bytes=24 * MIB),
        cost_estimate=cost(0, 14 * half * D),
        name="norm_back",
    )(at, own, crossed, x, kept, gain[None])


def first_kernel(core_ref, q_ref, k_ref, v_ref, w_ref, keep_ref, send_ref):
    half = keep_ref.shape[0]
    for out, at in ((send_ref, 1 - core_ref[0]), (keep_ref, core_ref[0])):
        lanes = pl.ds(pl.multiple_of(at * half, half), half)
        total = jnp.zeros(out.shape, F32)
        for i, ref in enumerate((q_ref, k_ref, v_ref)):
            total += dotf(ref[:, lanes].T, w_ref[i], NT)
        out[...] = total.astype(LOW)


def first_stage(core, q, k, v, w):
    local, T = q.shape
    D = w.shape[1]
    part = jax.ShapeDtypeStruct((T // 2, D), LOW)
    return pl.pallas_call(
        first_kernel,
        out_shape=(part, part),
        in_specs=[M, V, V, V, V],
        out_specs=(V, V),
        compiler_params=pltpu.CompilerParams(vmem_limit_bytes=24 * MIB),
        cost_estimate=cost(10**6, 1000),
        name="first_grad",
    )(core, q, k, v, w)


def feed_grads_kernel(g_ref, dm_ref, n2_ref, dh_ref, out_ref):
    steps = pl.num_programs(0) // 2
    rows = out_ref.shape[0]
    i = pl.program_id(0)
    lanes = pl.ds(pl.multiple_of(i % steps * rows, rows), rows)

    @pl.when(i < steps)
    def _():
        out_ref[...] = dotf(g_ref[:, lanes], dm_ref[...], TN).astype(LOW)

    @pl.when(i >= steps)
    def _():
        out_ref[...] = dotf(n2_ref[:, lanes], dh_ref[...], TN).astype(LOW)


def feed_grads(g, dm, n2, dh):
    T, F = g.shape
    D = dm.shape[1]
    rows = 256
    return pl.pallas_call(
        feed_grads_kernel,
        grid=((F + D) // rows,),
        out_shape=jax.ShapeDtypeStruct((F + D, D), LOW),
        in_specs=[V] * 4,
        out_specs=pl.BlockSpec((rows, D), lambda i: (i, 0)),
        compiler_params=pltpu.CompilerParams(vmem_limit_bytes=32 * MIB),
        cost_estimate=cost(4 * T * D * F, 12 * MIB),
        name="feed_grads",
    )(g, dm, n2, dh)


def do_kernel(core_ref, own_ref, other_ref, w_ref, o_ref, do_ref, grad_ref):
    half = own_ref.shape[0]
    grad = jnp.zeros(grad_ref.shape, F32)
    for ref, at in ((own_ref, core_ref[0]), (other_ref, 1 - core_ref[0])):
        lanes = pl.ds(pl.multiple_of(at * half, half), half)
        do_ref[:, lanes] = dotf(w_ref[...], ref[...], NT).astype(LOW)
        grad += dotf(o_ref[:, lanes], ref[...], NN)
    grad_ref[...] = grad.astype(LOW)


def do_stage(core, own, other, w_out, o_home):
    local, D = w_out.shape
    T = o_home.shape[1]
    return pl.pallas_call(
        do_kernel,
        out_shape=(jax.ShapeDtypeStruct((local, T), LOW), jax.ShapeDtypeStruct((local, D), LOW)),
        in_specs=[M, V, V, V, V],
        out_specs=(V, V),
        compiler_params=pltpu.CompilerParams(vmem_limit_bytes=24 * MIB),
        cost_estimate=cost(4 * T * D * local, 5 * MIB),
        name="heads_grad",
    )(core, own, other, w_out, o_home)


def grad_kernel(share, spot_ref, dq_ref, dk_ref, dv_ref, own_ref, *refs):
    parts, out_ref = refs[:-1], refs[-1]
    J = dq_ref.shape[0]
    for i, ref in enumerate((dq_ref, dk_ref, dv_ref)):
        total = dotf(ref[spot_ref[4]], own_ref[...], NN)
        for r, part in enumerate(parts):
            lanes = pl.ds(pl.multiple_of(spot_ref[r], share), share)
            for s in range(1, J):
                total += dotf(ref[spot_ref[4 + s], :, lanes], part[s - 1], NN)
        out_ref[i * HEAD_DIM : (i + 1) * HEAD_DIM] = total


def grad_heads(spots, dq, dk, dv, own, parts):
    J, _, T = dq.shape
    D = own.shape[1]
    return pl.pallas_call(
        functools.partial(grad_kernel, parts[0].shape[1]),
        out_shape=jax.ShapeDtypeStruct((3 * HEAD_DIM, D), F32),
        in_specs=[M] + [V] * (4 + len(parts)),
        out_specs=V,
        compiler_params=pltpu.CompilerParams(vmem_limit_bytes=24 * MIB),
        cost_estimate=cost(10**6, 1000),
        name="grad_heads",
    )(spots, dq, dk, dv, own, *parts)


def lay_kernel(S, spot_ref, *refs):
    parts, (qkv_ref, out_ref, held) = refs[:-3], refs[-3:]
    J, depth, _ = held.shape
    wide = parts[0].shape[1]
    few = (parts[0].shape[0] - depth) // S
    for i, part in enumerate(parts):
        jj, gg = spot_ref[2 * i], spot_ref[2 * i + 1]
        held[jj, :, pl.ds(pl.multiple_of(gg * wide, wide), wide)] = part[:depth]
        rest = part[depth:].astype(F32)
        rows = pl.ds(pl.multiple_of((gg * J + jj) * few, few), few)
        for e in range(S):
            out_ref[rows, e * wide : (e + 1) * wide] = rest[e * few : (e + 1) * few]
    for k in range(3):
        rows = [held[h, k * HEAD_DIM : (k + 1) * HEAD_DIM, :] for h in range(J)]
        qkv_ref[k] = jnp.concatenate(rows, 0).astype(F32).T


def lay_blocks(found, J, S):
    parts = [part for _, _, part in found]
    wide = parts[0].shape[1]
    spots = jnp.stack([x for jj, gg, _ in found for x in (jj, gg)]).astype(jnp.int32)
    return pl.pallas_call(
        functools.partial(lay_kernel, S),
        out_shape=(
            jax.ShapeDtypeStruct((3, S * wide, J * HEAD_DIM), F32),
            jax.ShapeDtypeStruct((J * HEAD_DIM, S * wide), F32),
        ),
        in_specs=[M] + [V] * len(parts),
        out_specs=(V, V),
        scratch_shapes=[pltpu.VMEM((J, 3 * HEAD_DIM, S * wide), LOW)],
        compiler_params=pltpu.CompilerParams(vmem_limit_bytes=24 * MIB),
        cost_estimate=cost(0, 6 * MIB),
        name="lay_blocks",
    )(spots, *parts)


def pair_kernel(core_ref, own_ref, other_ref, out_ref):
    half = own_ref.shape[0]
    for ref, at in ((own_ref, core_ref[0]), (other_ref, 1 - core_ref[0])):
        out_ref[pl.ds(pl.multiple_of(at * half, half), half), :] = ref[...]


def lay_pair(core, own, other):
    half, D = own.shape
    return pl.pallas_call(
        pair_kernel,
        out_shape=jax.ShapeDtypeStruct((2 * half, D), own.dtype),
        in_specs=[M, V, V],
        out_specs=V,
        compiler_params=pltpu.CompilerParams(vmem_limit_bytes=16 * MIB),
        cost_estimate=cost(0, 8 * half * D),
        name="lay_pair",
    )(core, own, other)


def shift_dp(value, steps):
    count = lax.axis_size("dp")
    return lax.ppermute(value, "dp", [(i, (i + steps) % count) for i in range(count)])


def shift_group(value, steps, S):
    count = lax.axis_size("dp")
    return lax.ppermute(
        value, "dp", [(i, i // S * S + (i % S + steps) % S) for i in range(count)]
    )


def swap_core(value):
    return lax.ppermute(value, "tensor", [(i, i ^ 1) for i in range(lax.axis_size("tensor"))])


def swap_x(value):
    return lax.ppermute(value, "tensor", [(i, i ^ 2) for i in range(lax.axis_size("tensor"))])


def rows_at(value, start, count):
    return lax.dynamic_slice_in_dim(value, start, count, 0)


def pick(value, index):
    return lax.dynamic_index_in_dim(value, index, 0, keepdims=False)


def gate(value, *before):
    return lax.optimization_barrier((value, *before))[0]


def tied(*values):
    return lax.optimization_barrier(values)


def sum_group(parts, g, S):
    total = pick(parts, g).astype(F32)
    for e in range(1, S):
        total = total + shift_group(pick(parts, (g + e) % S).astype(LOW), e, S).astype(F32)
    return total


def spread_blocks(blocks, j, g, S):
    J = len(blocks)
    found = []
    for s, part in enumerate(blocks):
        found.append(((j - s) % J, g, part))
        for e in range(1, S):
            found.append(((j - s) % J, (g - e) % S, shift_group(part, e, S)))
    return found


def add_low(own, other):
    return (own.astype(F32) + other.astype(F32)).astype(LOW)


def per_device(
    block_input,
    output_grad,
    seq_lengths,
    ln1_gain,
    ln1_bias,
    w_qkv,
    b_qv,
    w_out,
    b_out,
    ln2_gain,
    ln2_bias,
    w_fc,
    b_fc,
    w_proj,
    b_proj,
):
    T, D = block_input.shape
    local = w_qkv.shape[2]
    J = local // HEAD_DIM
    count = lax.axis_size("dp")
    S = count // J
    place = lax.axis_index("dp")
    j, g = place // S, place % S
    tensor = lax.axis_index("tensor")
    core, side = tensor % 2, tensor // 2
    half, share = T // 2, T // 4
    core_at = core[None].astype(jnp.int32)
    meta = g[None].astype(jnp.int32)
    groups = [[S * jj + gg for jj in range(J)] for gg in range(S)]

    def exchange(heads):
        return lax.all_to_all(heads, "dp", 0, 0, tiled=True, axis_index_groups=groups)

    def group(value):
        return [value] + [shift_group(value, e, S) for e in range(1, S)]

    first_low, queries, keys, values = qkv(block_input, ln1_gain, ln1_bias, w_qkv, b_qv)
    k_own, across = tied(exchange(keys), swap_x(w_out))
    ks = group(k_own)
    vs = group(gate(exchange(values), *ks[1:]))
    q_all = exchange(queries)

    pieces = jnp.stack([w_out, swap_core(w_out), across, swap_core(across)])
    order = jnp.stack([tensor ^ r for r in range(4)]).astype(jnp.int32)
    w_out_all = jnp.concatenate([pick(pieces, tensor ^ r) for r in range(4)], 0)

    q_all = gate(q_all, w_out_all)
    o_all, lse = attn_fwd(meta, seq_lengths, q_all, ks, vs)

    own_quarter = rows_at(first_low, core * half + side * share, share)
    o_home = exchange(o_all).reshape(local, T)
    own_quarter = gate(own_quarter, o_home)
    norm_own = lax.all_gather(own_quarter, "dp", axis_index_groups=groups)

    across = swap_x(o_home)
    o_pieces = (o_home, swap_core(o_home), across, swap_core(across))
    middle, second_low = out_stage(order, o_pieces, w_out_all, block_input, b_out, ln2_gain, ln2_bias)
    active_low, hidden_grad, sent, bias_one = mlp_stage(
        1 - core_at, second_low, output_grad, w_fc, w_proj, b_fc
    )
    arrived = swap_core(sent)
    active_low, hidden_grad, kept, bias_two = mlp_stage(
        core_at, second_low, output_grad, w_fc, w_proj, b_fc, (active_low, hidden_grad)
    )
    grad_b_fc = bias_one + bias_two
    second_half = add_low(kept, arrived)
    crossed = swap_x(second_half)
    grad_feed = feed_grads(active_low, output_grad, second_low, hidden_grad)
    feed_part = lax.psum_scatter(grad_feed, "dp", scatter_dimension=0, tiled=True)
    feed_made = dotf(gate(active_low, second_half), w_proj, NN).astype(LOW)
    feed_own = add_low(
        rows_at(feed_made, core * half, half),
        swap_core(rows_at(feed_made, (1 - core) * half, half)),
    )
    rolled = jnp.stack([pick(norm_own, (j + s) % J) for s in range(1, J)])
    crossed = gate(crossed, grad_feed, rolled, feed_own)
    middle_grad, branch_half, sums_two = norm_back(
        core_at, second_half, crossed, middle, output_grad, ln2_gain
    )
    heads_grad, grad_w_out = do_stage(core_at, branch_half, swap_core(branch_half), w_out, o_home)
    do_all = exchange(heads_grad.reshape(J, HEAD_DIM, T))
    out_cut = grad_w_out.reshape(S, J, local // count, D)
    out_moved = [shift_group(pick(out_cut, (g + e) % S), e, S) for e in range(1, S)]

    norm_across = swap_x(gate(rolled, branch_half))
    feed_across = swap_x(gate(feed_own, branch_half))

    dq, dks, dvs = attn_bwd(meta, seq_lengths, q_all, ks, vs, o_all, lse, do_all)
    dq, dks, dvs, feed_across, norm_across, out_moved = tied(
        dq, dks, dvs, feed_across, norm_across, out_moved
    )

    feed_sum = feed_own.astype(F32) + feed_across.astype(F32)
    middle_half = rows_at(middle, core * half, half)
    output_half = (middle_half + (feed_sum + b_proj)).astype(LOW)
    block_output = lay_pair(core_at, output_half, swap_core(output_half))
    norm_parts = [rolled, norm_across, swap_core(rolled), swap_core(norm_across)]

    def regroup(parts):
        return [shift_group(part, -e, S) for e, part in enumerate(parts) if e]

    def total(own, moved):
        for part in moved:
            own = own.astype(F32) + part.astype(F32)
        return own.astype(LOW)

    q_home, dk_moved = tied(exchange(dq), regroup(dks))
    dk = total(dks[0], dk_moved)
    k_home, dv_moved = tied(exchange(gate(dk, q_home)), regroup(dvs))
    dv = total(dvs[0], dv_moved)
    v_home = exchange(gate(dv, k_home))
    q_home, k_home, v_home = (x.reshape(local, T) for x in (q_home, k_home, v_home))

    spots = jnp.stack(
        [
            c * half + d * share
            for c, d in ((core, side), (core, 1 - side), (1 - core, side), (1 - core, 1 - side))
        ]
        + [(j + s) % J for s in range(J)]
    ).astype(jnp.int32)
    head_grad = grad_heads(spots, dq, dk, dv, first_low, norm_parts)
    v_home, head_grad, feed_part, block_output = tied(v_home, head_grad, feed_part, block_output)
    grad_feed = lax.all_gather(feed_part, "dp", axis=0, tiled=True)
    kept, sent = first_stage(core_at, q_home, k_home, v_home, w_qkv)
    first_half = add_low(kept, swap_core(sent))
    head_grad = gate(head_grad, first_half)
    cut = head_grad.reshape(3 * HEAD_DIM, S, D // S).transpose(1, 0, 2)
    head_grad = sum_group(cut, g, S).astype(LOW)
    grad_w_out = gate(pick(out_cut, g), first_half)
    grad_w_out = jnp.sum(exchange(total(grad_w_out, out_moved)).astype(F32), axis=0).astype(LOW)
    block = jnp.concatenate([head_grad] + jnp.split(grad_w_out, S, axis=1), 0)
    blocks = [shift_dp(block, s * S) for s in range(1, J)]

    first_across = gate(swap_x(first_half), block)
    _, input_half, sums_one = norm_back(
        core_at, first_half, first_across, block_input, middle_grad, ln1_gain
    )
    input_half, sums_one, blocks = tied(input_half, sums_one, blocks)
    input_grad = lay_pair(core_at, input_half, swap_core(input_half))
    grad_w_proj = grad_feed[: w_proj.shape[0]].astype(F32)
    grad_w_fc = grad_feed[w_proj.shape[0] :].astype(F32)
    found = spread_blocks([block, *blocks], j, g, S)
    grad_w_qkv, grad_w_out = lay_blocks(found, J, S)

    hidden_width = grad_b_fc.shape[1]
    wide_fc = lax.dynamic_update_slice_in_dim(
        jnp.zeros((1, hidden_width * lax.axis_size("tensor")), F32),
        grad_b_fc,
        tensor * hidden_width,
        1,
    ).reshape(-1, D)
    bias_qv = jnp.stack([jnp.sum(q_home.astype(F32), axis=1), jnp.sum(v_home.astype(F32), axis=1)])
    wide_qv = lax.dynamic_update_slice_in_dim(jnp.zeros((2, D), F32), bias_qv, tensor * local, 1)
    early = jnp.concatenate([wide_fc, wide_qv], 0)
    early = early + swap_x(early)
    small = jnp.concatenate([sums_two, sums_one[:2], early], 0)
    small = small + swap_core(small)
    step = 1
    while step < count:
        small = small + lax.ppermute(small, "dp", [(i, i ^ step) for i in range(count)])
        step *= 2
    tail = small.shape[0] - 2
    grad_b_qv = lax.dynamic_slice_in_dim(small[tail:], tensor * local, local, 1)
    grad_b_fc = rows_at(small[6:tail].reshape(-1), tensor * hidden_width, hidden_width)
    return (
        block_output,
        input_grad,
        small[4],
        small[5],
        grad_w_qkv,
        grad_b_qv,
        grad_w_out,
        small[2],
        small[0],
        small[1],
        grad_w_fc,
        grad_b_fc,
        grad_w_proj,
        small[3],
    )


def solution(mesh):
    placed = (
        P("dp", None),
        P("dp", None),
        P(),
        P(),
        P(),
        P(None, None, "tensor"),
        P(None, "tensor"),
        P("tensor", None),
        P(),
        P(),
        P(),
        P(None, "tensor"),
        P("tensor"),
        P("tensor", None),
        P(),
    )
    return jax.shard_map(
        per_device,
        mesh=mesh,
        in_specs=placed,
        out_specs=(
            P("dp", None),
            P("dp", None),
            P(),
            P(),
            P(None, None, "tensor"),
            P(None, "tensor"),
            P("tensor", None),
            P(),
            P(),
            P(),
            P(None, "tensor"),
            P("tensor"),
            P("tensor", None),
            P(),
        ),
        check_vma=False,
    )
```

time: 1550 us -> 468 us (0.30)
  waiting for transfers between devices: 909 us -> 163 us
  matrix products: 297 us -> 3.93 us
  other arithmetic: 148 us -> 31.4 us
  Pallas kernels: 0 us -> 95.8 us
  blocking collectives: 48.8 us -> 0 us
  starting transfers between devices: 66.6 us -> 109 us
    psum x1 -> x0, waiting for transfers between devices: 378 us -> none  [per_device(): lax.psum((grad_ln1_gain, grad_ln1_bias, grad_w_qkv, grad_b_qv, grad_w_out...]
    dot_general x32 -> x1, matrix products: 297 us -> 3.93 us  [dotf(): return lax.dot_general(a, b, dims, preferred_element_type=F32)]
    reduce_scatter x4 -> x1, waiting for transfers between devices: 221 us -> 0.01 us  [per_device(): lax.psum_scatter(grad_feed, 'dp', scatter_dimension=0, tiled=True)]
    ppermute x16 -> x36, waiting for transfers between devices: 264 us -> 96.8 us  [the longest x7 39 us: swap_x(): lax.ppermute(value, 'tensor', [(i, i ^ 2) for i in range(lax.axis_size('t...]
    pallas_call x0 -> x15, Pallas kernels: none -> 95.8 us  [the longest x1 25.6 us: attn_bwd(): pl.pallas_call(functools.partial(bwd_kernel, bq, bk, S), out_shape=[block...]
    all_to_all x0 -> x9, waiting for transfers between devices: none -> 66.2 us  [exchange(): lax.all_to_all(heads, 'dp', 0, 0, tiled=True, axis_index_groups=groups)]
    reduce_sum x17 -> x3, other arithmetic: 54.7 us -> 0.34 us  [the longest x1 0.15 us: per_device(): jnp.sum(q_home.astype(F32), axis=1)]
    convert_element_type x9, other arithmetic: 79 us -> 24.8 us  [the longest x3 7.48 us: add_low(): return (own.astype(F32) + other.astype(F32)).astype(LOW)]
  transfers between devices with their start and end apart: 25 -> 48, of which waited for: 11 -> 27; matrix products, arithmetic and copies ran while one was open for 4% -> 9% of each run, Pallas kernels for 0% -> 15%
where the time goes in v2:
time: 468 us; the launch traced here: 465 us
  waiting for transfers between devices  163 us (35%)
  starting transfers between devices  109 us (23%)
  Pallas kernels  95.8 us (20%)
  local copies, waits for them, and re-layouts  45.9 us (10%)
  other arithmetic  31.4 us (7%)
  between operations  16.2 us (3%)
    all_to_all x9, waiting for transfers between devices, exchange(): lax.all_to_all(heads, 'dp', 0, 0, tiled=True, axis_index_groups=groups)  66.2 us
    ppermute x7, waiting for transfers between devices, swap_x(): lax.ppermute(value, 'tensor', [(i, i ^ 2) for i in range(lax.axis_size('t...  39 us
    all_to_all x9, starting transfers between devices, exchange(): lax.all_to_all(heads, 'dp', 0, 0, tiled=True, axis_index_groups=groups)  36.6 us
    ppermute x10, waiting for transfers between devices, shift_group(): lax.ppermute(value, 'dp', [(i, i // S * S + (i % S + steps) % S) for i in...  35.2 us
    unnamed x123, local copies, waits for them, and re-layouts  34.3 us
    ppermute x3, starting transfers between devices, per_device(): lax.ppermute(small, 'dp', [(i, i ^ step) for i in range(count)])  29.7 us
    ppermute x10, starting transfers between devices, shift_group(): lax.ppermute(value, 'dp', [(i, i // S * S + (i % S + steps) % S) for i in...  26.6 us
    pallas_call x1, Pallas kernels, attn_bwd(): pl.pallas_call(functools.partial(bwd_kernel, bq, bk, S), out_shape=[block...  25.6 us
  transfers between devices with their start and end apart: 48, of which 27 were waited for; matrix products, arithmetic and copies ran while one was open for 9% of the time, Pallas kernels for 15%

profile of v2, /device:TPU:0, one launch (start us, length us, event | category | flops | bytes accessed | tf_op | source)
XLA Modules:
  0.0 465.4 jit_solution(11959127827501991164)
XLA Ops:
  18.8 6.3 %all-to-all-start.1 = ((bf16[4,64,1024]{2,1,0:T(8,128)(2,1)}), bf16[4,64,1024]{2,1,0:T(8,128)(2,1)S(1)}, u32[]{:S(2)}, u32[]{:S(2)}) async-start(bf16[4,64,1024]{2,1,0:T(8,128)(2,1)} %get-tuple-element.82), calls=%async_computation.1 | async-start | bytes 1048576 | tf_op jit(solution)/shard_map/all_to_all | solution.py:649
  26.6 13.0 %all-to-all-done.1.refs_0_ = bf16[4,64,1024]{2,1,0:T(8,128)(2,1)S(1)} async-done(((bf16[4,64,1024]{2,1,0:T(8,128)(2,1)}), bf16[4,64,1024]{2,1,0:T(8,128)(2,1)S(1)}, u32[]{:S(2)}, u32[]{:S(2)}) %all-to-all-start.1) | async-done | bytes 524320 | tf_op jit(solution)/shard_map/all_to_all | solution.py:649
  45.2 11.8 %all-to-all-done.2.refs_2_ = bf16[4,64,1024]{2,1,0:T(8,128)(2,1)S(1)} async-done(((bf16[4,64,1024]{2,1,0:T(8,128)(2,1)}), bf16[4,64,1024]{2,1,0:T(8,128)(2,1)S(1)}, u32[]{:S(2)}, u32[]{:S(2)}) %all-to-all-start.2) | async-done | bytes 524320 | tf_op jit(solution)/shard_map/all_to_all | solution.py:649
  65.5 9.0 %all-to-all-done.q_ref = bf16[4,64,1024]{2,1,0:T(8,128)(2,1)S(1)} async-done(((bf16[4,64,1024]{2,1,0:T(8,128)(2,1)}), bf16[4,64,1024]{2,1,0:T(8,128)(2,1)S(1)}, u32[]{:S(2)}, u32[]{:S(2)}) %all-to-all-start) | async-done | bytes 524320 | tf_op jit(solution)/shard_map/all_to_all | solution.py:649
  74.6 20.3 %attn_fwd.1 = (bf16[4,64,1024]{2,1,0:T(8,128)(2,1)}, f32[4,1,1024]{2,1,0:T(1,128)S(1)}) custom-call(s32[1]{0:T(128)} %bitcast.meta_ref, s32[4]{0:T(128)S(1)} %copy-done.53, bf16[4,64,1024]{2,1,0:T(8,128)(2,1)S(1)} %all-to-all-done.q_ref, bf16[4,64,1024]{2,1,0:T(8,128)(2,1)S(1)} %all-to-all-done.1.refs_0_, ...), custom_call_target="tpu_custom_call" | custom-call | tf_op jit(solution)/shard_map/attn_fwd/pallas_call | solution.py:189
  100.5 11.8 %all-to-all-done.3 = bf16[4,64,1024]{2,1,0:T(8,128)(2,1)S(1)} async-done(((bf16[4,64,1024]{2,1,0:T(8,128)(2,1)}), bf16[4,64,1024]{2,1,0:T(8,128)(2,1)S(1)}, u32[]{:S(2)}, u32[]{:S(2)}) %all-to-all-start.3) | async-done | bytes 524320 | tf_op jit(solution)/shard_map/all_to_all | solution.py:649
  114.1 11.4 %collective-permute-done.6.o2 = bf16[256,1024]{1,0:T(8,128)(2,1)S(1)} collective-permute-done((bf16[256,1024]{1,0:T(8,128)(2,1)S(1)}, bf16[256,1024]{1,0:T(8,128)(2,1)S(1)}, u32[]{:S(2)}, u32[]{:S(2)}) %collective-permute-start.6) | collective-permute-done | bytes 524320 | tf_op jit(solution)/shard_map/ppermute | solution.py:577
  148.8 6.2 %feed_grads.1 = bf16[2048,1024]{1,0:T(8,128)(2,1)S(1)} custom-call(bf16[1024,1024]{1,0:T(8,128)(2,1)S(1)} %get-tuple-element.99.g_ref, bf16[1024,1024]{1,0:T(8,128)(2,1)S(1)} %copy-done, bf16[1024,1024]{1,0:T(8,128)(2,1)S(1)} %get-tuple-element.90.n2_ref, bf16[1024,1024]{1,0:T(8,128)(2,1)S(1)} %get-tuple-element.96.dh_ref), custom_call_target="tpu_custom_call" | custom-call | tf_op jit(solution)/shard_map/feed_grads/pallas_call | solution.py:443
  178.8 17.7 %collective-permute-done.9.crossed_ref = bf16[512,1024]{1,0:T(8,128)(2,1)} collective-permute-done((bf16[512,1024]{1,0:T(8,128)(2,1)}, bf16[512,1024]{1,0:T(8,128)(2,1)}, u32[]{:S(2)}, u32[]{:S(2)}) %collective-permute-start.9) | collective-permute-done | bytes 1048608 | tf_op jit(solution)/shard_map/ppermute | solution.py:577
  211.4 6.9 %collective-permute-start.14 = (bf16[4,32,1024]{2,1,0:T(8,128)(2,1)}, bf16[4,32,1024]{2,1,0:T(8,128)(2,1)}, u32[]{:S(2)}, u32[]{:S(2)}) collective-permute-start(bf16[4,32,1024]{2,1,0:T(8,128)(2,1)} %get-tuple-element.158), channel_id=1, source_target_pairs={{0,4},{4,0},{8,12},{12,8},{16,20},{20,16},{24,28},{28,24},{1,5},{5... | collective-permute-start | bytes 786440 | tf_op jit(solution)/shard_map/ppermute | solution.py:567
  218.3 6.3 %all-to-all-done.4.refs_6_ = bf16[4,64,1024]{2,1,0:T(8,128)(2,1)S(1)} async-done(((bf16[4,64,1024]{2,1,0:T(8,128)(2,1)}), bf16[4,64,1024]{2,1,0:T(8,128)(2,1)S(1)}, u32[]{:S(2)}, u32[]{:S(2)}) %all-to-all-start.4) | async-done | bytes 524320 | tf_op jit(solution)/shard_map/all_to_all | solution.py:649
  224.6 25.6 %attn_bwd.1 = (bf16[4,64,1024]{2,1,0:T(8,128)(2,1)S(1)}, bf16[4,64,1024]{2,1,0:T(8,128)(2,1)S(1)}, bf16[4,64,1024]{2,1,0:T(8,128)(2,1)S(1)}, bf16[4,64,1024]{2,1,0:T(8,128)(2,1)S(1)}, bf16[4,64,1024]{2,1,0:T(8,128)(2,1)}) custom-call(s32[1]{0:T(128)} %bitcast.meta_ref, s32[4]{0:T(128)S(1)} %copy-done.53, bf16[4,64,1024]{2,1,0:T(8,128)(2,1)S(1)} %copy-done.15, ...), custom_call_target="tpu_custom_call" | custom-call | tf_op jit(solution)/shard_map/attn_bwd/pallas_call | solution.py:211
  253.4 6.4 %collective-permute-done.12 = bf16[512,1024]{1,0:T(8,128)(2,1)} collective-permute-done((bf16[512,1024]{1,0:T(8,128)(2,1)}, bf16[512,1024]{1,0:T(8,128)(2,1)}, u32[]{:S(2)}, u32[]{:S(2)}) %collective-permute-start.12) | collective-permute-done | bytes 1048608 | tf_op jit(solution)/shard_map/ppermute | solution.py:577
  263.4 6.9 %collective-permute-start.15 = (bf16[4,64,1024]{2,1,0:T(8,128)(2,1)}, bf16[4,64,1024]{2,1,0:T(8,128)(2,1)S(1)}, u32[]{:S(2)}, u32[]{:S(2)}) collective-permute-start(bf16[4,64,1024]{2,1,0:T(8,128)(2,1)} %copy-done.55), channel_id=1, source_target_pairs={{0,4},{4,0},{8,12},{12,8},{16,20},{20,16},{24,28},{28,24},{1,5},{5... | collective-permute-start | bytes 1572872 | tf_op jit(solution)/shard_map/ppermute | solution.py:567
  270.3 12.0 %collective-permute-done.15 = bf16[4,64,1024]{2,1,0:T(8,128)(2,1)S(1)} collective-permute-done((bf16[4,64,1024]{2,1,0:T(8,128)(2,1)}, bf16[4,64,1024]{2,1,0:T(8,128)(2,1)S(1)}, u32[]{:S(2)}, u32[]{:S(2)}) %collective-permute-start.15) | collective-permute-done | bytes 524320 | tf_op jit(solution)/shard_map/ppermute | solution.py:567
  294.1 7.7 %collective-permute-done.16 = bf16[4,64,1024]{2,1,0:T(8,128)(2,1)} collective-permute-done((bf16[4,64,1024]{2,1,0:T(8,128)(2,1)}, bf16[4,64,1024]{2,1,0:T(8,128)(2,1)}, u32[]{:S(2)}, u32[]{:S(2)}) %collective-permute-start.16) | collective-permute-done | bytes 524320 | tf_op jit(solution)/shard_map/ppermute | solution.py:567
  311.5 7.6 %grad_heads.1 = f32[192,1024]{1,0:T(8,128)S(1)} custom-call(s32[8]{0:T(128)S(1)} %stack.118.spot_ref, bf16[4,64,1024]{2,1,0:T(8,128)(2,1)S(1)} %copy-done.32, bf16[4,64,1024]{2,1,0:T(8,128)(2,1)} %add_convert_fusion.5.dk_ref, bf16[4,64,1024]{2,1,0:T(8,128)(2,1)} %add_convert_fusion.4.dv_ref, bf16[1024,1024]{1,0:T(8,128)(2,1)S(1)} %copy-done.20, ...), custom_call_target="tpu_custom_call" | custom-call | tf_op jit(solution)/shard_map/grad_heads/pallas_call | solution.py:494
  345.2 10.7 %all-to-all-done.8 = bf16[4,32,1024]{2,1,0:T(8,128)(2,1)S(1)} async-done(((bf16[4,32,1024]{2,1,0:T(8,128)(2,1)}), bf16[4,32,1024]{2,1,0:T(8,128)(2,1)S(1)}, u32[]{:S(2)}, u32[]{:S(2)}) %all-to-all-start.8) | async-done | bytes 262176 | tf_op jit(solution)/shard_map/all_to_all | solution.py:649
  372.2 9.1 %collective-permute-done.24.refs_4_ = bf16[256,512]{1,0:T(8,128)(2,1)S(1)} collective-permute-done((bf16[256,512]{1,0:T(8,128)(2,1)S(1)}, bf16[256,512]{1,0:T(8,128)(2,1)S(1)}, u32[]{:S(2)}, u32[]{:S(2)}) %collective-permute-start.24) | collective-permute-done | bytes 262176 | tf_op jit(solution)/shard_map/ppermute | solution.py:562
  384.8 8.5 %collective-permute-start.29 = (f32[12,1024]{1,0:T(8,128)S(1)}, f32[12,1024]{1,0:T(8,128)S(1)}, u32[]{:S(2)}, u32[]{:S(2)}) collective-permute-start(f32[12,1024]{1,0:T(8,128)S(1)} %fusion.3), channel_id=1, source_target_pairs={{0,4},{4,0},{8,12},{12,8},{16,20},{20,16},{24,28},{28,24},{1,5},{5... | collective-permute-start | bytes 147464 | tf_op jit(solution)/shard_map/ppermute | solution.py:777
  395.7 20.1 %collective-permute-start.30 = (f32[12,1024]{1,0:T(8,128)S(1)}, f32[12,1024]{1,0:T(8,128)S(1)}, u32[]{:S(2)}, u32[]{:S(2)}) collective-permute-start(f32[12,1024]{1,0:T(8,128)S(1)} %add.229), channel_id=1, source_target_pairs={{0,8},{4,12},{8,0},{12,4},{16,24},{20,28},{24,16},{28,20},{1,9},{5... | collective-permute-start | bytes 147464 | tf_op jit(solution)/shard_map/ppermute | solution.py:777
  428.6 5.6 %collective-permute-done.33.refs_3_ = bf16[256,512]{1,0:T(8,128)(2,1)S(1)} collective-permute-done((bf16[256,512]{1,0:T(8,128)(2,1)}, bf16[256,512]{1,0:T(8,128)(2,1)S(1)}, u32[]{:S(2)}, u32[]{:S(2)}) %collective-permute-start.33) | collective-permute-done | bytes 262176 | tf_op jit(solution)/shard_map/ppermute | solution.py:567
  434.2 5.6 %collective-permute-done.34.refs_5_ = bf16[256,512]{1,0:T(8,128)(2,1)S(1)} collective-permute-done((bf16[256,512]{1,0:T(8,128)(2,1)}, bf16[256,512]{1,0:T(8,128)(2,1)S(1)}, u32[]{:S(2)}, u32[]{:S(2)}) %collective-permute-start.34) | collective-permute-done | bytes 262176 | tf_op jit(solution)/shard_map/ppermute | solution.py:567
  451.3 6.7 %slice_convert_fusion = (f32[1024,1024]{1,0:T(8,128)}, f32[1024,1024]{1,0:T(8,128)}) fusion(bf16[2048,1024]{1,0:T(8,128)(2,1)} %all-gather.4.cloned.1.call-done), kind=kLoop, calls=%fused_computation | loop fusion | flops 2097152 | bytes 12582912 | tf_op jit(solution)/shard_map/convert_element_type | solution.py:757
  (262 shorter events, 195.9 us)
Async XLA Ops:
  18.8 20.8 %all-to-all-start.1 = ((bf16[4,64,1024]{2,1,0:T(8,128)(2,1)}), bf16[4,64,1024]{2,1,0:T(8,128)(2,1)S(1)}, u32[]{:S(2)}, u32[]{:S(2)}) async-start(bf16[4,64,1024]{2,1,0:T(8,128)(2,1)} %get-tuple-element.82), calls=%async_computation.1 | async-start | bytes 1048576 | tf_op jit(solution)/shard_map/all_to_all | solution.py:649
  25.2 18.0 %collective-permute-start.1 = (bf16[256,1024]{1,0:T(8,128)(2,1)S(1)}, bf16[256,1024]{1,0:T(8,128)(2,1)}, u32[]{:S(2)}, u32[]{:S(2)}) collective-permute-start(bf16[256,1024]{1,0:T(8,128)(2,1)S(1)} %copy-done.29), channel_id=1, source_target_pairs={{0,2},{1,3},{2,0},{3,1},{4,6},{5,7},{6,4},{7,5},{8,10},{9,11},{10,... | collective-permute-start | bytes 1572872 | tf_op jit(solution)/shard_map/ppermute | solution.py:577
  44.7 17.5 %collective-permute-start.2 = (bf16[256,1024]{1,0:T(8,128)(2,1)}, bf16[256,1024]{1,0:T(8,128)(2,1)}, u32[]{:S(2)}, u32[]{:S(2)}) collective-permute-start(bf16[256,1024]{1,0:T(8,128)(2,1)} %collective-permute-done.1), channel_id=1, source_target_pairs={{0,1},{1,0},{2,3},{3,2},{4,5},{5,4},{6,7},{7,6},{8,9},{9,8},{10,11... | collective-permute-start | bytes 1572872 | tf_op jit(solution)/shard_map/ppermute | solution.py:573
  98.6 73.7 %all-gather.6.cloned.1.call-start = ((), (), s32[]{:S(2)}) async-start(), calls=%async_computation.12 | async-start | bytes 2621440 | tf_op jit(solution)/shard_map/all_gather | solution.py:670
  112.3 209.9 %reduce-scatter.2.cloned.1.call-start = ((), (), s32[]{:S(2)}) async-start(), calls=%async_computation.10 | async-start | bytes 4718592 | tf_op jit(solution)/shard_map/reduce_scatter | solution.py:686
  170.7 25.8 %collective-permute-start.9 = (bf16[512,1024]{1,0:T(8,128)(2,1)}, bf16[512,1024]{1,0:T(8,128)(2,1)}, u32[]{:S(2)}, u32[]{:S(2)}) collective-permute-start(bf16[512,1024]{1,0:T(8,128)(2,1)} %add_convert_fusion.3.own_ref), channel_id=1, source_target_pairs={{0,2},{1,3},{2,0},{3,1},{4,6},{5,7},{6,4},{7,5},{8,10},{9,11},{10,... | collective-permute-start | bytes 3145736 | tf_op jit(solution)/shard_map/ppermute | solution.py:577
  200.3 59.6 %collective-permute-start.13 = (bf16[3,256,1024]{2,1,0:T(8,128)(2,1)}, bf16[3,256,1024]{2,1,0:T(8,128)(2,1)}, u32[]{:S(2)}, u32[]{:S(2)}) collective-permute-start(bf16[3,256,1024]{2,1,0:T(8,128)(2,1)} %pad_maximum_fusion.2.refs_0_), channel_id=1, source_target_pairs={{0,2},{1,3},{2,0},{3,1},{4,6},{5,7},{6,4},{7,5},{8,10},{9,11},{10,... | collective-permute-start | bytes 4718600 | tf_op jit(solution)/shard_map/ppermute | solution.py:577
  201.8 58.0 %collective-permute-start.12 = (bf16[512,1024]{1,0:T(8,128)(2,1)}, bf16[512,1024]{1,0:T(8,128)(2,1)}, u32[]{:S(2)}, u32[]{:S(2)}) collective-permute-start(bf16[512,1024]{1,0:T(8,128)(2,1)} %add_convert_fusion.2), channel_id=1, source_target_pairs={{0,2},{1,3},{2,0},{3,1},{4,6},{5,7},{6,4},{7,5},{8,10},{9,11},{10,... | collective-permute-start | bytes 3145736 | tf_op jit(solution)/shard_map/ppermute | solution.py:577
  205.8 18.7 %all-to-all-start.4 = ((bf16[4,64,1024]{2,1,0:T(8,128)(2,1)}), bf16[4,64,1024]{2,1,0:T(8,128)(2,1)S(1)}, u32[]{:S(2)}, u32[]{:S(2)}) async-start(bf16[4,64,1024]{2,1,0:T(8,128)(2,1)} %bitcast.78), calls=%async_computation.4 | async-start | bytes 1048576 | tf_op jit(solution)/shard_map/all_to_all | solution.py:649
  211.4 48.4 %collective-permute-start.14 = (bf16[4,32,1024]{2,1,0:T(8,128)(2,1)}, bf16[4,32,1024]{2,1,0:T(8,128)(2,1)}, u32[]{:S(2)}, u32[]{:S(2)}) collective-permute-start(bf16[4,32,1024]{2,1,0:T(8,128)(2,1)} %get-tuple-element.158), channel_id=1, source_target_pairs={{0,4},{4,0},{8,12},{12,8},{16,20},{20,16},{24,28},{28,24},{1,5},{5... | collective-permute-start | bytes 786440 | tf_op jit(solution)/shard_map/ppermute | solution.py:567
  259.9 22.4 %all-to-all-start.5 = ((bf16[4,64,1024]{2,1,0:T(8,128)(2,1)}), bf16[4,64,1024]{2,1,0:T(8,128)(2,1)S(1)}, u32[]{:S(2)}, u32[]{:S(2)}) async-start(bf16[4,64,1024]{2,1,0:T(8,128)(2,1)} %copy-done.31), calls=%async_computation.5 | async-start | bytes 1048576 | tf_op jit(solution)/shard_map/all_to_all | solution.py:649
  263.4 18.9 %collective-permute-start.15 = (bf16[4,64,1024]{2,1,0:T(8,128)(2,1)}, bf16[4,64,1024]{2,1,0:T(8,128)(2,1)S(1)}, u32[]{:S(2)}, u32[]{:S(2)}) collective-permute-start(bf16[4,64,1024]{2,1,0:T(8,128)(2,1)} %copy-done.55), channel_id=1, source_target_pairs={{0,4},{4,0},{8,12},{12,8},{16,20},{20,16},{24,28},{28,24},{1,5},{5... | collective-permute-start | bytes 1572872 | tf_op jit(solution)/shard_map/ppermute | solution.py:567
  284.3 18.1 %all-to-all-start.6 = ((bf16[4,64,1024]{2,1,0:T(8,128)(2,1)}), bf16[4,64,1024]{2,1,0:T(8,128)(2,1)S(1)}, u32[]{:S(2)}, u32[]{:S(2)}) async-start(bf16[4,64,1024]{2,1,0:T(8,128)(2,1)} %add_convert_fusion.5.dk_ref), calls=%async_computation.6 | async-start | bytes 1048576 | tf_op jit(solution)/shard_map/all_to_all | solution.py:649
  290.8 19.8 %collective-permute-start.17 = (bf16[3,256,1024]{2,1,0:T(8,128)(2,1)}, bf16[3,256,1024]{2,1,0:T(8,128)(2,1)}, u32[]{:S(2)}, u32[]{:S(2)}) collective-permute-start(bf16[3,256,1024]{2,1,0:T(8,128)(2,1)} %pad_maximum_fusion.2.refs_0_), channel_id=1, source_target_pairs={{0,1},{1,0},{2,3},{3,2},{4,5},{5,4},{6,7},{7,6},{8,9},{9,8},{10,11... | collective-permute-start | bytes 4718600 | tf_op jit(solution)/shard_map/ppermute | solution.py:573
  290.8 19.8 %collective-permute-start.18 = (bf16[3,256,1024]{2,1,0:T(8,128)(2,1)}, bf16[3,256,1024]{2,1,0:T(8,128)(2,1)}, u32[]{:S(2)}, u32[]{:S(2)}) collective-permute-start(bf16[3,256,1024]{2,1,0:T(8,128)(2,1)} %collective-permute-done.13.refs_1_), channel_id=1, source_target_pairs={{0,1},{1,0},{2,3},{3,2},{4,5},{5,4},{6,7},{7,6},{8,9},{9,8},{10,11... | collective-permute-start | bytes 4718600 | tf_op jit(solution)/shard_map/ppermute | solution.py:573
  309.0 142.3 %all-gather.4.cloned.1.call-start = ((), (), s32[]{:S(2)}) async-start(), calls=%async_computation.11 | async-start | bytes 4718592 | tf_op jit(solution)/shard_map/all_gather | solution.py:740
  336.8 19.1 %all-to-all-start.8 = ((bf16[4,32,1024]{2,1,0:T(8,128)(2,1)}), bf16[4,32,1024]{2,1,0:T(8,128)(2,1)S(1)}, u32[]{:S(2)}, u32[]{:S(2)}) async-start(bf16[4,32,1024]{2,1,0:T(8,128)(2,1)} %add_convert_fusion.6), calls=%async_computation.9 | async-start | bytes 524288 | tf_op jit(solution)/shard_map/all_to_all | solution.py:649
  340.5 25.7 %collective-permute-start.21 = (bf16[512,1024]{1,0:T(8,128)(2,1)S(1)}, bf16[512,1024]{1,0:T(8,128)(2,1)}, u32[]{:S(2)}, u32[]{:S(2)}) collective-permute-start(bf16[512,1024]{1,0:T(8,128)(2,1)S(1)} %add_convert_fusion.own_ref), channel_id=1, source_target_pairs={{0,2},{1,3},{2,0},{3,1},{4,6},{5,7},{6,4},{7,5},{8,10},{9,11},{10,... | collective-permute-start | bytes 3145736 | tf_op jit(solution)/shard_map/ppermute | solution.py:577
  357.0 24.3 %collective-permute-start.24 = (bf16[256,512]{1,0:T(8,128)(2,1)S(1)}, bf16[256,512]{1,0:T(8,128)(2,1)S(1)}, u32[]{:S(2)}, u32[]{:S(2)}) collective-permute-start(bf16[256,512]{1,0:T(8,128)(2,1)S(1)} %pad_maximum_fusion.3.refs_0_), channel_id=1, source_target_pairs={{0,16},{4,20},{8,24},{12,28},{16,0},{20,4},{24,8},{28,12},{1,17},{... | collective-permute-start | bytes 786440 | tf_op jit(solution)/shard_map/ppermute | solution.py:562
  358.4 22.9 %collective-permute-start.25 = (bf16[256,512]{1,0:T(8,128)(2,1)S(1)}, bf16[256,512]{1,0:T(8,128)(2,1)S(1)}, u32[]{:S(2)}, u32[]{:S(2)}) collective-permute-start(bf16[256,512]{1,0:T(8,128)(2,1)S(1)} %pad_maximum_fusion.3.refs_0_), channel_id=1, source_target_pairs={{0,24},{4,28},{8,0},{12,4},{16,8},{20,12},{24,16},{28,20},{1,25},{... | collective-permute-start | bytes 786440 | tf_op jit(solution)/shard_map/ppermute | solution.py:562
  382.0 66.6 %collective-permute-start.26 = (bf16[512,1024]{1,0:T(8,128)(2,1)}, bf16[512,1024]{1,0:T(8,128)(2,1)S(1)}, u32[]{:S(2)}, u32[]{:S(2)}) collective-permute-start(bf16[512,1024]{1,0:T(8,128)(2,1)} %get-tuple-element.137.own_ref), channel_id=1, source_target_pairs={{0,1},{1,0},{2,3},{3,2},{4,5},{5,4},{6,7},{7,6},{8,9},{9,8},{10,11... | collective-permute-start | bytes 3145736 | tf_op jit(solution)/shard_map/ppermute | solution.py:573
  395.7 22.3 %collective-permute-start.30 = (f32[12,1024]{1,0:T(8,128)S(1)}, f32[12,1024]{1,0:T(8,128)S(1)}, u32[]{:S(2)}, u32[]{:S(2)}) collective-permute-start(f32[12,1024]{1,0:T(8,128)S(1)} %add.229), channel_id=1, source_target_pairs={{0,8},{4,12},{8,0},{12,4},{16,24},{20,28},{24,16},{28,20},{1,9},{5... | collective-permute-start | bytes 147464 | tf_op jit(solution)/shard_map/ppermute | solution.py:777
  421.3 18.4 %collective-permute-start.34 = (bf16[256,512]{1,0:T(8,128)(2,1)}, bf16[256,512]{1,0:T(8,128)(2,1)S(1)}, u32[]{:S(2)}, u32[]{:S(2)}) collective-permute-start(bf16[256,512]{1,0:T(8,128)(2,1)} %copy-done.41), channel_id=1, source_target_pairs={{0,4},{4,0},{8,12},{12,8},{16,20},{20,16},{24,28},{28,24},{1,5},{5... | collective-permute-start | bytes 786440 | tf_op jit(solution)/shard_map/ppermute | solution.py:567
  423.3 19.3 %collective-permute-start.35 = (bf16[256,512]{1,0:T(8,128)(2,1)}, bf16[256,512]{1,0:T(8,128)(2,1)S(1)}, u32[]{:S(2)}, u32[]{:S(2)}) collective-permute-start(bf16[256,512]{1,0:T(8,128)(2,1)} %copy-done.43), channel_id=1, source_target_pairs={{0,4},{4,0},{8,12},{12,8},{16,20},{20,16},{24,28},{28,24},{1,5},{5... | collective-permute-start | bytes 786440 | tf_op jit(solution)/shard_map/ppermute | solution.py:567
  (84 other events, 834.0 us)
Sparse Core Ops, SparseCore 0:
  112.4 50.3 all-gather.5
Sparse Core Ops, SparseCore 1:
  158.4 91.5 reduce-scatter.1
  322.3 91.5 all-gather.3

commit v3 on v2

--- a/solution.py
+++ b/solution.py
@@ -77,19 +77,20 @@
         lax.fori_loop(0, J, one, 0)
 
 
-def fwd_kernel(bq, bk, S, meta_ref, seq_ref, q_ref, *refs):
+def fwd_kernel(bq, bk, S, part, meta_ref, seq_ref, q_ref, *refs):
     k_refs, v_refs = refs[:S], refs[S : 2 * S]
     o_ref, lse_ref, kt_ref, vf_ref = refs[2 * S :]
     J, _, T = q_ref.shape
     ends = read_ends(seq_ref)
     fill(k_refs, kt_ref, True)
     fill(v_refs, vf_ref, False)
-    per = T // bq
+    per = T // 2 // bq
     rows = lax.broadcasted_iota(jnp.int32, (bk, bq), 0)
 
     def q_tile(i, _):
         s = i // per
-        qo = pl.multiple_of(lax.rem(i, per) * bq, bq)
+        to = pl.multiple_of(lax.rem(i, per) * bq, bq)
+        qo = to + part * (T // 2)
         q0 = (s * S + meta_ref[0]) * T + qo
         q = q_ref[s, :, pl.ds(qo, bq)]
         place = q0 + lax.broadcasted_iota(jnp.int32, (1, bq), 1)
@@ -117,8 +118,8 @@
         c = lax.fori_loop(t2, t3, functools.partial(tile, True), c)
         c = lax.fori_loop(t0, t1, functools.partial(tile, True), c)
         m, l, acc = lax.fori_loop(t1, t2, functools.partial(tile, False), c)
-        o_ref[s, :, pl.ds(qo, bq)] = (acc / l).astype(LOW)
-        lse_ref[s, :, pl.ds(qo, bq)] = m + jnp.log(l)
+        o_ref[s, :, pl.ds(to, bq)] = (acc / l).astype(LOW)
+        lse_ref[s, :, pl.ds(to, bq)] = m + jnp.log(l)
         return 0
 
     lax.fori_loop(0, J * per, q_tile, 0)
@@ -183,14 +184,14 @@
     return pltpu.CompilerParams(vmem_limit_bytes=(58 if keys > 8192 else 40) * MIB)
 
 
-def attn_fwd(meta, seq, q, ks, vs, bq=512, bk=512):
+def attn_fwd(meta, seq, q, ks, vs, part, bq=512, bk=512):
     J, _, T = q.shape
     S = len(ks)
     return pl.pallas_call(
-        functools.partial(fwd_kernel, bq, bk, S),
+        functools.partial(fwd_kernel, bq, bk, S, part),
         out_shape=(
-            jax.ShapeDtypeStruct((J, HEAD_DIM, T), LOW),
-            jax.ShapeDtypeStruct((J, 1, T), F32),
+            jax.ShapeDtypeStruct((J, HEAD_DIM, T // 2), LOW),
+            jax.ShapeDtypeStruct((J, 1, T // 2), F32),
         ),
         in_specs=[M, M] + [V] * (1 + 2 * S),
         out_specs=(V, V),
@@ -262,14 +263,17 @@
     )(x, gain[None], bias[None], w, b)
 
 
-def out_kernel(pos_ref, o0, o1, o2, o3, w_ref, x_ref, b_ref, gain_ref, bias_ref, x1_ref, n2_ref, held):
+def out_kernel(pos_ref, *refs):
+    pieces = refs[:8]
+    w_ref, x_ref, b_ref, gain_ref, bias_ref, x1_ref, n2_ref, held = refs[8:]
     i = pl.program_id(0)
     rows = x1_ref.shape[0]
 
     @pl.when(i == 0)
     def _():
-        for r, piece in enumerate((o0, o1, o2, o3)):
-            held[pos_ref[r]] = piece[...]
+        for r, piece in enumerate(pieces):
+            half = piece.shape[1]
+            held[pos_ref[r % 4], :, r // 4 * half : (r // 4 + 1) * half] = piece[...]
 
     lanes = pl.ds(pl.multiple_of(i * rows, rows), rows)
     o = held[:, :, lanes].reshape(-1, rows)
@@ -287,7 +291,7 @@
         out_kernel,
         grid=(T // rows,),
         out_shape=(jax.ShapeDtypeStruct((T, D), F32), jax.ShapeDtypeStruct((T, D), LOW)),
-        in_specs=[M, V, V, V, V, V, row_spec, V, V, V],
+        in_specs=[M] + [V] * 9 + [row_spec, V, V, V],
         out_specs=(row_spec, row_spec),
         scratch_shapes=[pltpu.VMEM((4, local, T), LOW)],
         compiler_params=pltpu.CompilerParams(vmem_limit_bytes=32 * MIB),
@@ -452,28 +456,29 @@
     )(g, dm, n2, dh)
 
 
-def do_kernel(core_ref, own_ref, other_ref, w_ref, o_ref, do_ref, grad_ref):
+def do_kernel(core_ref, own_ref, other_ref, w_ref, one_ref, two_ref, do_ref, grad_ref):
     half = own_ref.shape[0]
     grad = jnp.zeros(grad_ref.shape, F32)
     for ref, at in ((own_ref, core_ref[0]), (other_ref, 1 - core_ref[0])):
         lanes = pl.ds(pl.multiple_of(at * half, half), half)
         do_ref[:, lanes] = dotf(w_ref[...], ref[...], NT).astype(LOW)
-        grad += dotf(o_ref[:, lanes], ref[...], NN)
+        o = jnp.where(at == 0, one_ref[...], two_ref[...])
+        grad += dotf(o, ref[...], NN)
     grad_ref[...] = grad.astype(LOW)
 
 
-def do_stage(core, own, other, w_out, o_home):
+def do_stage(core, own, other, w_out, home_one, home_two):
     local, D = w_out.shape
-    T = o_home.shape[1]
+    T = 2 * home_one.shape[1]
     return pl.pallas_call(
         do_kernel,
         out_shape=(jax.ShapeDtypeStruct((local, T), LOW), jax.ShapeDtypeStruct((local, D), LOW)),
-        in_specs=[M, V, V, V, V],
+        in_specs=[M, V, V, V, V, V],
         out_specs=(V, V),
         compiler_params=pltpu.CompilerParams(vmem_limit_bytes=24 * MIB),
         cost_estimate=cost(4 * T * D * local, 5 * MIB),
         name="heads_grad",
-    )(core, own, other, w_out, o_home)
+    )(core, own, other, w_out, home_one, home_two)
 
 
 def grad_kernel(share, spot_ref, dq_ref, dk_ref, dv_ref, own_ref, *refs):
@@ -511,7 +516,7 @@
         jj, gg = spot_ref[2 * i], spot_ref[2 * i + 1]
         held[jj, :, pl.ds(pl.multiple_of(gg * wide, wide), wide)] = part[:depth]
         rest = part[depth:].astype(F32)
-        rows = pl.ds(pl.multiple_of((gg * J + jj) * few, few), few)
+        rows = pl.ds(pl.multiple_of((jj * S + gg) * few, few), few)
         for e in range(S):
             out_ref[rows, e * wide : (e + 1) * wide] = rest[e * few : (e + 1) * few]
     for k in range(3):
@@ -538,6 +543,75 @@
     )(spots, *parts)
 
 
+def add_kernel(own_ref, other_ref, out_ref):
+    out_ref[...] = (own_ref[...].astype(F32) + other_ref[...].astype(F32)).astype(LOW)
+
+
+def add_low(own, other):
+    return pl.pallas_call(
+        add_kernel,
+        out_shape=jax.ShapeDtypeStruct(own.shape, LOW),
+        in_specs=[V, V],
+        out_specs=V,
+        compiler_params=pltpu.CompilerParams(vmem_limit_bytes=16 * MIB),
+        cost_estimate=cost(0, 6 * own.size),
+        name="add_low",
+    )(own, other)
+
+
+def feed_out_kernel(core_ref, g_ref, w_ref, kept_ref, sent_ref):
+    half = kept_ref.shape[0]
+    for out, at in ((sent_ref, 1 - core_ref[0]), (kept_ref, core_ref[0])):
+        rows = pl.ds(pl.multiple_of(at * half, half), half)
+        out[...] = dotf(g_ref[rows, :], w_ref[...], NN).astype(LOW)
+
+
+def feed_out(core, g, w):
+    T, F = g.shape
+    D = w.shape[1]
+    part = jax.ShapeDtypeStruct((T // 2, D), LOW)
+    return pl.pallas_call(
+        feed_out_kernel,
+        out_shape=(part, part),
+        in_specs=[M, V, V],
+        out_specs=(V, V),
+        compiler_params=pltpu.CompilerParams(vmem_limit_bytes=24 * MIB),
+        cost_estimate=cost(2 * T * F * D, 6 * MIB),
+        name="feed_out",
+    )(core, g, w)
+
+
+def widen_kernel(low_ref, first_ref, second_ref):
+    steps = pl.num_programs(0) // 2
+
+    @pl.when(pl.program_id(0) < steps)
+    def _():
+        first_ref[...] = low_ref[...].astype(F32)
+
+    @pl.when(pl.program_id(0) >= steps)
+    def _():
+        second_ref[...] = low_ref[...].astype(F32)
+
+
+def widen(low, first):
+    rows, D = low.shape
+    steps = 4
+    block = first // steps
+    return pl.pallas_call(
+        widen_kernel,
+        grid=(2 * steps,),
+        out_shape=(jax.ShapeDtypeStruct((first, D), F32), jax.ShapeDtypeStruct((rows - first, D), F32)),
+        in_specs=[pl.BlockSpec((block, D), lambda i: (i, 0))],
+        out_specs=(
+            pl.BlockSpec((block, D), lambda i: (jnp.minimum(i, steps - 1), 0)),
+            pl.BlockSpec((block, D), lambda i: (jnp.maximum(i - steps, 0), 0)),
+        ),
+        compiler_params=pltpu.CompilerParams(vmem_limit_bytes=16 * MIB),
+        cost_estimate=cost(0, 12 * MIB),
+        name="widen",
+    )(low)
+
+
 def pair_kernel(core_ref, own_ref, other_ref, out_ref):
     half = own_ref.shape[0]
     for ref, at in ((own_ref, core_ref[0]), (other_ref, 1 - core_ref[0])):
@@ -608,10 +682,6 @@
         for e in range(1, S):
             found.append(((j - s) % J, (g - e) % S, shift_group(part, e, S)))
     return found
-
-
-def add_low(own, other):
-    return (own.astype(F32) + other.astype(F32)).astype(LOW)
 
 
 def per_device(
@@ -662,15 +732,22 @@
     w_out_all = jnp.concatenate([pick(pieces, tensor ^ r) for r in range(4)], 0)
 
     q_all = gate(q_all, w_out_all)
-    o_all, lse = attn_fwd(meta, seq_lengths, q_all, ks, vs)
+    o_one, lse_one = attn_fwd(meta, seq_lengths, q_all, ks, vs, 0)
+    o_two, lse_two = attn_fwd(meta, seq_lengths, gate(q_all, o_one), ks, vs, 1)
+    home_one, o_two = tied(exchange(o_one), o_two)
+    home_one = home_one.reshape(local, half)
+    home_two, across = tied(exchange(o_two), swap_x(home_one))
+    home_two = home_two.reshape(local, half)
 
     own_quarter = rows_at(first_low, core * half + side * share, share)
-    o_home = exchange(o_all).reshape(local, T)
-    own_quarter = gate(own_quarter, o_home)
+    own_quarter = rows_at(first_low, core * half + side * share, share)
+    own_quarter = gate(own_quarter, home_two)
     norm_own = lax.all_gather(own_quarter, "dp", axis_index_groups=groups)
 
-    across = swap_x(o_home)
-    o_pieces = (o_home, swap_core(o_home), across, swap_core(across))
+    def gather_tensor(value, across):
+        return value, swap_core(value), across, swap_core(across)
+
+    o_pieces = gather_tensor(home_one, across) + gather_tensor(home_two, swap_x(home_two))
     middle, second_low = out_stage(order, o_pieces, w_out_all, block_input, b_out, ln2_gain, ln2_bias)
     active_low, hidden_grad, sent, bias_one = mlp_stage(
         1 - core_at, second_low, output_grad, w_fc, w_proj, b_fc
@@ -684,33 +761,23 @@
     crossed = swap_x(second_half)
     grad_feed = feed_grads(active_low, output_grad, second_low, hidden_grad)
     feed_part = lax.psum_scatter(grad_feed, "dp", scatter_dimension=0, tiled=True)
-    feed_made = dotf(gate(active_low, second_half), w_proj, NN).astype(LOW)
-    feed_own = add_low(
-        rows_at(feed_made, core * half, half),
-        swap_core(rows_at(feed_made, (1 - core) * half, half)),
-    )
+    feed_kept, feed_sent = feed_out(core_at, active_low, w_proj)
     rolled = jnp.stack([pick(norm_own, (j + s) % J) for s in range(1, J)])
-    crossed = gate(crossed, grad_feed, rolled, feed_own)
+    crossed = gate(crossed, grad_feed, rolled, feed_kept)
     middle_grad, branch_half, sums_two = norm_back(
         core_at, second_half, crossed, middle, output_grad, ln2_gain
     )
-    heads_grad, grad_w_out = do_stage(core_at, branch_half, swap_core(branch_half), w_out, o_home)
+    heads_grad, grad_w_out = do_stage(core_at, branch_half, swap_core(branch_half), w_out, home_one, home_two)
     do_all = exchange(heads_grad.reshape(J, HEAD_DIM, T))
-    out_cut = grad_w_out.reshape(S, J, local // count, D)
-    out_moved = [shift_group(pick(out_cut, (g + e) % S), e, S) for e in range(1, S)]
+    out_parts = lax.all_to_all(grad_w_out.reshape(count, local // count, D), "dp", 0, 0, tiled=True)
 
     norm_across = swap_x(gate(rolled, branch_half))
-    feed_across = swap_x(gate(feed_own, branch_half))
-
+
+    o_all = jnp.concatenate([o_one, o_two], 2)
+    lse = jnp.concatenate([lse_one, lse_two], 2)
     dq, dks, dvs = attn_bwd(meta, seq_lengths, q_all, ks, vs, o_all, lse, do_all)
-    dq, dks, dvs, feed_across, norm_across, out_moved = tied(
-        dq, dks, dvs, feed_across, norm_across, out_moved
-    )
-
-    feed_sum = feed_own.astype(F32) + feed_across.astype(F32)
-    middle_half = rows_at(middle, core * half, half)
-    output_half = (middle_half + (feed_sum + b_proj)).astype(LOW)
-    block_output = lay_pair(core_at, output_half, swap_core(output_half))
+    dq, dks, dvs, norm_across, out_parts = tied(dq, dks, dvs, norm_across, out_parts)
+
     norm_parts = [rolled, norm_across, swap_core(rolled), swap_core(norm_across)]
 
     def regroup(parts):
@@ -718,14 +785,16 @@
 
     def total(own, moved):
         for part in moved:
-            own = own.astype(F32) + part.astype(F32)
-        return own.astype(LOW)
+            own = add_low(own, part)
+        return own
 
     q_home, dk_moved = tied(exchange(dq), regroup(dks))
     dk = total(dks[0], dk_moved)
     k_home, dv_moved = tied(exchange(gate(dk, q_home)), regroup(dvs))
     dv = total(dvs[0], dv_moved)
     v_home = exchange(gate(dv, k_home))
+    feed_own = add_low(feed_kept, swap_core(gate(feed_sent, q_home)))
+    feed_across = swap_x(feed_own)
     q_home, k_home, v_home = (x.reshape(local, T) for x in (q_home, k_home, v_home))
 
     spots = jnp.stack(
@@ -736,28 +805,27 @@
         + [(j + s) % J for s in range(J)]
     ).astype(jnp.int32)
     head_grad = grad_heads(spots, dq, dk, dv, first_low, norm_parts)
-    v_home, head_grad, feed_part, block_output = tied(v_home, head_grad, feed_part, block_output)
+    v_home, head_grad, feed_across, feed_part = tied(v_home, head_grad, feed_across, feed_part)
     grad_feed = lax.all_gather(feed_part, "dp", axis=0, tiled=True)
     kept, sent = first_stage(core_at, q_home, k_home, v_home, w_qkv)
     first_half = add_low(kept, swap_core(sent))
-    head_grad = gate(head_grad, first_half)
     cut = head_grad.reshape(3 * HEAD_DIM, S, D // S).transpose(1, 0, 2)
     head_grad = sum_group(cut, g, S).astype(LOW)
-    grad_w_out = gate(pick(out_cut, g), first_half)
-    grad_w_out = jnp.sum(exchange(total(grad_w_out, out_moved)).astype(F32), axis=0).astype(LOW)
+    grad_w_out = jnp.sum(out_parts.astype(F32), axis=0).astype(LOW)
     block = jnp.concatenate([head_grad] + jnp.split(grad_w_out, S, axis=1), 0)
     blocks = [shift_dp(block, s * S) for s in range(1, J)]
 
-    first_across = gate(swap_x(first_half), block)
+    first_across = gate(swap_x(first_half), *blocks)
     _, input_half, sums_one = norm_back(
         core_at, first_half, first_across, block_input, middle_grad, ln1_gain
     )
-    input_half, sums_one, blocks = tied(input_half, sums_one, blocks)
     input_grad = lay_pair(core_at, input_half, swap_core(input_half))
-    grad_w_proj = grad_feed[: w_proj.shape[0]].astype(F32)
-    grad_w_fc = grad_feed[w_proj.shape[0] :].astype(F32)
-    found = spread_blocks([block, *blocks], j, g, S)
-    grad_w_qkv, grad_w_out = lay_blocks(found, J, S)
+
+    feed_across = gate(feed_across, input_half)
+    feed_sum = feed_own.astype(F32) + feed_across.astype(F32)
+    middle_half = rows_at(middle, core * half, half)
+    output_half = (middle_half + (feed_sum + b_proj)).astype(LOW)
+    block_output = lay_pair(core_at, output_half, swap_core(output_half))
 
     hidden_width = grad_b_fc.shape[1]
     wide_fc = lax.dynamic_update_slice_in_dim(
@@ -776,6 +844,9 @@
     while step < count:
         small = small + lax.ppermute(small, "dp", [(i, i ^ step) for i in range(count)])
         step *= 2
+    found = spread_blocks([block, *blocks], j, g, S)
+    grad_w_proj, grad_w_fc = widen(grad_feed, w_proj.shape[0])
+    grad_w_qkv, grad_w_out = lay_blocks(found, J, S)
     tail = small.shape[0] - 2
     grad_b_qv = lax.dynamic_slice_in_dim(small[tail:], tensor * local, local, 1)
     grad_b_fc = rows_at(small[6:tail].reshape(-1), tensor * hidden_width, hidden_width)

time: 468 us -> 446 us (0.953)
  other arithmetic: 31.4 us -> 10.1 us
  local copies, waits for them, and re-layouts: 45.9 us -> 59.2 us
  waiting for transfers between devices: 163 us -> 150 us
  Pallas kernels: 95.8 us -> 108 us
  starting transfers between devices: 109 us -> 99.7 us
    convert_element_type x7 -> x0, other arithmetic: 20.4 us -> none  [the longest x3 7.48 us: add_low(): return (own.astype(F32) + other.astype(F32)).astype(LOW)]
    ppermute x3, starting transfers between devices: 29.7 us -> 10.4 us  [per_device(): lax.ppermute(small, 'dp', [(i, i ^ step) for i in range(count)])]
    unnamed x123 -> x151, local copies, waits for them, and re-layouts: 34.3 us -> 49.3 us
    pallas_call x1 -> x9, Pallas kernels: 20.3 us -> 35.1 us  [the longest x2 21.1 us: attn_fwd(): pl.pallas_call(functools.partial(fwd_kernel, bq, bk, S, part), out_shape=...]
    all_to_all x9, waiting for transfers between devices: 66.2 us -> 54.3 us  [exchange(): lax.all_to_all(heads, 'dp', 0, 0, tiled=True, axis_index_groups=groups)]
    all_to_all x0 -> x1, starting transfers between devices: none -> 8.53 us  [per_device(): lax.all_to_all(grad_w_out.reshape(count, local // count, D), 'dp', 0, 0,...]
    ppermute x10 -> x9, starting transfers between devices: 26.6 us -> 20.4 us  [shift_group(): lax.ppermute(value, 'dp', [(i, i // S * S + (i % S + steps) % S) for i in...]
    all_to_all x9, starting transfers between devices: 36.6 us -> 41.5 us  [exchange(): lax.all_to_all(heads, 'dp', 0, 0, tiled=True, axis_index_groups=groups)]
  transfers between devices with their start and end apart: 48 -> 51, of which waited for: 27 -> 22; matrix products, arithmetic and copies ran while one was open for 9% -> 5% of each run, Pallas kernels for 15% -> 20%
where the time goes in v3:
time: 446 us; the launch traced here: 443 us
  waiting for transfers between devices  150 us (34%)
  Pallas kernels  108 us (24%)
  starting transfers between devices  99.7 us (22%)
  local copies, waits for them, and re-layouts  59.2 us (13%)
  between operations  16.2 us (4%)
  other arithmetic  10.1 us (2%)
    all_to_all x9, waiting for transfers between devices, exchange(): lax.all_to_all(heads, 'dp', 0, 0, tiled=True, axis_index_groups=groups)  54.3 us
    unnamed x151, local copies, waits for them, and re-layouts  49.3 us
    all_to_all x9, starting transfers between devices, exchange(): lax.all_to_all(heads, 'dp', 0, 0, tiled=True, axis_index_groups=groups)  41.5 us
    ppermute x9, waiting for transfers between devices, shift_group(): lax.ppermute(value, 'dp', [(i, i // S * S + (i % S + steps) % S) for i in...  39.5 us
    ppermute x8, waiting for transfers between devices, swap_x(): lax.ppermute(value, 'tensor', [(i, i ^ 2) for i in range(lax.axis_size('t...  34.9 us
    pallas_call x1, Pallas kernels, attn_bwd(): pl.pallas_call(functools.partial(bwd_kernel, bq, bk, S), out_shape=[block...  22.7 us
    pallas_call x2, Pallas kernels, attn_fwd(): pl.pallas_call(functools.partial(fwd_kernel, bq, bk, S, part), out_shape=...  21.1 us
    ppermute x9, starting transfers between devices, shift_group(): lax.ppermute(value, 'dp', [(i, i // S * S + (i % S + steps) % S) for i in...  20.4 us
  transfers between devices with their start and end apart: 51, of which 22 were waited for; matrix products, arithmetic and copies ran while one was open for 5% of the time, Pallas kernels for 20%

profile of v3, /device:TPU:0, one launch (start us, length us, event | category | flops | bytes accessed | tf_op | source)
XLA Modules:
  0.0 443.1 jit_solution(8139010835431582473)
XLA Ops:
  18.8 6.3 %all-to-all-start.1 = ((bf16[4,64,1024]{2,1,0:T(8,128)(2,1)}), bf16[4,64,1024]{2,1,0:T(8,128)(2,1)S(1)}, u32[]{:S(2)}, u32[]{:S(2)}) async-start(bf16[4,64,1024]{2,1,0:T(8,128)(2,1)} %get-tuple-element.85), calls=%async_computation.1 | async-start | bytes 1048576 | tf_op jit(solution)/shard_map/all_to_all | solution.py:719
  26.6 13.0 %all-to-all-done.1.refs_0_ = bf16[4,64,1024]{2,1,0:T(8,128)(2,1)S(1)} async-done(((bf16[4,64,1024]{2,1,0:T(8,128)(2,1)}), bf16[4,64,1024]{2,1,0:T(8,128)(2,1)S(1)}, u32[]{:S(2)}, u32[]{:S(2)}) %all-to-all-start.1) | async-done | bytes 524320 | tf_op jit(solution)/shard_map/all_to_all | solution.py:719
  45.2 11.8 %all-to-all-done.2.refs_2_ = bf16[4,64,1024]{2,1,0:T(8,128)(2,1)S(1)} async-done(((bf16[4,64,1024]{2,1,0:T(8,128)(2,1)}), bf16[4,64,1024]{2,1,0:T(8,128)(2,1)S(1)}, u32[]{:S(2)}, u32[]{:S(2)}) %all-to-all-start.2) | async-done | bytes 524320 | tf_op jit(solution)/shard_map/all_to_all | solution.py:719
  65.5 9.0 %all-to-all-done.q_ref = bf16[4,64,1024]{2,1,0:T(8,128)(2,1)S(1)} async-done(((bf16[4,64,1024]{2,1,0:T(8,128)(2,1)}), bf16[4,64,1024]{2,1,0:T(8,128)(2,1)S(1)}, u32[]{:S(2)}, u32[]{:S(2)}) %all-to-all-start) | async-done | bytes 524320 | tf_op jit(solution)/shard_map/all_to_all | solution.py:719
  74.5 9.2 %attn_fwd.2 = (bf16[4,64,512]{2,1,0:T(8,128)(2,1)}, f32[4,1,512]{2,1,0:T(1,128)S(1)}) custom-call(s32[1]{0:T(128)} %bitcast.5.meta_ref, s32[4]{0:T(128)S(1)} %copy-done.63, bf16[4,64,1024]{2,1,0:T(8,128)(2,1)S(1)} %all-to-all-done.q_ref, bf16[4,64,1024]{2,1,0:T(8,128)(2,1)S(1)} %all-to-all-done.1.refs_0_, ...), custom_call_target="tpu_custom_call" | custom-call | tf_op jit(solution)/shard_map/attn_fwd/pallas_call | solution.py:190
  87.4 11.9 %attn_fwd.3 = (bf16[4,64,512]{2,1,0:T(8,128)(2,1)}, f32[4,1,512]{2,1,0:T(1,128)S(1)}) custom-call(s32[1]{0:T(128)} %bitcast.5.meta_ref, s32[4]{0:T(128)S(1)} %copy-done.63, bf16[4,64,1024]{2,1,0:T(8,128)(2,1)S(1)} %all-to-all-done.q_ref, bf16[4,64,1024]{2,1,0:T(8,128)(2,1)S(1)} %all-to-all-done.1.refs_0_, ...), custom_call_target="tpu_custom_call" | custom-call | tf_op jit(solution)/shard_map/attn_fwd/pallas_call | solution.py:190
  99.3 5.1 %all-to-all-start.4 = ((bf16[4,64,512]{2,1,0:T(8,128)(2,1)}), bf16[4,64,512]{2,1,0:T(8,128)(2,1)S(1)}, u32[]{:S(2)}, u32[]{:S(2)}) async-start(bf16[4,64,512]{2,1,0:T(8,128)(2,1)} %get-tuple-element.95), calls=%async_computation.4 | async-start | bytes 524288 | tf_op jit(solution)/shard_map/all_to_all | solution.py:719
  124.8 5.0 %out_norm.1 = (f32[1024,1024]{1,0:T(8,128)S(1)}, bf16[1024,1024]{1,0:T(8,128)(2,1)S(1)}) custom-call(s32[4]{0:T(128)S(1)} %pad_add_fusion.pos_ref, bf16[256,512]{1,0:T(8,128)(2,1)S(1)} %bitcast.68, bf16[256,512]{1,0:T(8,128)(2,1)S(1)} %collective-permute-done.5.refs_1_, bf16[256,512]{1,0:T(8,128)(2,1)S(1)} %copy-done.58, ...), custom_call_target="tpu_custom_call" | custom-call | tf_op jit(solution)/shard_map/out_norm/pallas_call | solution.py:290
  141.9 6.2 %feed_grads.1 = bf16[2048,1024]{1,0:T(8,128)(2,1)S(1)} custom-call(bf16[1024,1024]{1,0:T(8,128)(2,1)S(1)} %get-tuple-element.102.g_ref, bf16[1024,1024]{1,0:T(8,128)(2,1)S(1)} %copy-done, bf16[1024,1024]{1,0:T(8,128)(2,1)S(1)} %get-tuple-element.99.n2_ref, bf16[1024,1024]{1,0:T(8,128)(2,1)S(1)} %get-tuple-element.109.dh_ref), custom_call_target="tpu_custom_call" | custom-call | tf_op jit(solution)/shard_map/feed_grads/pallas_call | solution.py:447
  169.6 12.8 %collective-permute-done.12.crossed_ref = bf16[512,1024]{1,0:T(8,128)(2,1)} collective-permute-done((bf16[512,1024]{1,0:T(8,128)(2,1)}, bf16[512,1024]{1,0:T(8,128)(2,1)}, u32[]{:S(2)}, u32[]{:S(2)}) %collective-permute-start.12) | collective-permute-done | bytes 1048608 | tf_op jit(solution)/shard_map/ppermute | solution.py:651
  199.1 16.5 %all-to-all-done.5.refs_6_ = bf16[4,64,1024]{2,1,0:T(8,128)(2,1)S(1)} async-done(((bf16[4,64,1024]{2,1,0:T(8,128)(2,1)}), bf16[4,64,1024]{2,1,0:T(8,128)(2,1)S(1)}, u32[]{:S(2)}, u32[]{:S(2)}) %all-to-all-start.5) | async-done | bytes 524320 | tf_op jit(solution)/shard_map/all_to_all | solution.py:719
  215.6 8.5 %all-to-all-start.6 = ((bf16[8,32,1024]{2,1,0:T(8,128)(2,1)}), bf16[8,32,1024]{2,1,0:T(8,128)(2,1)}, u32[]{:S(2)}, u32[]{:S(2)}) async-start(bf16[8,32,1024]{2,1,0:T(8,128)(2,1)} %bitcast.76), calls=%async_computation.6 | async-start | bytes 1048576 | tf_op jit(solution)/shard_map/all_to_all | solution.py:772
  225.3 22.7 %attn_bwd.1 = (bf16[4,64,1024]{2,1,0:T(8,128)(2,1)S(1)}, bf16[4,64,1024]{2,1,0:T(8,128)(2,1)S(1)}, bf16[4,64,1024]{2,1,0:T(8,128)(2,1)S(1)}, bf16[4,64,1024]{2,1,0:T(8,128)(2,1)S(1)}, bf16[4,64,1024]{2,1,0:T(8,128)(2,1)S(1)}) custom-call(s32[1]{0:T(128)} %bitcast.5.meta_ref, s32[4]{0:T(128)S(1)} %copy-done.63, bf16[4,64,1024]{2,1,0:T(8,128)(2,1)S(1)} %copy-done.13, ...), custom_call_target="tpu_custom_call" | custom-call | tf_op jit(solution)/shard_map/attn_bwd/pallas_call | solution.py:212
  252.1 5.2 %all-to-all-start.7 = ((bf16[4,64,1024]{2,1,0:T(8,128)(2,1)}), bf16[4,64,1024]{2,1,0:T(8,128)(2,1)S(1)}, u32[]{:S(2)}, u32[]{:S(2)}) async-start(bf16[4,64,1024]{2,1,0:T(8,128)(2,1)} %copy-done.34), calls=%async_computation.7 | async-start | bytes 1048576 | tf_op jit(solution)/shard_map/all_to_all | solution.py:719
  257.3 11.1 %collective-permute-start.15 = (bf16[4,64,1024]{2,1,0:T(8,128)(2,1)}, bf16[4,64,1024]{2,1,0:T(8,128)(2,1)S(1)}, u32[]{:S(2)}, u32[]{:S(2)}) collective-permute-start(bf16[4,64,1024]{2,1,0:T(8,128)(2,1)} %copy-done.71), channel_id=1, source_target_pairs={{0,4},{4,0},{8,12},{12,8},{16,20},{20,16},{24,28},{28,24},{1,5},{5... | collective-permute-start | bytes 1572872 | tf_op jit(solution)/shard_map/ppermute | solution.py:641
  268.4 10.6 %collective-permute-done.15.other_ref = bf16[4,64,1024]{2,1,0:T(8,128)(2,1)S(1)} collective-permute-done((bf16[4,64,1024]{2,1,0:T(8,128)(2,1)}, bf16[4,64,1024]{2,1,0:T(8,128)(2,1)S(1)}, u32[]{:S(2)}, u32[]{:S(2)}) %collective-permute-start.15) | collective-permute-done | bytes 524320 | tf_op jit(solution)/shard_map/ppermute | solution.py:641
  290.6 9.8 %collective-permute-done.17.other_ref = bf16[4,64,1024]{2,1,0:T(8,128)(2,1)S(1)} collective-permute-done((bf16[4,64,1024]{2,1,0:T(8,128)(2,1)}, bf16[4,64,1024]{2,1,0:T(8,128)(2,1)S(1)}, u32[]{:S(2)}, u32[]{:S(2)}) %collective-permute-start.17) | collective-permute-done | bytes 524320 | tf_op jit(solution)/shard_map/ppermute | solution.py:641
  312.0 7.6 %grad_heads.1 = f32[192,1024]{1,0:T(8,128)S(1)} custom-call(s32[8]{0:T(128)S(1)} %stack.118.spot_ref, bf16[4,64,1024]{2,1,0:T(8,128)(2,1)S(1)} %copy-done.35, bf16[4,64,1024]{2,1,0:T(8,128)(2,1)} %add_low.7.dk_ref, bf16[4,64,1024]{2,1,0:T(8,128)(2,1)} %add_low.8.dv_ref, bf16[1024,1024]{1,0:T(8,128)(2,1)S(1)} %copy-done.24, ...), custom_call_target="tpu_custom_call" | custom-call | tf_op jit(solution)/shard_map/grad_heads/pallas_call | solution.py:499
  348.7 14.7 %collective-permute-done.29 = f32[6,1024]{1,0:T(8,128)S(1)} collective-permute-done((f32[6,1024]{1,0:T(8,128)S(1)}, f32[6,1024]{1,0:T(8,128)S(1)}, u32[]{:S(2)}, u32[]{:S(2)}) %collective-permute-start.29) | collective-permute-done | bytes 24608 | tf_op jit(solution)/shard_map/ppermute | solution.py:651
  363.9 7.1 %collective-permute-done.25.refs_4_ = bf16[256,512]{1,0:T(8,128)(2,1)} collective-permute-done((bf16[256,512]{1,0:T(8,128)(2,1)S(1)}, bf16[256,512]{1,0:T(8,128)(2,1)}, u32[]{:S(2)}, u32[]{:S(2)}) %collective-permute-start.25) | collective-permute-done | bytes 262176 | tf_op jit(solution)/shard_map/ppermute | solution.py:636
  380.5 6.1 %collective-permute-done.31 = f32[12,1024]{1,0:T(8,128)S(1)} collective-permute-done((f32[12,1024]{1,0:T(8,128)S(1)}, f32[12,1024]{1,0:T(8,128)S(1)}, u32[]{:S(2)}, u32[]{:S(2)}) %collective-permute-start.31) | collective-permute-done | bytes 49184 | tf_op jit(solution)/shard_map/ppermute | solution.py:845
  386.7 10.3 %collective-permute-start.32 = (f32[12,1024]{1,0:T(8,128)S(1)}, f32[12,1024]{1,0:T(8,128)S(1)}, u32[]{:S(2)}, u32[]{:S(2)}) collective-permute-start(f32[12,1024]{1,0:T(8,128)S(1)} %add.195), channel_id=1, source_target_pairs={{0,8},{4,12},{8,0},{12,4},{16,24},{20,28},{24,16},{28,20},{1,9},{5... | collective-permute-start | bytes 147464 | tf_op jit(solution)/shard_map/ppermute | solution.py:845
  399.8 6.4 %collective-permute-done.35.refs_3_ = bf16[256,512]{1,0:T(8,128)(2,1)S(1)} collective-permute-done((bf16[256,512]{1,0:T(8,128)(2,1)S(1)}, bf16[256,512]{1,0:T(8,128)(2,1)S(1)}, u32[]{:S(2)}, u32[]{:S(2)}) %collective-permute-start.35) | collective-permute-done | bytes 262176 | tf_op jit(solution)/shard_map/ppermute | solution.py:641
  407.0 4.9 %collective-permute-done.36.refs_5_ = bf16[256,512]{1,0:T(8,128)(2,1)} collective-permute-done((bf16[256,512]{1,0:T(8,128)(2,1)}, bf16[256,512]{1,0:T(8,128)(2,1)}, u32[]{:S(2)}, u32[]{:S(2)}) %collective-permute-start.36) | collective-permute-done | bytes 262176 | tf_op jit(solution)/shard_map/ppermute | solution.py:641
  (296 shorter events, 195.1 us)
Async XLA Ops:
  18.8 20.8 %all-to-all-start.1 = ((bf16[4,64,1024]{2,1,0:T(8,128)(2,1)}), bf16[4,64,1024]{2,1,0:T(8,128)(2,1)S(1)}, u32[]{:S(2)}, u32[]{:S(2)}) async-start(bf16[4,64,1024]{2,1,0:T(8,128)(2,1)} %get-tuple-element.85), calls=%async_computation.1 | async-start | bytes 1048576 | tf_op jit(solution)/shard_map/all_to_all | solution.py:719
  25.2 18.0 %collective-permute-start.1 = (bf16[256,1024]{1,0:T(8,128)(2,1)S(1)}, bf16[256,1024]{1,0:T(8,128)(2,1)}, u32[]{:S(2)}, u32[]{:S(2)}) collective-permute-start(bf16[256,1024]{1,0:T(8,128)(2,1)S(1)} %copy-done.32), channel_id=1, source_target_pairs={{0,2},{1,3},{2,0},{3,1},{4,6},{5,7},{6,4},{7,5},{8,10},{9,11},{10,... | collective-permute-start | bytes 1572872 | tf_op jit(solution)/shard_map/ppermute | solution.py:651
  44.7 17.5 %collective-permute-start = (bf16[256,1024]{1,0:T(8,128)(2,1)S(1)}, bf16[256,1024]{1,0:T(8,128)(2,1)}, u32[]{:S(2)}, u32[]{:S(2)}) collective-permute-start(bf16[256,1024]{1,0:T(8,128)(2,1)S(1)} %copy-done.32), channel_id=1, source_target_pairs={{0,1},{1,0},{2,3},{3,2},{4,5},{5,4},{6,7},{7,6},{8,9},{9,8},{10,11... | collective-permute-start | bytes 1572872 | tf_op jit(solution)/shard_map/ppermute | solution.py:647
  104.4 62.0 %all-gather.6.cloned.1.call-start = ((), (), s32[]{:S(2)}) async-start(), calls=%async_computation.13 | async-start | bytes 2621440 | tf_op jit(solution)/shard_map/all_gather | solution.py:745
  111.4 211.6 %reduce-scatter.2.cloned.1.call-start = ((), (), s32[]{:S(2)}) async-start(), calls=%async_computation.11 | async-start | bytes 4718592 | tf_op jit(solution)/shard_map/reduce_scatter | solution.py:763
  156.8 25.5 %collective-permute-start.12 = (bf16[512,1024]{1,0:T(8,128)(2,1)}, bf16[512,1024]{1,0:T(8,128)(2,1)}, u32[]{:S(2)}, u32[]{:S(2)}) collective-permute-start(bf16[512,1024]{1,0:T(8,128)(2,1)} %add_low.5.own_ref), channel_id=1, source_target_pairs={{0,2},{1,3},{2,0},{3,1},{4,6},{5,7},{6,4},{7,5},{8,10},{9,11},{10,... | collective-permute-start | bytes 3145736 | tf_op jit(solution)/shard_map/ppermute | solution.py:651
  192.9 22.7 %all-to-all-start.5 = ((bf16[4,64,1024]{2,1,0:T(8,128)(2,1)}), bf16[4,64,1024]{2,1,0:T(8,128)(2,1)S(1)}, u32[]{:S(2)}, u32[]{:S(2)}) async-start(bf16[4,64,1024]{2,1,0:T(8,128)(2,1)} %bitcast.77), calls=%async_computation.5 | async-start | bytes 1048576 | tf_op jit(solution)/shard_map/all_to_all | solution.py:719
  197.5 54.6 %collective-permute-start.14 = (bf16[3,256,1024]{2,1,0:T(8,128)(2,1)}, bf16[3,256,1024]{2,1,0:T(8,128)(2,1)}, u32[]{:S(2)}, u32[]{:S(2)}) collective-permute-start(bf16[3,256,1024]{2,1,0:T(8,128)(2,1)} %pad_maximum_fusion.2.refs_0_), channel_id=1, source_target_pairs={{0,2},{1,3},{2,0},{3,1},{4,6},{5,7},{6,4},{7,5},{8,10},{9,11},{10,... | collective-permute-start | bytes 4718600 | tf_op jit(solution)/shard_map/ppermute | solution.py:651
  215.6 36.5 %all-to-all-start.6 = ((bf16[8,32,1024]{2,1,0:T(8,128)(2,1)}), bf16[8,32,1024]{2,1,0:T(8,128)(2,1)}, u32[]{:S(2)}, u32[]{:S(2)}) async-start(bf16[8,32,1024]{2,1,0:T(8,128)(2,1)} %bitcast.76), calls=%async_computation.6 | async-start | bytes 1048576 | tf_op jit(solution)/shard_map/all_to_all | solution.py:772
  252.1 26.8 %all-to-all-start.7 = ((bf16[4,64,1024]{2,1,0:T(8,128)(2,1)}), bf16[4,64,1024]{2,1,0:T(8,128)(2,1)S(1)}, u32[]{:S(2)}, u32[]{:S(2)}) async-start(bf16[4,64,1024]{2,1,0:T(8,128)(2,1)} %copy-done.34), calls=%async_computation.7 | async-start | bytes 1048576 | tf_op jit(solution)/shard_map/all_to_all | solution.py:719
  257.3 21.6 %collective-permute-start.15 = (bf16[4,64,1024]{2,1,0:T(8,128)(2,1)}, bf16[4,64,1024]{2,1,0:T(8,128)(2,1)S(1)}, u32[]{:S(2)}, u32[]{:S(2)}) collective-permute-start(bf16[4,64,1024]{2,1,0:T(8,128)(2,1)} %copy-done.71), channel_id=1, source_target_pairs={{0,4},{4,0},{8,12},{12,8},{16,20},{20,16},{24,28},{28,24},{1,5},{5... | collective-permute-start | bytes 1572872 | tf_op jit(solution)/shard_map/ppermute | solution.py:641
  280.9 20.3 %all-to-all-start.8 = ((bf16[4,64,1024]{2,1,0:T(8,128)(2,1)}), bf16[4,64,1024]{2,1,0:T(8,128)(2,1)S(1)}, u32[]{:S(2)}, u32[]{:S(2)}) async-start(bf16[4,64,1024]{2,1,0:T(8,128)(2,1)} %add_low.7.dk_ref), calls=%async_computation.8 | async-start | bytes 1048576 | tf_op jit(solution)/shard_map/all_to_all | solution.py:719
  285.7 23.6 %collective-permute-start.18 = (bf16[3,256,1024]{2,1,0:T(8,128)(2,1)}, bf16[3,256,1024]{2,1,0:T(8,128)(2,1)}, u32[]{:S(2)}, u32[]{:S(2)}) collective-permute-start(bf16[3,256,1024]{2,1,0:T(8,128)(2,1)} %pad_maximum_fusion.2.refs_0_), channel_id=1, source_target_pairs={{0,1},{1,0},{2,3},{3,2},{4,5},{5,4},{6,7},{7,6},{8,9},{9,8},{10,11... | collective-permute-start | bytes 4718600 | tf_op jit(solution)/shard_map/ppermute | solution.py:647
  285.9 23.4 %collective-permute-start.19 = (bf16[3,256,1024]{2,1,0:T(8,128)(2,1)}, bf16[3,256,1024]{2,1,0:T(8,128)(2,1)}, u32[]{:S(2)}, u32[]{:S(2)}) collective-permute-start(bf16[3,256,1024]{2,1,0:T(8,128)(2,1)} %collective-permute-done.14.refs_1_), channel_id=1, source_target_pairs={{0,1},{1,0},{2,3},{3,2},{4,5},{5,4},{6,7},{7,6},{8,9},{9,8},{10,11... | collective-permute-start | bytes 4718600 | tf_op jit(solution)/shard_map/ppermute | solution.py:647
  289.1 33.9 %collective-permute-start.20 = (bf16[512,1024]{1,0:T(8,128)(2,1)}, bf16[512,1024]{1,0:T(8,128)(2,1)}, u32[]{:S(2)}, u32[]{:S(2)}) collective-permute-start(bf16[512,1024]{1,0:T(8,128)(2,1)} %add_low.6), channel_id=1, source_target_pairs={{0,2},{1,3},{2,0},{3,1},{4,6},{5,7},{6,4},{7,5},{8,10},{9,11},{10,... | collective-permute-start | bytes 3145736 | tf_op jit(solution)/shard_map/ppermute | solution.py:651
  304.3 18.8 %all-to-all-start.9 = ((bf16[4,64,1024]{2,1,0:T(8,128)(2,1)}), bf16[4,64,1024]{2,1,0:T(8,128)(2,1)S(1)}, u32[]{:S(2)}, u32[]{:S(2)}) async-start(bf16[4,64,1024]{2,1,0:T(8,128)(2,1)} %add_low.8.dv_ref), calls=%async_computation.9 | async-start | bytes 1048576 | tf_op jit(solution)/shard_map/all_to_all | solution.py:719
  309.2 119.5 %all-gather.4.cloned.1.call-start = ((), (), s32[]{:S(2)}) async-start(), calls=%async_computation.12 | async-start | bytes 4718592 | tf_op jit(solution)/shard_map/all_gather | solution.py:809
  337.2 33.8 %collective-permute-start.22 = (bf16[512,1024]{1,0:T(8,128)(2,1)}, bf16[512,1024]{1,0:T(8,128)(2,1)}, u32[]{:S(2)}, u32[]{:S(2)}) collective-permute-start(bf16[512,1024]{1,0:T(8,128)(2,1)} %add_low.9.own_ref), channel_id=1, source_target_pairs={{0,2},{1,3},{2,0},{3,1},{4,6},{5,7},{6,4},{7,5},{8,10},{9,11},{10,... | collective-permute-start | bytes 3145736 | tf_op jit(solution)/shard_map/ppermute | solution.py:651
  343.1 20.8 %collective-permute-start.24 = (bf16[256,512]{1,0:T(8,128)(2,1)S(1)}, bf16[256,512]{1,0:T(8,128)(2,1)S(1)}, u32[]{:S(2)}, u32[]{:S(2)}) collective-permute-start(bf16[256,512]{1,0:T(8,128)(2,1)S(1)} %pad_maximum_fusion.4.refs_0_), channel_id=1, source_target_pairs={{0,8},{4,12},{8,16},{12,20},{16,24},{20,28},{24,0},{28,4},{1,9},{5... | collective-permute-start | bytes 786440 | tf_op jit(solution)/shard_map/ppermute | solution.py:636
  343.4 27.6 %collective-permute-start.25 = (bf16[256,512]{1,0:T(8,128)(2,1)S(1)}, bf16[256,512]{1,0:T(8,128)(2,1)}, u32[]{:S(2)}, u32[]{:S(2)}) collective-permute-start(bf16[256,512]{1,0:T(8,128)(2,1)S(1)} %pad_maximum_fusion.4.refs_0_), channel_id=1, source_target_pairs={{0,16},{4,20},{8,24},{12,28},{16,0},{20,4},{24,8},{28,12},{1,17},{... | collective-permute-start | bytes 786440 | tf_op jit(solution)/shard_map/ppermute | solution.py:636
  346.8 24.3 %collective-permute-start.26 = (bf16[256,512]{1,0:T(8,128)(2,1)S(1)}, bf16[256,512]{1,0:T(8,128)(2,1)}, u32[]{:S(2)}, u32[]{:S(2)}) collective-permute-start(bf16[256,512]{1,0:T(8,128)(2,1)S(1)} %pad_maximum_fusion.4.refs_0_), channel_id=1, source_target_pairs={{0,24},{4,28},{8,0},{12,4},{16,8},{20,12},{24,16},{28,20},{1,25},{... | collective-permute-start | bytes 786440 | tf_op jit(solution)/shard_map/ppermute | solution.py:636
  363.5 33.6 %collective-permute-start.34 = (bf16[256,512]{1,0:T(8,128)(2,1)S(1)}, bf16[256,512]{1,0:T(8,128)(2,1)S(1)}, u32[]{:S(2)}, u32[]{:S(2)}) collective-permute-start(bf16[256,512]{1,0:T(8,128)(2,1)S(1)} %pad_maximum_fusion.4.refs_0_), channel_id=1, source_target_pairs={{0,4},{4,0},{8,12},{12,8},{16,20},{20,16},{24,28},{28,24},{1,5},{5... | collective-permute-start | bytes 786440 | tf_op jit(solution)/shard_map/ppermute | solution.py:641
  377.7 46.8 %collective-permute-start.28 = (bf16[512,1024]{1,0:T(8,128)(2,1)}, bf16[512,1024]{1,0:T(8,128)(2,1)S(1)}, u32[]{:S(2)}, u32[]{:S(2)}) collective-permute-start(bf16[512,1024]{1,0:T(8,128)(2,1)} %get-tuple-element.143.own_ref), channel_id=1, source_target_pairs={{0,1},{1,0},{2,3},{3,2},{4,5},{5,4},{6,7},{7,6},{8,9},{9,8},{10,11... | collective-permute-start | bytes 3145736 | tf_op jit(solution)/shard_map/ppermute | solution.py:647
  380.2 47.0 %collective-permute-start.27 = (bf16[512,1024]{1,0:T(8,128)(2,1)S(1)}, bf16[512,1024]{1,0:T(8,128)(2,1)S(1)}, u32[]{:S(2)}, u32[]{:S(2)}) collective-permute-start(bf16[512,1024]{1,0:T(8,128)(2,1)S(1)} %add_convert_fusion.own_ref), channel_id=1, source_target_pairs={{0,1},{1,0},{2,3},{3,2},{4,5},{5,4},{6,7},{7,6},{8,9},{9,8},{10,11... | collective-permute-start | bytes 3145736 | tf_op jit(solution)/shard_map/ppermute | solution.py:647
  (101 other events, 866.5 us)
Sparse Core Ops, SparseCore 0:
  111.6 54.8 all-gather.5
Sparse Core Ops, SparseCore 1:
  151.5 104.1 reduce-scatter.1
  323.2 93.7 all-gather.3

commit v4 on v3

--- a/solution.py
+++ b/solution.py
@@ -30,6 +30,10 @@
     centred = values - jnp.mean(values, axis=-1, keepdims=True)
     spread = jnp.mean(centred * centred, axis=-1, keepdims=True)
     return centred * lax.rsqrt(spread + EPS) * weight_row + shift_row
+
+
+def far(value):
+    return pltpu.with_memory_space_constraint(value, pltpu.HBM)
 
 
 def cost(flops, moved):
@@ -181,7 +185,7 @@
 
 
 def attn_params(keys):
-    return pltpu.CompilerParams(vmem_limit_bytes=(58 if keys > 8192 else 40) * MIB)
+    return pltpu.CompilerParams(vmem_limit_bytes=(58 if keys > 8192 else 24) * MIB)
 
 
 def attn_fwd(meta, seq, q, ks, vs, part, bq=512, bk=512):
@@ -254,13 +258,13 @@
     return pl.pallas_call(
         qkv_kernel,
         grid=(T // rows,),
-        out_shape=(jax.ShapeDtypeStruct((T, D), LOW), heads, heads, heads),
+        out_shape=(pltpu.HBM((T, D), LOW), heads, heads, heads),
         in_specs=[row_spec, V, V, V, V],
         out_specs=(row_spec, head_spec, head_spec, head_spec),
-        compiler_params=pltpu.CompilerParams(vmem_limit_bytes=24 * MIB),
+        compiler_params=pltpu.CompilerParams(vmem_limit_bytes=12 * MIB),
         cost_estimate=cost(6 * T * D * local, 8 * MIB),
         name="norm_qkv",
-    )(x, gain[None], bias[None], w, b)
+    )(far(x), far(gain[None]), far(bias[None]), far(w), far(b))
 
 
 def out_kernel(pos_ref, *refs):
@@ -290,14 +294,14 @@
     return pl.pallas_call(
         out_kernel,
         grid=(T // rows,),
-        out_shape=(jax.ShapeDtypeStruct((T, D), F32), jax.ShapeDtypeStruct((T, D), LOW)),
+        out_shape=(pltpu.HBM((T, D), F32), jax.ShapeDtypeStruct((T, D), LOW)),
         in_specs=[M] + [V] * 9 + [row_spec, V, V, V],
         out_specs=(row_spec, row_spec),
         scratch_shapes=[pltpu.VMEM((4, local, T), LOW)],
-        compiler_params=pltpu.CompilerParams(vmem_limit_bytes=32 * MIB),
+        compiler_params=pltpu.CompilerParams(vmem_limit_bytes=16 * MIB),
         cost_estimate=cost(2 * T * D * 4 * local, 12 * MIB),
         name="out_norm",
-    )(pos, *pieces, w, x, b[None], gain[None], bias[None])
+    )(pos, *pieces, far(w), far(x), far(b[None]), far(gain[None]), far(bias[None]))
 
 
 def mlp_kernel(at_ref, n2_ref, dm_ref, wf_ref, wp_ref, b_ref, *refs):
@@ -342,11 +346,11 @@
         out_shape=(
             jax.ShapeDtypeStruct((T, F), LOW),
             jax.ShapeDtypeStruct((T, F), LOW),
-            jax.ShapeDtypeStruct((T // 2, D), LOW),
+            pltpu.HBM((T // 2, D), LOW),
             jax.ShapeDtypeStruct((1, F), F32),
         ),
         input_output_aliases={6 + i: i for i in range(len(before))},
-        compiler_params=pltpu.CompilerParams(vmem_limit_bytes=40 * MIB),
+        compiler_params=pltpu.CompilerParams(vmem_limit_bytes=18 * MIB),
         cost_estimate=cost(3 * T * D * F, 9 * MIB),
         name="feed",
     )(at, n2, dm, w_fc, w_proj, b_fc[None], *before)
@@ -394,10 +398,10 @@
             jax.ShapeDtypeStruct((half, D), LOW),
             jax.ShapeDtypeStruct((4, D), F32),
         ),
-        compiler_params=pltpu.CompilerParams(vmem_limit_bytes=24 * MIB),
+        compiler_params=pltpu.CompilerParams(vmem_limit_bytes=12 * MIB),
         cost_estimate=cost(0, 14 * half * D),
         name="norm_back",
-    )(at, own, crossed, x, kept, gain[None])
+    )(at, own, crossed, far(x), kept, gain[None])
 
 
 def first_kernel(core_ref, q_ref, k_ref, v_ref, w_ref, keep_ref, send_ref):
@@ -419,7 +423,7 @@
         out_shape=(part, part),
         in_specs=[M, V, V, V, V],
         out_specs=(V, V),
-        compiler_params=pltpu.CompilerParams(vmem_limit_bytes=24 * MIB),
+        compiler_params=pltpu.CompilerParams(vmem_limit_bytes=10 * MIB),
         cost_estimate=cost(10**6, 1000),
         name="first_grad",
     )(core, q, k, v, w)
@@ -447,10 +451,10 @@
     return pl.pallas_call(
         feed_grads_kernel,
         grid=((F + D) // rows,),
-        out_shape=jax.ShapeDtypeStruct((F + D, D), LOW),
+        out_shape=pltpu.HBM((F + D, D), LOW),
         in_specs=[V] * 4,
         out_specs=pl.BlockSpec((rows, D), lambda i: (i, 0)),
-        compiler_params=pltpu.CompilerParams(vmem_limit_bytes=32 * MIB),
+        compiler_params=pltpu.CompilerParams(vmem_limit_bytes=10 * MIB),
         cost_estimate=cost(4 * T * D * F, 12 * MIB),
         name="feed_grads",
     )(g, dm, n2, dh)
@@ -475,7 +479,7 @@
         out_shape=(jax.ShapeDtypeStruct((local, T), LOW), jax.ShapeDtypeStruct((local, D), LOW)),
         in_specs=[M, V, V, V, V, V],
         out_specs=(V, V),
-        compiler_params=pltpu.CompilerParams(vmem_limit_bytes=24 * MIB),
+        compiler_params=pltpu.CompilerParams(vmem_limit_bytes=8 * MIB),
         cost_estimate=cost(4 * T * D * local, 5 * MIB),
         name="heads_grad",
     )(core, own, other, w_out, home_one, home_two)
@@ -501,7 +505,7 @@
         out_shape=jax.ShapeDtypeStruct((3 * HEAD_DIM, D), F32),
         in_specs=[M] + [V] * (4 + len(parts)),
         out_specs=V,
-        compiler_params=pltpu.CompilerParams(vmem_limit_bytes=24 * MIB),
+        compiler_params=pltpu.CompilerParams(vmem_limit_bytes=12 * MIB),
         cost_estimate=cost(10**6, 1000),
         name="grad_heads",
     )(spots, dq, dk, dv, own, *parts)
@@ -537,7 +541,7 @@
         in_specs=[M] + [V] * len(parts),
         out_specs=(V, V),
         scratch_shapes=[pltpu.VMEM((J, 3 * HEAD_DIM, S * wide), LOW)],
-        compiler_params=pltpu.CompilerParams(vmem_limit_bytes=24 * MIB),
+        compiler_params=pltpu.CompilerParams(vmem_limit_bytes=12 * MIB),
         cost_estimate=cost(0, 6 * MIB),
         name="lay_blocks",
     )(spots, *parts)
@@ -553,7 +557,7 @@
         out_shape=jax.ShapeDtypeStruct(own.shape, LOW),
         in_specs=[V, V],
         out_specs=V,
-        compiler_params=pltpu.CompilerParams(vmem_limit_bytes=16 * MIB),
+        compiler_params=pltpu.CompilerParams(vmem_limit_bytes=6 * MIB),
         cost_estimate=cost(0, 6 * own.size),
         name="add_low",
     )(own, other)
@@ -575,7 +579,7 @@
         out_shape=(part, part),
         in_specs=[M, V, V],
         out_specs=(V, V),
-        compiler_params=pltpu.CompilerParams(vmem_limit_bytes=24 * MIB),
+        compiler_params=pltpu.CompilerParams(vmem_limit_bytes=8 * MIB),
         cost_estimate=cost(2 * T * F * D, 6 * MIB),
         name="feed_out",
     )(core, g, w)
@@ -606,7 +610,7 @@
             pl.BlockSpec((block, D), lambda i: (jnp.minimum(i, steps - 1), 0)),
             pl.BlockSpec((block, D), lambda i: (jnp.maximum(i - steps, 0), 0)),
         ),
-        compiler_params=pltpu.CompilerParams(vmem_limit_bytes=16 * MIB),
+        compiler_params=pltpu.CompilerParams(vmem_limit_bytes=8 * MIB),
         cost_estimate=cost(0, 12 * MIB),
         name="widen",
     )(low)
@@ -625,7 +629,7 @@
         out_shape=jax.ShapeDtypeStruct((2 * half, D), own.dtype),
         in_specs=[M, V, V],
         out_specs=V,
-        compiler_params=pltpu.CompilerParams(vmem_limit_bytes=16 * MIB),
+        compiler_params=pltpu.CompilerParams(vmem_limit_bytes=6 * MIB),
         cost_estimate=cost(0, 8 * half * D),
         name="lay_pair",
     )(core, own, other)
@@ -821,7 +825,7 @@
     )
     input_grad = lay_pair(core_at, input_half, swap_core(input_half))
 
-    feed_across = gate(feed_across, input_half)
+    feed_across = gate(feed_across, block)
     feed_sum = feed_own.astype(F32) + feed_across.astype(F32)
     middle_half = rows_at(middle, core * half, half)
     output_half = (middle_half + (feed_sum + b_proj)).astype(LOW)
@@ -843,6 +847,8 @@
     step = 1
     while step < count:
         small = small + lax.ppermute(small, "dp", [(i, i ^ step) for i in range(count)])
+        if step == 2:
+            small, input_grad, block_output = tied(small, input_grad, block_output)
         step *= 2
     found = spread_blocks([block, *blocks], j, g, S)
     grad_w_proj, grad_w_fc = widen(grad_feed, w_proj.shape[0])

time: 446 us -> 435 us (0.975)
  local copies, waits for them, and re-layouts: 59.2 us -> 38.2 us
  Pallas kernels: 108 us -> 116 us
    unnamed x151 -> x101, local copies, waits for them, and re-layouts: 49.3 us -> 27.5 us
    ppermute x8, waiting for transfers between devices: 34.9 us -> 21.2 us  [swap_x(): lax.ppermute(value, 'tensor', [(i, i ^ 2) for i in range(lax.axis_size('t...]
    ppermute x3, waiting for transfers between devices: 7.1 us -> 20 us  [shift_dp(): lax.ppermute(value, 'dp', [(i, (i + steps) % count) for i in range(count)])]
    pallas_call x3, Pallas kernels: 15.6 us -> 21 us  [the longest x1 7.54 us: out_stage(): pl.pallas_call(out_kernel, grid=(T // rows,), out_shape=(pltpu.HBM((T, D)...]
  transfers between devices with their start and end apart: 51 -> 51, of which waited for: 22 -> 26; matrix products, arithmetic and copies ran while one was open for 5% -> 5% of each run, Pallas kernels for 20% -> 22%
where the time goes in v4:
time: 435 us; the launch traced here: 432 us
  waiting for transfers between devices  153 us (35%)
  Pallas kernels  116 us (27%)
  starting transfers between devices  96.8 us (22%)
  local copies, waits for them, and re-layouts  38.2 us (9%)
  between operations  16.1 us (4%)
  other arithmetic  11.6 us (3%)
    all_to_all x9, waiting for transfers between devices, exchange(): lax.all_to_all(heads, 'dp', 0, 0, tiled=True, axis_index_groups=groups)  51.5 us
    all_to_all x9, starting transfers between devices, exchange(): lax.all_to_all(heads, 'dp', 0, 0, tiled=True, axis_index_groups=groups)  41.4 us
    ppermute x9, waiting for transfers between devices, shift_group(): lax.ppermute(value, 'dp', [(i, i // S * S + (i % S + steps) % S) for i in...  40.6 us
    unnamed x101, local copies, waits for them, and re-layouts  27.5 us
    pallas_call x1, Pallas kernels, attn_bwd(): pl.pallas_call(functools.partial(bwd_kernel, bq, bk, S), out_shape=[block...  24.4 us
    pallas_call x2, Pallas kernels, attn_fwd(): pl.pallas_call(functools.partial(fwd_kernel, bq, bk, S, part), out_shape=...  22.5 us
    ppermute x8, waiting for transfers between devices, swap_x(): lax.ppermute(value, 'tensor', [(i, i ^ 2) for i in range(lax.axis_size('t...  21.2 us
    ppermute x3, waiting for transfers between devices, shift_dp(): lax.ppermute(value, 'dp', [(i, (i + steps) % count) for i in range(count)])  20 us
  transfers between devices with their start and end apart: 51, of which 26 were waited for; matrix products, arithmetic and copies ran while one was open for 5% of the time, Pallas kernels for 22%

profile of v4, /device:TPU:0, one launch (start us, length us, event | category | flops | bytes accessed | tf_op | source)
XLA Modules:
  0.0 431.7 jit_solution(15446148881374066671)
XLA Ops:
  8.0 6.5 %norm_qkv.1 = (bf16[1024,1024]{1,0:T(8,128)(2,1)}, bf16[4,64,1024]{2,1,0:T(8,128)(2,1)}, bf16[4,64,1024]{2,1,0:T(8,128)(2,1)}, bf16[4,64,1024]{2,1,0:T(8,128)(2,1)}) custom-call(bf16[1024,1024]{1,0:T(8,128)(2,1)} %x_ref.3, f32[1,1024]{1,0:T(1,128)} %bitcast.82, f32[1,1024]{1,0:T(1,128)} %bitcast.87, bf16[3,1024,256]{2,1,0:T(8,128)(2,1)} %w_ref.7, f32[2,256]{1,0:T(2,128)} %b_ref.1), custom_call_target="tpu_custom_call" | custom-call | tf_op jit(solution)/shard_map/norm_qkv/pallas_call | solution.py:258
  14.5 6.3 %all-to-all-start.1 = ((bf16[4,64,1024]{2,1,0:T(8,128)(2,1)}), bf16[4,64,1024]{2,1,0:T(8,128)(2,1)S(1)}, u32[]{:S(2)}, u32[]{:S(2)}) async-start(bf16[4,64,1024]{2,1,0:T(8,128)(2,1)} %get-tuple-element.88), calls=%async_computation.1 | async-start | bytes 1048576 | tf_op jit(solution)/shard_map/all_to_all | solution.py:723
  22.3 13.0 %all-to-all-done.1.refs_0_ = bf16[4,64,1024]{2,1,0:T(8,128)(2,1)S(1)} async-done(((bf16[4,64,1024]{2,1,0:T(8,128)(2,1)}), bf16[4,64,1024]{2,1,0:T(8,128)(2,1)S(1)}, u32[]{:S(2)}, u32[]{:S(2)}) %all-to-all-start.1) | async-done | bytes 524320 | tf_op jit(solution)/shard_map/all_to_all | solution.py:723
  40.9 11.9 %all-to-all-done.2.refs_2_ = bf16[4,64,1024]{2,1,0:T(8,128)(2,1)S(1)} async-done(((bf16[4,64,1024]{2,1,0:T(8,128)(2,1)}), bf16[4,64,1024]{2,1,0:T(8,128)(2,1)S(1)}, u32[]{:S(2)}, u32[]{:S(2)}) %all-to-all-start.2) | async-done | bytes 524320 | tf_op jit(solution)/shard_map/all_to_all | solution.py:723
  61.2 9.0 %all-to-all-done.q_ref = bf16[4,64,1024]{2,1,0:T(8,128)(2,1)S(1)} async-done(((bf16[4,64,1024]{2,1,0:T(8,128)(2,1)}), bf16[4,64,1024]{2,1,0:T(8,128)(2,1)S(1)}, u32[]{:S(2)}, u32[]{:S(2)}) %all-to-all-start) | async-done | bytes 524320 | tf_op jit(solution)/shard_map/all_to_all | solution.py:723
  70.2 9.8 %attn_fwd.2 = (bf16[4,64,512]{2,1,0:T(8,128)(2,1)}, f32[4,1,512]{2,1,0:T(1,128)S(1)}) custom-call(s32[1]{0:T(128)} %bitcast.5.meta_ref, s32[4]{0:T(128)S(1)} %copy-done.44, bf16[4,64,1024]{2,1,0:T(8,128)(2,1)S(1)} %all-to-all-done.q_ref, bf16[4,64,1024]{2,1,0:T(8,128)(2,1)S(1)} %all-to-all-done.1.refs_0_, ...), custom_call_target="tpu_custom_call" | custom-call | tf_op jit(solution)/shard_map/attn_fwd/pallas_call | solution.py:194
  83.7 12.7 %attn_fwd.3 = (bf16[4,64,512]{2,1,0:T(8,128)(2,1)}, f32[4,1,512]{2,1,0:T(1,128)S(1)}) custom-call(s32[1]{0:T(128)} %bitcast.5.meta_ref, s32[4]{0:T(128)S(1)} %copy-done.44, bf16[4,64,1024]{2,1,0:T(8,128)(2,1)S(1)} %all-to-all-done.q_ref, bf16[4,64,1024]{2,1,0:T(8,128)(2,1)S(1)} %all-to-all-done.1.refs_0_, ...), custom_call_target="tpu_custom_call" | custom-call | tf_op jit(solution)/shard_map/attn_fwd/pallas_call | solution.py:194
  118.6 7.5 %out_norm.1 = (f32[1024,1024]{1,0:T(8,128)}, bf16[1024,1024]{1,0:T(8,128)(2,1)S(1)}) custom-call(s32[4]{0:T(128)S(1)} %pad_add_fusion.pos_ref, bf16[256,512]{1,0:T(8,128)(2,1)S(1)} %bitcast.68, bf16[256,512]{1,0:T(8,128)(2,1)S(1)} %collective-permute-done.5.refs_1_, bf16[256,512]{1,0:T(8,128)(2,1)S(1)} %copy-done.40, ...), custom_call_target="tpu_custom_call" | custom-call | tf_op jit(solution)/shard_map/out_norm/pallas_call | solution.py:294
  135.8 7.0 %feed_grads.1 = bf16[2048,1024]{1,0:T(8,128)(2,1)} custom-call(bf16[1024,1024]{1,0:T(8,128)(2,1)S(1)} %get-tuple-element.106.g_ref, bf16[1024,1024]{1,0:T(8,128)(2,1)S(1)} %copy-done, bf16[1024,1024]{1,0:T(8,128)(2,1)S(1)} %get-tuple-element.101.n2_ref, bf16[1024,1024]{1,0:T(8,128)(2,1)S(1)} %get-tuple-element.107.dh_ref), custom_call_target="tpu_custom_call" | custom-call | tf_op jit(solution)/shard_map/feed_grads/pallas_call | solution.py:451
  163.6 11.3 %collective-permute-done.12.crossed_ref = bf16[512,1024]{1,0:T(8,128)(2,1)} collective-permute-done((bf16[512,1024]{1,0:T(8,128)(2,1)}, bf16[512,1024]{1,0:T(8,128)(2,1)}, u32[]{:S(2)}, u32[]{:S(2)}) %collective-permute-start.12) | collective-permute-done | bytes 1048608 | tf_op jit(solution)/shard_map/ppermute | solution.py:655
  191.8 13.7 %all-to-all-done.5.refs_6_ = bf16[4,64,1024]{2,1,0:T(8,128)(2,1)S(1)} async-done(((bf16[4,64,1024]{2,1,0:T(8,128)(2,1)}), bf16[4,64,1024]{2,1,0:T(8,128)(2,1)S(1)}, u32[]{:S(2)}, u32[]{:S(2)}) %all-to-all-start.5) | async-done | bytes 524320 | tf_op jit(solution)/shard_map/all_to_all | solution.py:723
  205.6 8.5 %all-to-all-start.6 = ((bf16[8,32,1024]{2,1,0:T(8,128)(2,1)}), bf16[8,32,1024]{2,1,0:T(8,128)(2,1)}, u32[]{:S(2)}, u32[]{:S(2)}) async-start(bf16[8,32,1024]{2,1,0:T(8,128)(2,1)} %bitcast.76), calls=%async_computation.6 | async-start | bytes 1048576 | tf_op jit(solution)/shard_map/all_to_all | solution.py:776
  215.2 24.4 %attn_bwd.1 = (bf16[4,64,1024]{2,1,0:T(8,128)(2,1)S(1)}, bf16[4,64,1024]{2,1,0:T(8,128)(2,1)S(1)}, bf16[4,64,1024]{2,1,0:T(8,128)(2,1)S(1)}, bf16[4,64,1024]{2,1,0:T(8,128)(2,1)S(1)}, bf16[4,64,1024]{2,1,0:T(8,128)(2,1)S(1)}) custom-call(s32[1]{0:T(128)} %bitcast.5.meta_ref, s32[4]{0:T(128)S(1)} %copy-done.44, bf16[4,64,1024]{2,1,0:T(8,128)(2,1)S(1)} %copy-done.6, ...), custom_call_target="tpu_custom_call" | custom-call | tf_op jit(solution)/shard_map/attn_bwd/pallas_call | solution.py:216
  243.7 5.2 %all-to-all-start.7 = ((bf16[4,64,1024]{2,1,0:T(8,128)(2,1)}), bf16[4,64,1024]{2,1,0:T(8,128)(2,1)S(1)}, u32[]{:S(2)}, u32[]{:S(2)}) async-start(bf16[4,64,1024]{2,1,0:T(8,128)(2,1)} %copy-done.24), calls=%async_computation.7 | async-start | bytes 1048576 | tf_op jit(solution)/shard_map/all_to_all | solution.py:723
  248.9 7.8 %collective-permute-start.15 = (bf16[4,64,1024]{2,1,0:T(8,128)(2,1)}, bf16[4,64,1024]{2,1,0:T(8,128)(2,1)S(1)}, u32[]{:S(2)}, u32[]{:S(2)}) collective-permute-start(bf16[4,64,1024]{2,1,0:T(8,128)(2,1)} %copy-done.47), channel_id=1, source_target_pairs={{0,4},{4,0},{8,12},{12,8},{16,20},{20,16},{24,28},{28,24},{1,5},{5... | collective-permute-start | bytes 1572872 | tf_op jit(solution)/shard_map/ppermute | solution.py:645
  256.7 10.5 %collective-permute-done.15.other_ref = bf16[4,64,1024]{2,1,0:T(8,128)(2,1)S(1)} collective-permute-done((bf16[4,64,1024]{2,1,0:T(8,128)(2,1)}, bf16[4,64,1024]{2,1,0:T(8,128)(2,1)S(1)}, u32[]{:S(2)}, u32[]{:S(2)}) %collective-permute-start.15) | collective-permute-done | bytes 524320 | tf_op jit(solution)/shard_map/ppermute | solution.py:645
  278.9 9.8 %collective-permute-done.16.other_ref = bf16[4,64,1024]{2,1,0:T(8,128)(2,1)S(1)} collective-permute-done((bf16[4,64,1024]{2,1,0:T(8,128)(2,1)}, bf16[4,64,1024]{2,1,0:T(8,128)(2,1)S(1)}, u32[]{:S(2)}, u32[]{:S(2)}) %collective-permute-start.16) | collective-permute-done | bytes 524320 | tf_op jit(solution)/shard_map/ppermute | solution.py:645
  300.4 7.6 %grad_heads.1 = f32[192,1024]{1,0:T(8,128)S(1)} custom-call(s32[8]{0:T(128)S(1)} %stack.118.spot_ref, bf16[4,64,1024]{2,1,0:T(8,128)(2,1)S(1)} %copy-done.25, bf16[4,64,1024]{2,1,0:T(8,128)(2,1)} %add_low.6.dk_ref, bf16[4,64,1024]{2,1,0:T(8,128)(2,1)} %add_low.7.dv_ref, bf16[1024,1024]{1,0:T(8,128)(2,1)S(1)} %copy-done.14, ...), custom_call_target="tpu_custom_call" | custom-call | tf_op jit(solution)/shard_map/grad_heads/pallas_call | solution.py:503
  339.5 9.4 %collective-permute-done.24.refs_2_ = bf16[256,512]{1,0:T(8,128)(2,1)S(1)} collective-permute-done((bf16[256,512]{1,0:T(8,128)(2,1)S(1)}, bf16[256,512]{1,0:T(8,128)(2,1)S(1)}, u32[]{:S(2)}, u32[]{:S(2)}) %collective-permute-start.24) | collective-permute-done | bytes 262176 | tf_op jit(solution)/shard_map/ppermute | solution.py:640
  348.8 10.7 %collective-permute-done.25.refs_4_ = bf16[256,512]{1,0:T(8,128)(2,1)S(1)} collective-permute-done((bf16[256,512]{1,0:T(8,128)(2,1)S(1)}, bf16[256,512]{1,0:T(8,128)(2,1)S(1)}, u32[]{:S(2)}, u32[]{:S(2)}) %collective-permute-start.25) | collective-permute-done | bytes 262176 | tf_op jit(solution)/shard_map/ppermute | solution.py:640
  369.3 6.0 %collective-permute-done.29 = f32[12,1024]{1,0:T(8,128)S(1)} collective-permute-done((f32[12,1024]{1,0:T(8,128)S(1)}, f32[12,1024]{1,0:T(8,128)S(1)}, u32[]{:S(2)}, u32[]{:S(2)}) %collective-permute-start.29) | collective-permute-done | bytes 49184 | tf_op jit(solution)/shard_map/ppermute | solution.py:849
  375.3 12.0 %collective-permute-start.30 = (f32[12,1024]{1,0:T(8,128)S(1)}, f32[12,1024]{1,0:T(8,128)S(1)}, u32[]{:S(2)}, u32[]{:S(2)}) collective-permute-start(f32[12,1024]{1,0:T(8,128)S(1)} %add.190), channel_id=1, source_target_pairs={{0,8},{4,12},{8,0},{12,4},{16,24},{20,28},{24,16},{28,20},{1,9},{5... | collective-permute-start | bytes 147464 | tf_op jit(solution)/shard_map/ppermute | solution.py:849
  396.6 5.6 %collective-permute-done.35.refs_3_ = bf16[256,512]{1,0:T(8,128)(2,1)S(1)} collective-permute-done((bf16[256,512]{1,0:T(8,128)(2,1)S(1)}, bf16[256,512]{1,0:T(8,128)(2,1)S(1)}, u32[]{:S(2)}, u32[]{:S(2)}) %collective-permute-start.35) | collective-permute-done | bytes 262176 | tf_op jit(solution)/shard_map/ppermute | solution.py:645
  402.2 5.6 %collective-permute-done.36.refs_5_ = bf16[256,512]{1,0:T(8,128)(2,1)S(1)} collective-permute-done((bf16[256,512]{1,0:T(8,128)(2,1)S(1)}, bf16[256,512]{1,0:T(8,128)(2,1)S(1)}, u32[]{:S(2)}, u32[]{:S(2)}) %collective-permute-start.36) | collective-permute-done | bytes 262176 | tf_op jit(solution)/shard_map/ppermute | solution.py:645
  (246 shorter events, 183.7 us)
Async XLA Ops:
  14.5 20.8 %all-to-all-start.1 = ((bf16[4,64,1024]{2,1,0:T(8,128)(2,1)}), bf16[4,64,1024]{2,1,0:T(8,128)(2,1)S(1)}, u32[]{:S(2)}, u32[]{:S(2)}) async-start(bf16[4,64,1024]{2,1,0:T(8,128)(2,1)} %get-tuple-element.88), calls=%async_computation.1 | async-start | bytes 1048576 | tf_op jit(solution)/shard_map/all_to_all | solution.py:723
  20.8 18.0 %collective-permute-start.1 = (bf16[256,1024]{1,0:T(8,128)(2,1)S(1)}, bf16[256,1024]{1,0:T(8,128)(2,1)}, u32[]{:S(2)}, u32[]{:S(2)}) collective-permute-start(bf16[256,1024]{1,0:T(8,128)(2,1)S(1)} %copy-done.22), channel_id=1, source_target_pairs={{0,2},{1,3},{2,0},{3,1},{4,6},{5,7},{6,4},{7,5},{8,10},{9,11},{10,... | collective-permute-start | bytes 1572872 | tf_op jit(solution)/shard_map/ppermute | solution.py:655
  101.5 59.4 %all-gather.6.cloned.1.call-start = ((), (), s32[]{:S(2)}) async-start(), calls=%async_computation.13 | async-start | bytes 2621440 | tf_op jit(solution)/shard_map/all_gather | solution.py:749
  108.5 203.0 %reduce-scatter.2.cloned.1.call-start = ((), (), s32[]{:S(2)}) async-start(), calls=%async_computation.11 | async-start | bytes 4718592 | tf_op jit(solution)/shard_map/reduce_scatter | solution.py:767
  149.5 25.5 %collective-permute-start.12 = (bf16[512,1024]{1,0:T(8,128)(2,1)}, bf16[512,1024]{1,0:T(8,128)(2,1)}, u32[]{:S(2)}, u32[]{:S(2)}) collective-permute-start(bf16[512,1024]{1,0:T(8,128)(2,1)} %add_low.5.own_ref), channel_id=1, source_target_pairs={{0,2},{1,3},{2,0},{3,1},{4,6},{5,7},{6,4},{7,5},{8,10},{9,11},{10,... | collective-permute-start | bytes 3145736 | tf_op jit(solution)/shard_map/ppermute | solution.py:655
  185.9 19.6 %all-to-all-start.5 = ((bf16[4,64,1024]{2,1,0:T(8,128)(2,1)}), bf16[4,64,1024]{2,1,0:T(8,128)(2,1)S(1)}, u32[]{:S(2)}, u32[]{:S(2)}) async-start(bf16[4,64,1024]{2,1,0:T(8,128)(2,1)} %bitcast.77), calls=%async_computation.5 | async-start | bytes 1048576 | tf_op jit(solution)/shard_map/all_to_all | solution.py:723
  190.4 53.3 %collective-permute-start.14 = (bf16[3,256,1024]{2,1,0:T(8,128)(2,1)}, bf16[3,256,1024]{2,1,0:T(8,128)(2,1)}, u32[]{:S(2)}, u32[]{:S(2)}) collective-permute-start(bf16[3,256,1024]{2,1,0:T(8,128)(2,1)} %pad_maximum_fusion.2.refs_0_), channel_id=1, source_target_pairs={{0,2},{1,3},{2,0},{3,1},{4,6},{5,7},{6,4},{7,5},{8,10},{9,11},{10,... | collective-permute-start | bytes 4718600 | tf_op jit(solution)/shard_map/ppermute | solution.py:655
  205.6 38.1 %all-to-all-start.6 = ((bf16[8,32,1024]{2,1,0:T(8,128)(2,1)}), bf16[8,32,1024]{2,1,0:T(8,128)(2,1)}, u32[]{:S(2)}, u32[]{:S(2)}) async-start(bf16[8,32,1024]{2,1,0:T(8,128)(2,1)} %bitcast.76), calls=%async_computation.6 | async-start | bytes 1048576 | tf_op jit(solution)/shard_map/all_to_all | solution.py:776
  243.7 23.6 %all-to-all-start.7 = ((bf16[4,64,1024]{2,1,0:T(8,128)(2,1)}), bf16[4,64,1024]{2,1,0:T(8,128)(2,1)S(1)}, u32[]{:S(2)}, u32[]{:S(2)}) async-start(bf16[4,64,1024]{2,1,0:T(8,128)(2,1)} %copy-done.24), calls=%async_computation.7 | async-start | bytes 1048576 | tf_op jit(solution)/shard_map/all_to_all | solution.py:723
  248.9 18.4 %collective-permute-start.15 = (bf16[4,64,1024]{2,1,0:T(8,128)(2,1)}, bf16[4,64,1024]{2,1,0:T(8,128)(2,1)S(1)}, u32[]{:S(2)}, u32[]{:S(2)}) collective-permute-start(bf16[4,64,1024]{2,1,0:T(8,128)(2,1)} %copy-done.47), channel_id=1, source_target_pairs={{0,4},{4,0},{8,12},{12,8},{16,20},{20,16},{24,28},{28,24},{1,5},{5... | collective-permute-start | bytes 1572872 | tf_op jit(solution)/shard_map/ppermute | solution.py:645
  269.3 20.3 %all-to-all-start.8 = ((bf16[4,64,1024]{2,1,0:T(8,128)(2,1)}), bf16[4,64,1024]{2,1,0:T(8,128)(2,1)S(1)}, u32[]{:S(2)}, u32[]{:S(2)}) async-start(bf16[4,64,1024]{2,1,0:T(8,128)(2,1)} %add_low.6.dk_ref), calls=%async_computation.8 | async-start | bytes 1048576 | tf_op jit(solution)/shard_map/all_to_all | solution.py:723
  274.0 23.7 %collective-permute-start.17 = (bf16[3,256,1024]{2,1,0:T(8,128)(2,1)}, bf16[3,256,1024]{2,1,0:T(8,128)(2,1)}, u32[]{:S(2)}, u32[]{:S(2)}) collective-permute-start(bf16[3,256,1024]{2,1,0:T(8,128)(2,1)} %pad_maximum_fusion.2.refs_0_), channel_id=1, source_target_pairs={{0,1},{1,0},{2,3},{3,2},{4,5},{5,4},{6,7},{7,6},{8,9},{9,8},{10,11... | collective-permute-start | bytes 4718600 | tf_op jit(solution)/shard_map/ppermute | solution.py:651
  274.2 23.4 %collective-permute-start.18 = (bf16[3,256,1024]{2,1,0:T(8,128)(2,1)}, bf16[3,256,1024]{2,1,0:T(8,128)(2,1)}, u32[]{:S(2)}, u32[]{:S(2)}) collective-permute-start(bf16[3,256,1024]{2,1,0:T(8,128)(2,1)} %collective-permute-done.14.refs_1_), channel_id=1, source_target_pairs={{0,1},{1,0},{2,3},{3,2},{4,5},{5,4},{6,7},{7,6},{8,9},{9,8},{10,11... | collective-permute-start | bytes 4718600 | tf_op jit(solution)/shard_map/ppermute | solution.py:651
  277.5 34.0 %collective-permute-start.20 = (bf16[512,1024]{1,0:T(8,128)(2,1)}, bf16[512,1024]{1,0:T(8,128)(2,1)}, u32[]{:S(2)}, u32[]{:S(2)}) collective-permute-start(bf16[512,1024]{1,0:T(8,128)(2,1)} %add_low.8), channel_id=1, source_target_pairs={{0,2},{1,3},{2,0},{3,1},{4,6},{5,7},{6,4},{7,5},{8,10},{9,11},{10,... | collective-permute-start | bytes 3145736 | tf_op jit(solution)/shard_map/ppermute | solution.py:655
  292.7 18.8 %all-to-all-start.9 = ((bf16[4,64,1024]{2,1,0:T(8,128)(2,1)}), bf16[4,64,1024]{2,1,0:T(8,128)(2,1)S(1)}, u32[]{:S(2)}, u32[]{:S(2)}) async-start(bf16[4,64,1024]{2,1,0:T(8,128)(2,1)} %add_low.7.dv_ref), calls=%async_computation.9 | async-start | bytes 1048576 | tf_op jit(solution)/shard_map/all_to_all | solution.py:723
  297.6 119.7 %all-gather.4.cloned.1.call-start = ((), (), s32[]{:S(2)}) async-start(), calls=%async_computation.12 | async-start | bytes 4718592 | tf_op jit(solution)/shard_map/all_gather | solution.py:813
  324.4 35.1 %collective-permute-start.22 = (bf16[512,1024]{1,0:T(8,128)(2,1)S(1)}, bf16[512,1024]{1,0:T(8,128)(2,1)S(1)}, u32[]{:S(2)}, u32[]{:S(2)}) collective-permute-start(bf16[512,1024]{1,0:T(8,128)(2,1)S(1)} %add_low.9.own_ref), channel_id=1, source_target_pairs={{0,2},{1,3},{2,0},{3,1},{4,6},{5,7},{6,4},{7,5},{8,10},{9,11},{10,... | collective-permute-start | bytes 3145736 | tf_op jit(solution)/shard_map/ppermute | solution.py:655
  332.7 26.8 %collective-permute-start.25 = (bf16[256,512]{1,0:T(8,128)(2,1)S(1)}, bf16[256,512]{1,0:T(8,128)(2,1)S(1)}, u32[]{:S(2)}, u32[]{:S(2)}) collective-permute-start(bf16[256,512]{1,0:T(8,128)(2,1)S(1)} %pad_maximum_fusion.4.refs_0_), channel_id=1, source_target_pairs={{0,16},{4,20},{8,24},{12,28},{16,0},{20,4},{24,8},{28,12},{1,17},{... | collective-permute-start | bytes 786440 | tf_op jit(solution)/shard_map/ppermute | solution.py:640
  335.7 23.7 %collective-permute-start.26 = (bf16[256,512]{1,0:T(8,128)(2,1)S(1)}, bf16[256,512]{1,0:T(8,128)(2,1)}, u32[]{:S(2)}, u32[]{:S(2)}) collective-permute-start(bf16[256,512]{1,0:T(8,128)(2,1)S(1)} %pad_maximum_fusion.4.refs_0_), channel_id=1, source_target_pairs={{0,24},{4,28},{8,0},{12,4},{16,8},{20,12},{24,16},{28,20},{1,25},{... | collective-permute-start | bytes 786440 | tf_op jit(solution)/shard_map/ppermute | solution.py:640
  339.2 50.2 %collective-permute-start.32 = (bf16[512,1024]{1,0:T(8,128)(2,1)S(1)}, bf16[512,1024]{1,0:T(8,128)(2,1)S(1)}, u32[]{:S(2)}, u32[]{:S(2)}) collective-permute-start(bf16[512,1024]{1,0:T(8,128)(2,1)S(1)} %add_convert_fusion.own_ref), channel_id=1, source_target_pairs={{0,1},{1,0},{2,3},{3,2},{4,5},{5,4},{6,7},{7,6},{8,9},{9,8},{10,11... | collective-permute-start | bytes 3145736 | tf_op jit(solution)/shard_map/ppermute | solution.py:651
  363.8 30.1 %collective-permute-start.31 = (bf16[512,1024]{1,0:T(8,128)(2,1)S(1)}, bf16[512,1024]{1,0:T(8,128)(2,1)S(1)}, u32[]{:S(2)}, u32[]{:S(2)}) collective-permute-start(bf16[512,1024]{1,0:T(8,128)(2,1)S(1)} %get-tuple-element.149.own_ref), channel_id=1, source_target_pairs={{0,1},{1,0},{2,3},{3,2},{4,5},{5,4},{6,7},{7,6},{8,9},{9,8},{10,11... | collective-permute-start | bytes 3145736 | tf_op jit(solution)/shard_map/ppermute | solution.py:651
  389.4 18.4 %collective-permute-start.36 = (bf16[256,512]{1,0:T(8,128)(2,1)S(1)}, bf16[256,512]{1,0:T(8,128)(2,1)S(1)}, u32[]{:S(2)}, u32[]{:S(2)}) collective-permute-start(bf16[256,512]{1,0:T(8,128)(2,1)S(1)} %collective-permute-done.25.refs_4_), channel_id=1, source_target_pairs={{0,4},{4,0},{8,12},{12,8},{16,20},{20,16},{24,28},{28,24},{1,5},{5... | collective-permute-start | bytes 786440 | tf_op jit(solution)/shard_map/ppermute | solution.py:645
  392.4 19.4 %collective-permute-start.37 = (bf16[256,512]{1,0:T(8,128)(2,1)}, bf16[256,512]{1,0:T(8,128)(2,1)S(1)}, u32[]{:S(2)}, u32[]{:S(2)}) collective-permute-start(bf16[256,512]{1,0:T(8,128)(2,1)} %collective-permute-done.26.refs_6_), channel_id=1, source_target_pairs={{0,4},{4,0},{8,12},{12,8},{16,20},{20,16},{24,28},{28,24},{1,5},{5... | collective-permute-start | bytes 786440 | tf_op jit(solution)/shard_map/ppermute | solution.py:645
  395.4 20.0 %collective-permute-start.33 = (f32[12,1024]{1,0:T(8,128)S(1)}, f32[12,1024]{1,0:T(8,128)S(1)}, u32[]{:S(2)}, u32[]{:S(2)}) collective-permute-start(f32[12,1024]{1,0:T(8,128)S(1)} %add.191), channel_id=1, source_target_pairs={{0,16},{4,20},{8,24},{12,28},{16,0},{20,4},{24,8},{28,12},{1,17},{... | collective-permute-start | bytes 147464 | tf_op jit(solution)/shard_map/ppermute | solution.py:849
  (76 other events, 691.4 us)
Sparse Core Ops, SparseCore 0:
  108.6 52.1 all-gather.5
Sparse Core Ops, SparseCore 1:
  144.2 101.3 reduce-scatter.1
  311.6 92.6 all-gather.3

commit v5 on v4

--- a/solution.py
+++ b/solution.py
@@ -212,12 +212,12 @@
 def attn_bwd(meta, seq, q, ks, vs, o, lse, do, bq=512, bk=512):
     J, _, T = q.shape
     S = len(ks)
-    block = jax.ShapeDtypeStruct((J, HEAD_DIM, T), LOW)
+    block = pltpu.HBM((J, HEAD_DIM, T), LOW)
     out = pl.pallas_call(
         functools.partial(bwd_kernel, bq, bk, S),
         out_shape=[block] * (1 + 2 * S),
         in_specs=[M, M] + [V] * (4 + 2 * S),
-        out_specs=[V] * (1 + 2 * S),
+        out_specs=[pl.BlockSpec()] * (1 + 2 * S),
         scratch_shapes=[
             pltpu.VMEM((S * J, T, HEAD_DIM), LOW),
             pltpu.VMEM((S * J, HEAD_DIM, T), LOW),
@@ -394,7 +394,7 @@
             out_specs=(spec, spec, whole),
         ),
         out_shape=(
-            jax.ShapeDtypeStruct((half, D), F32),
+            pltpu.HBM((half, D), F32),
             jax.ShapeDtypeStruct((half, D), LOW),
             jax.ShapeDtypeStruct((4, D), F32),
         ),
@@ -476,9 +476,9 @@
     T = 2 * home_one.shape[1]
     return pl.pallas_call(
         do_kernel,
-        out_shape=(jax.ShapeDtypeStruct((local, T), LOW), jax.ShapeDtypeStruct((local, D), LOW)),
+        out_shape=(pltpu.HBM((local, T), LOW), pltpu.HBM((local, D), LOW)),
         in_specs=[M, V, V, V, V, V],
-        out_specs=(V, V),
+        out_specs=(pl.BlockSpec(), pl.BlockSpec()),
         compiler_params=pltpu.CompilerParams(vmem_limit_bytes=8 * MIB),
         cost_estimate=cost(4 * T * D * local, 5 * MIB),
         name="heads_grad",

time: 435 us -> 433 us (level)
  local copies, waits for them, and re-layouts: 38.2 us -> 31.4 us
    unnamed x101 -> x85, local copies, waits for them, and re-layouts: 27.5 us -> 20.6 us
where the time goes in v5:
time: 433 us; the launch traced here: 430 us
  waiting for transfers between devices  157 us (36%)
  Pallas kernels  116 us (27%)
  starting transfers between devices  99 us (23%)
  local copies, waits for them, and re-layouts  31.4 us (7%)
  between operations  16 us (4%)
  other arithmetic  11.6 us (3%)
    all_to_all x9, waiting for transfers between devices, exchange(): lax.all_to_all(heads, 'dp', 0, 0, tiled=True, axis_index_groups=groups)  55.6 us
    all_to_all x9, starting transfers between devices, exchange(): lax.all_to_all(heads, 'dp', 0, 0, tiled=True, axis_index_groups=groups)  41.5 us
    ppermute x9, waiting for transfers between devices, shift_group(): lax.ppermute(value, 'dp', [(i, i // S * S + (i % S + steps) % S) for i in...  40.6 us
    pallas_call x1, Pallas kernels, attn_bwd(): pl.pallas_call(functools.partial(bwd_kernel, bq, bk, S), out_shape=[block...  24 us
    pallas_call x2, Pallas kernels, attn_fwd(): pl.pallas_call(functools.partial(fwd_kernel, bq, bk, S, part), out_shape=...  21.1 us
    unnamed x85, local copies, waits for them, and re-layouts  20.6 us
    ppermute x9, starting transfers between devices, shift_group(): lax.ppermute(value, 'dp', [(i, i // S * S + (i % S + steps) % S) for i in...  20.1 us
    ppermute x3, waiting for transfers between devices, shift_dp(): lax.ppermute(value, 'dp', [(i, (i + steps) % count) for i in range(count)])  20 us
  transfers between devices with their start and end apart: 51, of which 26 were waited for; matrix products, arithmetic and copies ran while one was open for 5% of the time, Pallas kernels for 22%

profile of v5, /device:TPU:0, one launch (start us, length us, event | category | flops | bytes accessed | tf_op | source)
XLA Modules:
  0.0 430.3 jit_solution(7695318983279340032)
XLA Ops:
  8.0 6.5 %norm_qkv.1 = (bf16[1024,1024]{1,0:T(8,128)(2,1)}, bf16[4,64,1024]{2,1,0:T(8,128)(2,1)}, bf16[4,64,1024]{2,1,0:T(8,128)(2,1)}, bf16[4,64,1024]{2,1,0:T(8,128)(2,1)}) custom-call(bf16[1024,1024]{1,0:T(8,128)(2,1)} %x_ref.3, f32[1,1024]{1,0:T(1,128)} %bitcast.80, f32[1,1024]{1,0:T(1,128)} %bitcast.87, bf16[3,1024,256]{2,1,0:T(8,128)(2,1)} %w_ref.7, f32[2,256]{1,0:T(2,128)} %b_ref.1), custom_call_target="tpu_custom_call" | custom-call | tf_op jit(solution)/shard_map/norm_qkv/pallas_call | solution.py:258
  14.5 6.3 %all-to-all-start.1 = ((bf16[4,64,1024]{2,1,0:T(8,128)(2,1)}), bf16[4,64,1024]{2,1,0:T(8,128)(2,1)S(1)}, u32[]{:S(2)}, u32[]{:S(2)}) async-start(bf16[4,64,1024]{2,1,0:T(8,128)(2,1)} %get-tuple-element.88), calls=%async_computation.1 | async-start | bytes 1048576 | tf_op jit(solution)/shard_map/all_to_all | solution.py:723
  22.3 13.0 %all-to-all-done.1.refs_0_ = bf16[4,64,1024]{2,1,0:T(8,128)(2,1)S(1)} async-done(((bf16[4,64,1024]{2,1,0:T(8,128)(2,1)}), bf16[4,64,1024]{2,1,0:T(8,128)(2,1)S(1)}, u32[]{:S(2)}, u32[]{:S(2)}) %all-to-all-start.1) | async-done | bytes 524320 | tf_op jit(solution)/shard_map/all_to_all | solution.py:723
  40.9 11.9 %all-to-all-done.2.refs_2_ = bf16[4,64,1024]{2,1,0:T(8,128)(2,1)S(1)} async-done(((bf16[4,64,1024]{2,1,0:T(8,128)(2,1)}), bf16[4,64,1024]{2,1,0:T(8,128)(2,1)S(1)}, u32[]{:S(2)}, u32[]{:S(2)}) %all-to-all-start.2) | async-done | bytes 524320 | tf_op jit(solution)/shard_map/all_to_all | solution.py:723
  61.2 9.0 %all-to-all-done.q_ref = bf16[4,64,1024]{2,1,0:T(8,128)(2,1)S(1)} async-done(((bf16[4,64,1024]{2,1,0:T(8,128)(2,1)}), bf16[4,64,1024]{2,1,0:T(8,128)(2,1)S(1)}, u32[]{:S(2)}, u32[]{:S(2)}) %all-to-all-start) | async-done | bytes 524320 | tf_op jit(solution)/shard_map/all_to_all | solution.py:723
  70.2 9.2 %attn_fwd.2 = (bf16[4,64,512]{2,1,0:T(8,128)(2,1)}, f32[4,1,512]{2,1,0:T(1,128)S(1)}) custom-call(s32[1]{0:T(128)} %bitcast.5.meta_ref, s32[4]{0:T(128)S(1)} %copy-done.38, bf16[4,64,1024]{2,1,0:T(8,128)(2,1)S(1)} %all-to-all-done.q_ref, bf16[4,64,1024]{2,1,0:T(8,128)(2,1)S(1)} %all-to-all-done.1.refs_0_, ...), custom_call_target="tpu_custom_call" | custom-call | tf_op jit(solution)/shard_map/attn_fwd/pallas_call | solution.py:194
  83.1 11.9 %attn_fwd.3 = (bf16[4,64,512]{2,1,0:T(8,128)(2,1)}, f32[4,1,512]{2,1,0:T(1,128)S(1)}) custom-call(s32[1]{0:T(128)} %bitcast.5.meta_ref, s32[4]{0:T(128)S(1)} %copy-done.38, bf16[4,64,1024]{2,1,0:T(8,128)(2,1)S(1)} %all-to-all-done.q_ref, bf16[4,64,1024]{2,1,0:T(8,128)(2,1)S(1)} %all-to-all-done.1.refs_0_, ...), custom_call_target="tpu_custom_call" | custom-call | tf_op jit(solution)/shard_map/attn_fwd/pallas_call | solution.py:194
  117.2 7.5 %out_norm.1 = (f32[1024,1024]{1,0:T(8,128)}, bf16[1024,1024]{1,0:T(8,128)(2,1)S(1)}) custom-call(s32[4]{0:T(128)S(1)} %pad_add_fusion.pos_ref, bf16[256,512]{1,0:T(8,128)(2,1)S(1)} %bitcast.68, bf16[256,512]{1,0:T(8,128)(2,1)S(1)} %collective-permute-done.5.refs_1_, bf16[256,512]{1,0:T(8,128)(2,1)S(1)} %copy-done.34, ...), custom_call_target="tpu_custom_call" | custom-call | tf_op jit(solution)/shard_map/out_norm/pallas_call | solution.py:294
  134.3 7.0 %feed_grads.1 = bf16[2048,1024]{1,0:T(8,128)(2,1)} custom-call(bf16[1024,1024]{1,0:T(8,128)(2,1)S(1)} %get-tuple-element.106.g_ref, bf16[1024,1024]{1,0:T(8,128)(2,1)S(1)} %copy-done, bf16[1024,1024]{1,0:T(8,128)(2,1)S(1)} %get-tuple-element.101.n2_ref, bf16[1024,1024]{1,0:T(8,128)(2,1)S(1)} %get-tuple-element.107.dh_ref), custom_call_target="tpu_custom_call" | custom-call | tf_op jit(solution)/shard_map/feed_grads/pallas_call | solution.py:451
  165.0 8.6 %collective-permute-done.12.crossed_ref = bf16[512,1024]{1,0:T(8,128)(2,1)} collective-permute-done((bf16[512,1024]{1,0:T(8,128)(2,1)}, bf16[512,1024]{1,0:T(8,128)(2,1)}, u32[]{:S(2)}, u32[]{:S(2)}) %collective-permute-start.12) | collective-permute-done | bytes 1048608 | tf_op jit(solution)/shard_map/ppermute | solution.py:655
  189.0 17.7 %all-to-all-done.5.refs_6_ = bf16[4,64,1024]{2,1,0:T(8,128)(2,1)S(1)} async-done(((bf16[4,64,1024]{2,1,0:T(8,128)(2,1)}), bf16[4,64,1024]{2,1,0:T(8,128)(2,1)S(1)}, u32[]{:S(2)}, u32[]{:S(2)}) %all-to-all-start.5) | async-done | bytes 524320 | tf_op jit(solution)/shard_map/all_to_all | solution.py:723
  206.7 7.3 %all-to-all-start.6 = ((bf16[8,32,1024]{2,1,0:T(8,128)(2,1)}), bf16[8,32,1024]{2,1,0:T(8,128)(2,1)}, u32[]{:S(2)}, u32[]{:S(2)}) async-start(bf16[8,32,1024]{2,1,0:T(8,128)(2,1)} %bitcast.83), calls=%async_computation.6 | async-start | bytes 1048576 | tf_op jit(solution)/shard_map/all_to_all | solution.py:776
  215.1 24.0 %attn_bwd.1 = (bf16[4,64,1024]{2,1,0:T(8,128)(2,1)}, bf16[4,64,1024]{2,1,0:T(8,128)(2,1)}, bf16[4,64,1024]{2,1,0:T(8,128)(2,1)}, bf16[4,64,1024]{2,1,0:T(8,128)(2,1)}, bf16[4,64,1024]{2,1,0:T(8,128)(2,1)}) custom-call(s32[1]{0:T(128)} %bitcast.5.meta_ref, s32[4]{0:T(128)S(1)} %copy-done.38, bf16[4,64,1024]{2,1,0:T(8,128)(2,1)S(1)} %copy-done.6, ...), custom_call_target="tpu_custom_call" | custom-call | tf_op jit(solution)/shard_map/attn_bwd/pallas_call | solution.py:216
  239.2 5.2 %all-to-all-start.7 = ((bf16[4,64,1024]{2,1,0:T(8,128)(2,1)}), bf16[4,64,1024]{2,1,0:T(8,128)(2,1)S(1)}, u32[]{:S(2)}, u32[]{:S(2)}) async-start(bf16[4,64,1024]{2,1,0:T(8,128)(2,1)} %get-tuple-element.125.dq_ref), calls=%async_computation.7 | async-start | bytes 1048576 | tf_op jit(solution)/shard_map/all_to_all | solution.py:723
  244.4 11.0 %collective-permute-start.15 = (bf16[4,64,1024]{2,1,0:T(8,128)(2,1)}, bf16[4,64,1024]{2,1,0:T(8,128)(2,1)S(1)}, u32[]{:S(2)}, u32[]{:S(2)}) collective-permute-start(bf16[4,64,1024]{2,1,0:T(8,128)(2,1)} %get-tuple-element.126), channel_id=1, source_target_pairs={{0,4},{4,0},{8,12},{12,8},{16,20},{20,16},{24,28},{28,24},{1,5},{5... | collective-permute-start | bytes 1572872 | tf_op jit(solution)/shard_map/ppermute | solution.py:645
  255.4 10.5 %collective-permute-done.15.other_ref = bf16[4,64,1024]{2,1,0:T(8,128)(2,1)S(1)} collective-permute-done((bf16[4,64,1024]{2,1,0:T(8,128)(2,1)}, bf16[4,64,1024]{2,1,0:T(8,128)(2,1)S(1)}, u32[]{:S(2)}, u32[]{:S(2)}) %collective-permute-start.15) | collective-permute-done | bytes 524320 | tf_op jit(solution)/shard_map/ppermute | solution.py:645
  277.7 9.8 %collective-permute-done.16.other_ref = bf16[4,64,1024]{2,1,0:T(8,128)(2,1)S(1)} collective-permute-done((bf16[4,64,1024]{2,1,0:T(8,128)(2,1)}, bf16[4,64,1024]{2,1,0:T(8,128)(2,1)S(1)}, u32[]{:S(2)}, u32[]{:S(2)}) %collective-permute-start.16) | collective-permute-done | bytes 524320 | tf_op jit(solution)/shard_map/ppermute | solution.py:645
  299.1 7.6 %grad_heads.1 = f32[192,1024]{1,0:T(8,128)S(1)} custom-call(s32[8]{0:T(128)S(1)} %stack.118.spot_ref, bf16[4,64,1024]{2,1,0:T(8,128)(2,1)S(1)} %copy-done.23, bf16[4,64,1024]{2,1,0:T(8,128)(2,1)} %add_low.6.dk_ref, bf16[4,64,1024]{2,1,0:T(8,128)(2,1)} %add_low.7.dv_ref, bf16[1024,1024]{1,0:T(8,128)(2,1)S(1)} %copy-done.14, ...), custom_call_target="tpu_custom_call" | custom-call | tf_op jit(solution)/shard_map/grad_heads/pallas_call | solution.py:503
  338.1 9.4 %collective-permute-done.24.refs_2_ = bf16[256,512]{1,0:T(8,128)(2,1)S(1)} collective-permute-done((bf16[256,512]{1,0:T(8,128)(2,1)S(1)}, bf16[256,512]{1,0:T(8,128)(2,1)S(1)}, u32[]{:S(2)}, u32[]{:S(2)}) %collective-permute-start.24) | collective-permute-done | bytes 262176 | tf_op jit(solution)/shard_map/ppermute | solution.py:640
  347.5 10.6 %collective-permute-done.25.refs_4_ = bf16[256,512]{1,0:T(8,128)(2,1)S(1)} collective-permute-done((bf16[256,512]{1,0:T(8,128)(2,1)S(1)}, bf16[256,512]{1,0:T(8,128)(2,1)S(1)}, u32[]{:S(2)}, u32[]{:S(2)}) %collective-permute-start.25) | collective-permute-done | bytes 262176 | tf_op jit(solution)/shard_map/ppermute | solution.py:640
  367.9 6.0 %collective-permute-done.29 = f32[12,1024]{1,0:T(8,128)S(1)} collective-permute-done((f32[12,1024]{1,0:T(8,128)S(1)}, f32[12,1024]{1,0:T(8,128)S(1)}, u32[]{:S(2)}, u32[]{:S(2)}) %collective-permute-start.29) | collective-permute-done | bytes 49184 | tf_op jit(solution)/shard_map/ppermute | solution.py:849
  374.0 12.0 %collective-permute-start.30 = (f32[12,1024]{1,0:T(8,128)S(1)}, f32[12,1024]{1,0:T(8,128)S(1)}, u32[]{:S(2)}, u32[]{:S(2)}) collective-permute-start(f32[12,1024]{1,0:T(8,128)S(1)} %add.190), channel_id=1, source_target_pairs={{0,8},{4,12},{8,0},{12,4},{16,24},{20,28},{24,16},{28,20},{1,9},{5... | collective-permute-start | bytes 147464 | tf_op jit(solution)/shard_map/ppermute | solution.py:849
  395.2 5.6 %collective-permute-done.35.refs_3_ = bf16[256,512]{1,0:T(8,128)(2,1)S(1)} collective-permute-done((bf16[256,512]{1,0:T(8,128)(2,1)S(1)}, bf16[256,512]{1,0:T(8,128)(2,1)S(1)}, u32[]{:S(2)}, u32[]{:S(2)}) %collective-permute-start.35) | collective-permute-done | bytes 262176 | tf_op jit(solution)/shard_map/ppermute | solution.py:645
  400.8 5.6 %collective-permute-done.36.refs_5_ = bf16[256,512]{1,0:T(8,128)(2,1)S(1)} collective-permute-done((bf16[256,512]{1,0:T(8,128)(2,1)S(1)}, bf16[256,512]{1,0:T(8,128)(2,1)S(1)}, u32[]{:S(2)}, u32[]{:S(2)}) %collective-permute-start.36) | collective-permute-done | bytes 262176 | tf_op jit(solution)/shard_map/ppermute | solution.py:645
  (230 shorter events, 181.0 us)
Async XLA Ops:
  14.5 20.8 %all-to-all-start.1 = ((bf16[4,64,1024]{2,1,0:T(8,128)(2,1)}), bf16[4,64,1024]{2,1,0:T(8,128)(2,1)S(1)}, u32[]{:S(2)}, u32[]{:S(2)}) async-start(bf16[4,64,1024]{2,1,0:T(8,128)(2,1)} %get-tuple-element.88), calls=%async_computation.1 | async-start | bytes 1048576 | tf_op jit(solution)/shard_map/all_to_all | solution.py:723
  20.8 18.0 %collective-permute-start.1 = (bf16[256,1024]{1,0:T(8,128)(2,1)S(1)}, bf16[256,1024]{1,0:T(8,128)(2,1)}, u32[]{:S(2)}, u32[]{:S(2)}) collective-permute-start(bf16[256,1024]{1,0:T(8,128)(2,1)S(1)} %copy-done.21), channel_id=1, source_target_pairs={{0,2},{1,3},{2,0},{3,1},{4,6},{5,7},{6,4},{7,5},{8,10},{9,11},{10,... | collective-permute-start | bytes 1572872 | tf_op jit(solution)/shard_map/ppermute | solution.py:655
  100.1 62.1 %all-gather.6.cloned.1.call-start = ((), (), s32[]{:S(2)}) async-start(), calls=%async_computation.13 | async-start | bytes 2621440 | tf_op jit(solution)/shard_map/all_gather | solution.py:749
  107.1 203.0 %reduce-scatter.2.cloned.1.call-start = ((), (), s32[]{:S(2)}) async-start(), calls=%async_computation.11 | async-start | bytes 4718592 | tf_op jit(solution)/shard_map/reduce_scatter | solution.py:767
  148.1 25.5 %collective-permute-start.12 = (bf16[512,1024]{1,0:T(8,128)(2,1)}, bf16[512,1024]{1,0:T(8,128)(2,1)}, u32[]{:S(2)}, u32[]{:S(2)}) collective-permute-start(bf16[512,1024]{1,0:T(8,128)(2,1)} %add_low.5.own_ref), channel_id=1, source_target_pairs={{0,2},{1,3},{2,0},{3,1},{4,6},{5,7},{6,4},{7,5},{8,10},{9,11},{10,... | collective-permute-start | bytes 3145736 | tf_op jit(solution)/shard_map/ppermute | solution.py:655
  182.9 23.8 %all-to-all-start.5 = ((bf16[4,64,1024]{2,1,0:T(8,128)(2,1)}), bf16[4,64,1024]{2,1,0:T(8,128)(2,1)S(1)}, u32[]{:S(2)}, u32[]{:S(2)}) async-start(bf16[4,64,1024]{2,1,0:T(8,128)(2,1)} %bitcast.84), calls=%async_computation.5 | async-start | bytes 1048576 | tf_op jit(solution)/shard_map/all_to_all | solution.py:723
  187.5 51.7 %collective-permute-start.14 = (bf16[3,256,1024]{2,1,0:T(8,128)(2,1)}, bf16[3,256,1024]{2,1,0:T(8,128)(2,1)}, u32[]{:S(2)}, u32[]{:S(2)}) collective-permute-start(bf16[3,256,1024]{2,1,0:T(8,128)(2,1)} %pad_maximum_fusion.2.refs_0_), channel_id=1, source_target_pairs={{0,2},{1,3},{2,0},{3,1},{4,6},{5,7},{6,4},{7,5},{8,10},{9,11},{10,... | collective-permute-start | bytes 4718600 | tf_op jit(solution)/shard_map/ppermute | solution.py:655
  206.7 32.5 %all-to-all-start.6 = ((bf16[8,32,1024]{2,1,0:T(8,128)(2,1)}), bf16[8,32,1024]{2,1,0:T(8,128)(2,1)}, u32[]{:S(2)}, u32[]{:S(2)}) async-start(bf16[8,32,1024]{2,1,0:T(8,128)(2,1)} %bitcast.83), calls=%async_computation.6 | async-start | bytes 1048576 | tf_op jit(solution)/shard_map/all_to_all | solution.py:776
  239.2 26.8 %all-to-all-start.7 = ((bf16[4,64,1024]{2,1,0:T(8,128)(2,1)}), bf16[4,64,1024]{2,1,0:T(8,128)(2,1)S(1)}, u32[]{:S(2)}, u32[]{:S(2)}) async-start(bf16[4,64,1024]{2,1,0:T(8,128)(2,1)} %get-tuple-element.125.dq_ref), calls=%async_computation.7 | async-start | bytes 1048576 | tf_op jit(solution)/shard_map/all_to_all | solution.py:723
  244.4 21.6 %collective-permute-start.15 = (bf16[4,64,1024]{2,1,0:T(8,128)(2,1)}, bf16[4,64,1024]{2,1,0:T(8,128)(2,1)S(1)}, u32[]{:S(2)}, u32[]{:S(2)}) collective-permute-start(bf16[4,64,1024]{2,1,0:T(8,128)(2,1)} %get-tuple-element.126), channel_id=1, source_target_pairs={{0,4},{4,0},{8,12},{12,8},{16,20},{20,16},{24,28},{28,24},{1,5},{5... | collective-permute-start | bytes 1572872 | tf_op jit(solution)/shard_map/ppermute | solution.py:645
  268.0 20.3 %all-to-all-start.8 = ((bf16[4,64,1024]{2,1,0:T(8,128)(2,1)}), bf16[4,64,1024]{2,1,0:T(8,128)(2,1)S(1)}, u32[]{:S(2)}, u32[]{:S(2)}) async-start(bf16[4,64,1024]{2,1,0:T(8,128)(2,1)} %add_low.6.dk_ref), calls=%async_computation.8 | async-start | bytes 1048576 | tf_op jit(solution)/shard_map/all_to_all | solution.py:723
  272.7 23.6 %collective-permute-start.17 = (bf16[3,256,1024]{2,1,0:T(8,128)(2,1)}, bf16[3,256,1024]{2,1,0:T(8,128)(2,1)}, u32[]{:S(2)}, u32[]{:S(2)}) collective-permute-start(bf16[3,256,1024]{2,1,0:T(8,128)(2,1)} %pad_maximum_fusion.2.refs_0_), channel_id=1, source_target_pairs={{0,1},{1,0},{2,3},{3,2},{4,5},{5,4},{6,7},{7,6},{8,9},{9,8},{10,11... | collective-permute-start | bytes 4718600 | tf_op jit(solution)/shard_map/ppermute | solution.py:651
  272.9 23.4 %collective-permute-start.18 = (bf16[3,256,1024]{2,1,0:T(8,128)(2,1)}, bf16[3,256,1024]{2,1,0:T(8,128)(2,1)}, u32[]{:S(2)}, u32[]{:S(2)}) collective-permute-start(bf16[3,256,1024]{2,1,0:T(8,128)(2,1)} %collective-permute-done.14.refs_1_), channel_id=1, source_target_pairs={{0,1},{1,0},{2,3},{3,2},{4,5},{5,4},{6,7},{7,6},{8,9},{9,8},{10,11... | collective-permute-start | bytes 4718600 | tf_op jit(solution)/shard_map/ppermute | solution.py:651
  276.2 34.0 %collective-permute-start.20 = (bf16[512,1024]{1,0:T(8,128)(2,1)}, bf16[512,1024]{1,0:T(8,128)(2,1)}, u32[]{:S(2)}, u32[]{:S(2)}) collective-permute-start(bf16[512,1024]{1,0:T(8,128)(2,1)} %add_low.8), channel_id=1, source_target_pairs={{0,2},{1,3},{2,0},{3,1},{4,6},{5,7},{6,4},{7,5},{8,10},{9,11},{10,... | collective-permute-start | bytes 3145736 | tf_op jit(solution)/shard_map/ppermute | solution.py:655
  291.3 18.8 %all-to-all-start.9 = ((bf16[4,64,1024]{2,1,0:T(8,128)(2,1)}), bf16[4,64,1024]{2,1,0:T(8,128)(2,1)S(1)}, u32[]{:S(2)}, u32[]{:S(2)}) async-start(bf16[4,64,1024]{2,1,0:T(8,128)(2,1)} %add_low.7.dv_ref), calls=%async_computation.9 | async-start | bytes 1048576 | tf_op jit(solution)/shard_map/all_to_all | solution.py:723
  296.2 119.6 %all-gather.4.cloned.1.call-start = ((), (), s32[]{:S(2)}) async-start(), calls=%async_computation.12 | async-start | bytes 4718592 | tf_op jit(solution)/shard_map/all_gather | solution.py:813
  323.0 35.1 %collective-permute-start.22 = (bf16[512,1024]{1,0:T(8,128)(2,1)S(1)}, bf16[512,1024]{1,0:T(8,128)(2,1)S(1)}, u32[]{:S(2)}, u32[]{:S(2)}) collective-permute-start(bf16[512,1024]{1,0:T(8,128)(2,1)S(1)} %add_low.9.own_ref), channel_id=1, source_target_pairs={{0,2},{1,3},{2,0},{3,1},{4,6},{5,7},{6,4},{7,5},{8,10},{9,11},{10,... | collective-permute-start | bytes 3145736 | tf_op jit(solution)/shard_map/ppermute | solution.py:655
  331.3 26.8 %collective-permute-start.25 = (bf16[256,512]{1,0:T(8,128)(2,1)S(1)}, bf16[256,512]{1,0:T(8,128)(2,1)S(1)}, u32[]{:S(2)}, u32[]{:S(2)}) collective-permute-start(bf16[256,512]{1,0:T(8,128)(2,1)S(1)} %pad_maximum_fusion.4.refs_0_), channel_id=1, source_target_pairs={{0,16},{4,20},{8,24},{12,28},{16,0},{20,4},{24,8},{28,12},{1,17},{... | collective-permute-start | bytes 786440 | tf_op jit(solution)/shard_map/ppermute | solution.py:640
  334.4 23.7 %collective-permute-start.26 = (bf16[256,512]{1,0:T(8,128)(2,1)S(1)}, bf16[256,512]{1,0:T(8,128)(2,1)}, u32[]{:S(2)}, u32[]{:S(2)}) collective-permute-start(bf16[256,512]{1,0:T(8,128)(2,1)S(1)} %pad_maximum_fusion.4.refs_0_), channel_id=1, source_target_pairs={{0,24},{4,28},{8,0},{12,4},{16,8},{20,12},{24,16},{28,20},{1,25},{... | collective-permute-start | bytes 786440 | tf_op jit(solution)/shard_map/ppermute | solution.py:640
  337.9 50.1 %collective-permute-start.32 = (bf16[512,1024]{1,0:T(8,128)(2,1)S(1)}, bf16[512,1024]{1,0:T(8,128)(2,1)S(1)}, u32[]{:S(2)}, u32[]{:S(2)}) collective-permute-start(bf16[512,1024]{1,0:T(8,128)(2,1)S(1)} %add_convert_fusion.own_ref), channel_id=1, source_target_pairs={{0,1},{1,0},{2,3},{3,2},{4,5},{5,4},{6,7},{7,6},{8,9},{9,8},{10,11... | collective-permute-start | bytes 3145736 | tf_op jit(solution)/shard_map/ppermute | solution.py:651
  362.4 30.0 %collective-permute-start.31 = (bf16[512,1024]{1,0:T(8,128)(2,1)S(1)}, bf16[512,1024]{1,0:T(8,128)(2,1)S(1)}, u32[]{:S(2)}, u32[]{:S(2)}) collective-permute-start(bf16[512,1024]{1,0:T(8,128)(2,1)S(1)} %get-tuple-element.149.own_ref), channel_id=1, source_target_pairs={{0,1},{1,0},{2,3},{3,2},{4,5},{5,4},{6,7},{7,6},{8,9},{9,8},{10,11... | collective-permute-start | bytes 3145736 | tf_op jit(solution)/shard_map/ppermute | solution.py:651
  388.0 18.4 %collective-permute-start.36 = (bf16[256,512]{1,0:T(8,128)(2,1)S(1)}, bf16[256,512]{1,0:T(8,128)(2,1)S(1)}, u32[]{:S(2)}, u32[]{:S(2)}) collective-permute-start(bf16[256,512]{1,0:T(8,128)(2,1)S(1)} %collective-permute-done.25.refs_4_), channel_id=1, source_target_pairs={{0,4},{4,0},{8,12},{12,8},{16,20},{20,16},{24,28},{28,24},{1,5},{5... | collective-permute-start | bytes 786440 | tf_op jit(solution)/shard_map/ppermute | solution.py:645
  391.0 19.4 %collective-permute-start.37 = (bf16[256,512]{1,0:T(8,128)(2,1)}, bf16[256,512]{1,0:T(8,128)(2,1)S(1)}, u32[]{:S(2)}, u32[]{:S(2)}) collective-permute-start(bf16[256,512]{1,0:T(8,128)(2,1)} %collective-permute-done.26.refs_6_), channel_id=1, source_target_pairs={{0,4},{4,0},{8,12},{12,8},{16,20},{20,16},{24,28},{28,24},{1,5},{5... | collective-permute-start | bytes 786440 | tf_op jit(solution)/shard_map/ppermute | solution.py:645
  393.9 20.0 %collective-permute-start.33 = (f32[12,1024]{1,0:T(8,128)S(1)}, f32[12,1024]{1,0:T(8,128)S(1)}, u32[]{:S(2)}, u32[]{:S(2)}) collective-permute-start(f32[12,1024]{1,0:T(8,128)S(1)} %add.191), channel_id=1, source_target_pairs={{0,16},{4,20},{8,24},{12,28},{16,0},{20,4},{24,8},{28,12},{1,17},{... | collective-permute-start | bytes 147464 | tf_op jit(solution)/shard_map/ppermute | solution.py:849
  (68 other events, 685.3 us)
Sparse Core Ops, SparseCore 0:
  107.2 54.9 all-gather.5
Sparse Core Ops, SparseCore 1:
  142.7 102.7 reduce-scatter.1
  310.2 92.7 all-gather.3

commit v6 on v5

--- a/solution.py
+++ b/solution.py
@@ -194,11 +194,11 @@
     return pl.pallas_call(
         functools.partial(fwd_kernel, bq, bk, S, part),
         out_shape=(
-            jax.ShapeDtypeStruct((J, HEAD_DIM, T // 2), LOW),
+            pltpu.HBM((J, HEAD_DIM, T // 2), LOW),
             jax.ShapeDtypeStruct((J, 1, T // 2), F32),
         ),
         in_specs=[M, M] + [V] * (1 + 2 * S),
-        out_specs=(V, V),
+        out_specs=(pl.BlockSpec(), V),
         scratch_shapes=[
             pltpu.VMEM((S * J, T, HEAD_DIM), LOW),
             pltpu.VMEM((S * J, HEAD_DIM, T), LOW),
@@ -417,12 +417,12 @@
 def first_stage(core, q, k, v, w):
     local, T = q.shape
     D = w.shape[1]
-    part = jax.ShapeDtypeStruct((T // 2, D), LOW)
+    part = pltpu.HBM((T // 2, D), LOW)
     return pl.pallas_call(
         first_kernel,
         out_shape=(part, part),
         in_specs=[M, V, V, V, V],
-        out_specs=(V, V),
+        out_specs=(pl.BlockSpec(), pl.BlockSpec()),
         compiler_params=pltpu.CompilerParams(vmem_limit_bytes=10 * MIB),
         cost_estimate=cost(10**6, 1000),
         name="first_grad",

time: 433 us -> 432 us (level)
  no operation moved by 1% of the time
where the time goes in v6:
time: 432 us; the launch traced here: 430 us
  waiting for transfers between devices  157 us (36%)
  Pallas kernels  116 us (27%)
  starting transfers between devices  99.1 us (23%)
  local copies, waits for them, and re-layouts  30.4 us (7%)
  between operations  16 us (4%)
  other arithmetic  11.5 us (3%)
    all_to_all x9, waiting for transfers between devices, exchange(): lax.all_to_all(heads, 'dp', 0, 0, tiled=True, axis_index_groups=groups)  55.6 us
    all_to_all x9, starting transfers between devices, exchange(): lax.all_to_all(heads, 'dp', 0, 0, tiled=True, axis_index_groups=groups)  41.5 us
    ppermute x9, waiting for transfers between devices, shift_group(): lax.ppermute(value, 'dp', [(i, i // S * S + (i % S + steps) % S) for i in...  40.5 us
    pallas_call x1, Pallas kernels, attn_bwd(): pl.pallas_call(functools.partial(bwd_kernel, bq, bk, S), out_shape=[block...  24 us
    pallas_call x2, Pallas kernels, attn_fwd(): pl.pallas_call(functools.partial(fwd_kernel, bq, bk, S, part), out_shape=...  21.1 us
    ppermute x9, starting transfers between devices, shift_group(): lax.ppermute(value, 'dp', [(i, i // S * S + (i % S + steps) % S) for i in...  20.2 us
    ppermute x3, waiting for transfers between devices, shift_dp(): lax.ppermute(value, 'dp', [(i, (i + steps) % count) for i in range(count)])  19.9 us
    unnamed x85, local copies, waits for them, and re-layouts  19.7 us
  transfers between devices with their start and end apart: 51, of which 26 were waited for; matrix products, arithmetic and copies ran while one was open for 5% of the time, Pallas kernels for 22%

profile of v6, /device:TPU:0, one launch (start us, length us, event | category | flops | bytes accessed | tf_op | source)
XLA Modules:
  0.0 430.1 jit_solution(17129828939059263205)
XLA Ops:
  8.0 6.5 %norm_qkv.1 = (bf16[1024,1024]{1,0:T(8,128)(2,1)}, bf16[4,64,1024]{2,1,0:T(8,128)(2,1)}, bf16[4,64,1024]{2,1,0:T(8,128)(2,1)}, bf16[4,64,1024]{2,1,0:T(8,128)(2,1)}) custom-call(bf16[1024,1024]{1,0:T(8,128)(2,1)} %x_ref.3, f32[1,1024]{1,0:T(1,128)} %bitcast.80, f32[1,1024]{1,0:T(1,128)} %bitcast.87, bf16[3,1024,256]{2,1,0:T(8,128)(2,1)} %w_ref.7, f32[2,256]{1,0:T(2,128)} %b_ref.1), custom_call_target="tpu_custom_call" | custom-call | tf_op jit(solution)/shard_map/norm_qkv/pallas_call | solution.py:258
  14.5 6.3 %all-to-all-start.1 = ((bf16[4,64,1024]{2,1,0:T(8,128)(2,1)}), bf16[4,64,1024]{2,1,0:T(8,128)(2,1)S(1)}, u32[]{:S(2)}, u32[]{:S(2)}) async-start(bf16[4,64,1024]{2,1,0:T(8,128)(2,1)} %get-tuple-element.88), calls=%async_computation.1 | async-start | bytes 1048576 | tf_op jit(solution)/shard_map/all_to_all | solution.py:723
  22.3 13.0 %all-to-all-done.1.refs_0_ = bf16[4,64,1024]{2,1,0:T(8,128)(2,1)S(1)} async-done(((bf16[4,64,1024]{2,1,0:T(8,128)(2,1)}), bf16[4,64,1024]{2,1,0:T(8,128)(2,1)S(1)}, u32[]{:S(2)}, u32[]{:S(2)}) %all-to-all-start.1) | async-done | bytes 524320 | tf_op jit(solution)/shard_map/all_to_all | solution.py:723
  40.9 11.9 %all-to-all-done.2.refs_2_ = bf16[4,64,1024]{2,1,0:T(8,128)(2,1)S(1)} async-done(((bf16[4,64,1024]{2,1,0:T(8,128)(2,1)}), bf16[4,64,1024]{2,1,0:T(8,128)(2,1)S(1)}, u32[]{:S(2)}, u32[]{:S(2)}) %all-to-all-start.2) | async-done | bytes 524320 | tf_op jit(solution)/shard_map/all_to_all | solution.py:723
  61.2 9.0 %all-to-all-done.q_ref = bf16[4,64,1024]{2,1,0:T(8,128)(2,1)S(1)} async-done(((bf16[4,64,1024]{2,1,0:T(8,128)(2,1)}), bf16[4,64,1024]{2,1,0:T(8,128)(2,1)S(1)}, u32[]{:S(2)}, u32[]{:S(2)}) %all-to-all-start) | async-done | bytes 524320 | tf_op jit(solution)/shard_map/all_to_all | solution.py:723
  70.2 9.2 %attn_fwd.2 = (bf16[4,64,512]{2,1,0:T(8,128)(2,1)}, f32[4,1,512]{2,1,0:T(1,128)S(1)}) custom-call(s32[1]{0:T(128)} %bitcast.5.meta_ref, s32[4]{0:T(128)S(1)} %copy-done.37, bf16[4,64,1024]{2,1,0:T(8,128)(2,1)S(1)} %all-to-all-done.q_ref, bf16[4,64,1024]{2,1,0:T(8,128)(2,1)S(1)} %all-to-all-done.1.refs_0_, ...), custom_call_target="tpu_custom_call" | custom-call | tf_op jit(solution)/shard_map/attn_fwd/pallas_call | solution.py:194
  83.1 11.9 %attn_fwd.3 = (bf16[4,64,512]{2,1,0:T(8,128)(2,1)}, f32[4,1,512]{2,1,0:T(1,128)S(1)}) custom-call(s32[1]{0:T(128)} %bitcast.5.meta_ref, s32[4]{0:T(128)S(1)} %copy-done.37, bf16[4,64,1024]{2,1,0:T(8,128)(2,1)S(1)} %all-to-all-done.q_ref, bf16[4,64,1024]{2,1,0:T(8,128)(2,1)S(1)} %all-to-all-done.1.refs_0_, ...), custom_call_target="tpu_custom_call" | custom-call | tf_op jit(solution)/shard_map/attn_fwd/pallas_call | solution.py:194
  117.2 7.5 %out_norm.1 = (f32[1024,1024]{1,0:T(8,128)}, bf16[1024,1024]{1,0:T(8,128)(2,1)S(1)}) custom-call(s32[4]{0:T(128)S(1)} %pad_add_fusion.pos_ref, bf16[256,512]{1,0:T(8,128)(2,1)S(1)} %bitcast.68, bf16[256,512]{1,0:T(8,128)(2,1)S(1)} %collective-permute-done.5.refs_1_, bf16[256,512]{1,0:T(8,128)(2,1)S(1)} %copy-done.33, ...), custom_call_target="tpu_custom_call" | custom-call | tf_op jit(solution)/shard_map/out_norm/pallas_call | solution.py:294
  134.3 7.0 %feed_grads.1 = bf16[2048,1024]{1,0:T(8,128)(2,1)} custom-call(bf16[1024,1024]{1,0:T(8,128)(2,1)S(1)} %get-tuple-element.106.g_ref, bf16[1024,1024]{1,0:T(8,128)(2,1)S(1)} %copy-done, bf16[1024,1024]{1,0:T(8,128)(2,1)S(1)} %get-tuple-element.101.n2_ref, bf16[1024,1024]{1,0:T(8,128)(2,1)S(1)} %get-tuple-element.107.dh_ref), custom_call_target="tpu_custom_call" | custom-call | tf_op jit(solution)/shard_map/feed_grads/pallas_call | solution.py:451
  165.0 8.6 %collective-permute-done.12.crossed_ref = bf16[512,1024]{1,0:T(8,128)(2,1)} collective-permute-done((bf16[512,1024]{1,0:T(8,128)(2,1)}, bf16[512,1024]{1,0:T(8,128)(2,1)}, u32[]{:S(2)}, u32[]{:S(2)}) %collective-permute-start.12) | collective-permute-done | bytes 1048608 | tf_op jit(solution)/shard_map/ppermute | solution.py:655
  189.0 17.7 %all-to-all-done.5.refs_6_ = bf16[4,64,1024]{2,1,0:T(8,128)(2,1)S(1)} async-done(((bf16[4,64,1024]{2,1,0:T(8,128)(2,1)}), bf16[4,64,1024]{2,1,0:T(8,128)(2,1)S(1)}, u32[]{:S(2)}, u32[]{:S(2)}) %all-to-all-start.5) | async-done | bytes 524320 | tf_op jit(solution)/shard_map/all_to_all | solution.py:723
  206.7 7.3 %all-to-all-start.6 = ((bf16[8,32,1024]{2,1,0:T(8,128)(2,1)}), bf16[8,32,1024]{2,1,0:T(8,128)(2,1)}, u32[]{:S(2)}, u32[]{:S(2)}) async-start(bf16[8,32,1024]{2,1,0:T(8,128)(2,1)} %bitcast.83), calls=%async_computation.6 | async-start | bytes 1048576 | tf_op jit(solution)/shard_map/all_to_all | solution.py:776
  215.1 24.0 %attn_bwd.1 = (bf16[4,64,1024]{2,1,0:T(8,128)(2,1)}, bf16[4,64,1024]{2,1,0:T(8,128)(2,1)}, bf16[4,64,1024]{2,1,0:T(8,128)(2,1)}, bf16[4,64,1024]{2,1,0:T(8,128)(2,1)}, bf16[4,64,1024]{2,1,0:T(8,128)(2,1)}) custom-call(s32[1]{0:T(128)} %bitcast.5.meta_ref, s32[4]{0:T(128)S(1)} %copy-done.37, bf16[4,64,1024]{2,1,0:T(8,128)(2,1)S(1)} %copy-done.6, ...), custom_call_target="tpu_custom_call" | custom-call | tf_op jit(solution)/shard_map/attn_bwd/pallas_call | solution.py:216
  239.1 5.2 %all-to-all-start.7 = ((bf16[4,64,1024]{2,1,0:T(8,128)(2,1)}), bf16[4,64,1024]{2,1,0:T(8,128)(2,1)S(1)}, u32[]{:S(2)}, u32[]{:S(2)}) async-start(bf16[4,64,1024]{2,1,0:T(8,128)(2,1)} %get-tuple-element.125.dq_ref), calls=%async_computation.7 | async-start | bytes 1048576 | tf_op jit(solution)/shard_map/all_to_all | solution.py:723
  244.3 11.0 %collective-permute-start.15 = (bf16[4,64,1024]{2,1,0:T(8,128)(2,1)}, bf16[4,64,1024]{2,1,0:T(8,128)(2,1)S(1)}, u32[]{:S(2)}, u32[]{:S(2)}) collective-permute-start(bf16[4,64,1024]{2,1,0:T(8,128)(2,1)} %get-tuple-element.126), channel_id=1, source_target_pairs={{0,4},{4,0},{8,12},{12,8},{16,20},{20,16},{24,28},{28,24},{1,5},{5... | collective-permute-start | bytes 1572872 | tf_op jit(solution)/shard_map/ppermute | solution.py:645
  255.4 10.5 %collective-permute-done.15.other_ref = bf16[4,64,1024]{2,1,0:T(8,128)(2,1)S(1)} collective-permute-done((bf16[4,64,1024]{2,1,0:T(8,128)(2,1)}, bf16[4,64,1024]{2,1,0:T(8,128)(2,1)S(1)}, u32[]{:S(2)}, u32[]{:S(2)}) %collective-permute-start.15) | collective-permute-done | bytes 524320 | tf_op jit(solution)/shard_map/ppermute | solution.py:645
  277.6 9.8 %collective-permute-done.16.other_ref = bf16[4,64,1024]{2,1,0:T(8,128)(2,1)S(1)} collective-permute-done((bf16[4,64,1024]{2,1,0:T(8,128)(2,1)}, bf16[4,64,1024]{2,1,0:T(8,128)(2,1)S(1)}, u32[]{:S(2)}, u32[]{:S(2)}) %collective-permute-start.16) | collective-permute-done | bytes 524320 | tf_op jit(solution)/shard_map/ppermute | solution.py:645
  299.0 7.6 %grad_heads.1 = f32[192,1024]{1,0:T(8,128)S(1)} custom-call(s32[8]{0:T(128)S(1)} %stack.118.spot_ref, bf16[4,64,1024]{2,1,0:T(8,128)(2,1)S(1)} %copy-done.23, bf16[4,64,1024]{2,1,0:T(8,128)(2,1)} %add_low.6.dk_ref, bf16[4,64,1024]{2,1,0:T(8,128)(2,1)} %add_low.7.dv_ref, bf16[1024,1024]{1,0:T(8,128)(2,1)S(1)} %copy-done.14, ...), custom_call_target="tpu_custom_call" | custom-call | tf_op jit(solution)/shard_map/grad_heads/pallas_call | solution.py:503
  338.1 9.4 %collective-permute-done.24.refs_2_ = bf16[256,512]{1,0:T(8,128)(2,1)S(1)} collective-permute-done((bf16[256,512]{1,0:T(8,128)(2,1)S(1)}, bf16[256,512]{1,0:T(8,128)(2,1)S(1)}, u32[]{:S(2)}, u32[]{:S(2)}) %collective-permute-start.24) | collective-permute-done | bytes 262176 | tf_op jit(solution)/shard_map/ppermute | solution.py:640
  347.5 10.5 %collective-permute-done.25.refs_4_ = bf16[256,512]{1,0:T(8,128)(2,1)S(1)} collective-permute-done((bf16[256,512]{1,0:T(8,128)(2,1)S(1)}, bf16[256,512]{1,0:T(8,128)(2,1)S(1)}, u32[]{:S(2)}, u32[]{:S(2)}) %collective-permute-start.25) | collective-permute-done | bytes 262176 | tf_op jit(solution)/shard_map/ppermute | solution.py:640
  367.7 6.1 %collective-permute-done.29 = f32[12,1024]{1,0:T(8,128)S(1)} collective-permute-done((f32[12,1024]{1,0:T(8,128)S(1)}, f32[12,1024]{1,0:T(8,128)S(1)}, u32[]{:S(2)}, u32[]{:S(2)}) %collective-permute-start.29) | collective-permute-done | bytes 49184 | tf_op jit(solution)/shard_map/ppermute | solution.py:849
  373.8 12.0 %collective-permute-start.30 = (f32[12,1024]{1,0:T(8,128)S(1)}, f32[12,1024]{1,0:T(8,128)S(1)}, u32[]{:S(2)}, u32[]{:S(2)}) collective-permute-start(f32[12,1024]{1,0:T(8,128)S(1)} %add.190), channel_id=1, source_target_pairs={{0,8},{4,12},{8,0},{12,4},{16,24},{20,28},{24,16},{28,20},{1,9},{5... | collective-permute-start | bytes 147464 | tf_op jit(solution)/shard_map/ppermute | solution.py:849
  395.0 5.6 %collective-permute-done.35.refs_3_ = bf16[256,512]{1,0:T(8,128)(2,1)S(1)} collective-permute-done((bf16[256,512]{1,0:T(8,128)(2,1)S(1)}, bf16[256,512]{1,0:T(8,128)(2,1)S(1)}, u32[]{:S(2)}, u32[]{:S(2)}) %collective-permute-start.35) | collective-permute-done | bytes 262176 | tf_op jit(solution)/shard_map/ppermute | solution.py:645
  400.6 5.6 %collective-permute-done.36.refs_5_ = bf16[256,512]{1,0:T(8,128)(2,1)S(1)} collective-permute-done((bf16[256,512]{1,0:T(8,128)(2,1)S(1)}, bf16[256,512]{1,0:T(8,128)(2,1)S(1)}, u32[]{:S(2)}, u32[]{:S(2)}) %collective-permute-start.36) | collective-permute-done | bytes 262176 | tf_op jit(solution)/shard_map/ppermute | solution.py:645
  (230 shorter events, 180.9 us)
Async XLA Ops:
  14.5 20.8 %all-to-all-start.1 = ((bf16[4,64,1024]{2,1,0:T(8,128)(2,1)}), bf16[4,64,1024]{2,1,0:T(8,128)(2,1)S(1)}, u32[]{:S(2)}, u32[]{:S(2)}) async-start(bf16[4,64,1024]{2,1,0:T(8,128)(2,1)} %get-tuple-element.88), calls=%async_computation.1 | async-start | bytes 1048576 | tf_op jit(solution)/shard_map/all_to_all | solution.py:723
  20.8 18.0 %collective-permute-start.1 = (bf16[256,1024]{1,0:T(8,128)(2,1)S(1)}, bf16[256,1024]{1,0:T(8,128)(2,1)}, u32[]{:S(2)}, u32[]{:S(2)}) collective-permute-start(bf16[256,1024]{1,0:T(8,128)(2,1)S(1)} %copy-done.21), channel_id=1, source_target_pairs={{0,2},{1,3},{2,0},{3,1},{4,6},{5,7},{6,4},{7,5},{8,10},{9,11},{10,... | collective-permute-start | bytes 1572872 | tf_op jit(solution)/shard_map/ppermute | solution.py:655
  100.1 62.1 %all-gather.6.cloned.1.call-start = ((), (), s32[]{:S(2)}) async-start(), calls=%async_computation.13 | async-start | bytes 2621440 | tf_op jit(solution)/shard_map/all_gather | solution.py:749
  107.1 203.0 %reduce-scatter.2.cloned.1.call-start = ((), (), s32[]{:S(2)}) async-start(), calls=%async_computation.11 | async-start | bytes 4718592 | tf_op jit(solution)/shard_map/reduce_scatter | solution.py:767
  148.1 25.5 %collective-permute-start.12 = (bf16[512,1024]{1,0:T(8,128)(2,1)}, bf16[512,1024]{1,0:T(8,128)(2,1)}, u32[]{:S(2)}, u32[]{:S(2)}) collective-permute-start(bf16[512,1024]{1,0:T(8,128)(2,1)} %add_low.5.own_ref), channel_id=1, source_target_pairs={{0,2},{1,3},{2,0},{3,1},{4,6},{5,7},{6,4},{7,5},{8,10},{9,11},{10,... | collective-permute-start | bytes 3145736 | tf_op jit(solution)/shard_map/ppermute | solution.py:655
  182.9 23.8 %all-to-all-start.5 = ((bf16[4,64,1024]{2,1,0:T(8,128)(2,1)}), bf16[4,64,1024]{2,1,0:T(8,128)(2,1)S(1)}, u32[]{:S(2)}, u32[]{:S(2)}) async-start(bf16[4,64,1024]{2,1,0:T(8,128)(2,1)} %bitcast.84), calls=%async_computation.5 | async-start | bytes 1048576 | tf_op jit(solution)/shard_map/all_to_all | solution.py:723
  187.5 51.6 %collective-permute-start.14 = (bf16[3,256,1024]{2,1,0:T(8,128)(2,1)}, bf16[3,256,1024]{2,1,0:T(8,128)(2,1)}, u32[]{:S(2)}, u32[]{:S(2)}) collective-permute-start(bf16[3,256,1024]{2,1,0:T(8,128)(2,1)} %pad_maximum_fusion.2.refs_0_), channel_id=1, source_target_pairs={{0,2},{1,3},{2,0},{3,1},{4,6},{5,7},{6,4},{7,5},{8,10},{9,11},{10,... | collective-permute-start | bytes 4718600 | tf_op jit(solution)/shard_map/ppermute | solution.py:655
  206.7 32.4 %all-to-all-start.6 = ((bf16[8,32,1024]{2,1,0:T(8,128)(2,1)}), bf16[8,32,1024]{2,1,0:T(8,128)(2,1)}, u32[]{:S(2)}, u32[]{:S(2)}) async-start(bf16[8,32,1024]{2,1,0:T(8,128)(2,1)} %bitcast.83), calls=%async_computation.6 | async-start | bytes 1048576 | tf_op jit(solution)/shard_map/all_to_all | solution.py:776
  239.1 26.8 %all-to-all-start.7 = ((bf16[4,64,1024]{2,1,0:T(8,128)(2,1)}), bf16[4,64,1024]{2,1,0:T(8,128)(2,1)S(1)}, u32[]{:S(2)}, u32[]{:S(2)}) async-start(bf16[4,64,1024]{2,1,0:T(8,128)(2,1)} %get-tuple-element.125.dq_ref), calls=%async_computation.7 | async-start | bytes 1048576 | tf_op jit(solution)/shard_map/all_to_all | solution.py:723
  244.3 21.6 %collective-permute-start.15 = (bf16[4,64,1024]{2,1,0:T(8,128)(2,1)}, bf16[4,64,1024]{2,1,0:T(8,128)(2,1)S(1)}, u32[]{:S(2)}, u32[]{:S(2)}) collective-permute-start(bf16[4,64,1024]{2,1,0:T(8,128)(2,1)} %get-tuple-element.126), channel_id=1, source_target_pairs={{0,4},{4,0},{8,12},{12,8},{16,20},{20,16},{24,28},{28,24},{1,5},{5... | collective-permute-start | bytes 1572872 | tf_op jit(solution)/shard_map/ppermute | solution.py:645
  267.9 20.3 %all-to-all-start.8 = ((bf16[4,64,1024]{2,1,0:T(8,128)(2,1)}), bf16[4,64,1024]{2,1,0:T(8,128)(2,1)S(1)}, u32[]{:S(2)}, u32[]{:S(2)}) async-start(bf16[4,64,1024]{2,1,0:T(8,128)(2,1)} %add_low.6.dk_ref), calls=%async_computation.8 | async-start | bytes 1048576 | tf_op jit(solution)/shard_map/all_to_all | solution.py:723
  272.6 23.6 %collective-permute-start.17 = (bf16[3,256,1024]{2,1,0:T(8,128)(2,1)}, bf16[3,256,1024]{2,1,0:T(8,128)(2,1)}, u32[]{:S(2)}, u32[]{:S(2)}) collective-permute-start(bf16[3,256,1024]{2,1,0:T(8,128)(2,1)} %pad_maximum_fusion.2.refs_0_), channel_id=1, source_target_pairs={{0,1},{1,0},{2,3},{3,2},{4,5},{5,4},{6,7},{7,6},{8,9},{9,8},{10,11... | collective-permute-start | bytes 4718600 | tf_op jit(solution)/shard_map/ppermute | solution.py:651
  272.9 23.4 %collective-permute-start.18 = (bf16[3,256,1024]{2,1,0:T(8,128)(2,1)}, bf16[3,256,1024]{2,1,0:T(8,128)(2,1)}, u32[]{:S(2)}, u32[]{:S(2)}) collective-permute-start(bf16[3,256,1024]{2,1,0:T(8,128)(2,1)} %collective-permute-done.14.refs_1_), channel_id=1, source_target_pairs={{0,1},{1,0},{2,3},{3,2},{4,5},{5,4},{6,7},{7,6},{8,9},{9,8},{10,11... | collective-permute-start | bytes 4718600 | tf_op jit(solution)/shard_map/ppermute | solution.py:651
  276.1 34.0 %collective-permute-start.20 = (bf16[512,1024]{1,0:T(8,128)(2,1)}, bf16[512,1024]{1,0:T(8,128)(2,1)}, u32[]{:S(2)}, u32[]{:S(2)}) collective-permute-start(bf16[512,1024]{1,0:T(8,128)(2,1)} %add_low.8), channel_id=1, source_target_pairs={{0,2},{1,3},{2,0},{3,1},{4,6},{5,7},{6,4},{7,5},{8,10},{9,11},{10,... | collective-permute-start | bytes 3145736 | tf_op jit(solution)/shard_map/ppermute | solution.py:655
  291.3 18.8 %all-to-all-start.9 = ((bf16[4,64,1024]{2,1,0:T(8,128)(2,1)}), bf16[4,64,1024]{2,1,0:T(8,128)(2,1)S(1)}, u32[]{:S(2)}, u32[]{:S(2)}) async-start(bf16[4,64,1024]{2,1,0:T(8,128)(2,1)} %add_low.7.dv_ref), calls=%async_computation.9 | async-start | bytes 1048576 | tf_op jit(solution)/shard_map/all_to_all | solution.py:723
  296.1 119.5 %all-gather.4.cloned.1.call-start = ((), (), s32[]{:S(2)}) async-start(), calls=%async_computation.12 | async-start | bytes 4718592 | tf_op jit(solution)/shard_map/all_gather | solution.py:813
  322.8 35.2 %collective-permute-start.22 = (bf16[512,1024]{1,0:T(8,128)(2,1)S(1)}, bf16[512,1024]{1,0:T(8,128)(2,1)S(1)}, u32[]{:S(2)}, u32[]{:S(2)}) collective-permute-start(bf16[512,1024]{1,0:T(8,128)(2,1)S(1)} %add_low.9.own_ref), channel_id=1, source_target_pairs={{0,2},{1,3},{2,0},{3,1},{4,6},{5,7},{6,4},{7,5},{8,10},{9,11},{10,... | collective-permute-start | bytes 3145736 | tf_op jit(solution)/shard_map/ppermute | solution.py:655
  331.2 26.7 %collective-permute-start.25 = (bf16[256,512]{1,0:T(8,128)(2,1)S(1)}, bf16[256,512]{1,0:T(8,128)(2,1)S(1)}, u32[]{:S(2)}, u32[]{:S(2)}) collective-permute-start(bf16[256,512]{1,0:T(8,128)(2,1)S(1)} %pad_maximum_fusion.4.refs_0_), channel_id=1, source_target_pairs={{0,16},{4,20},{8,24},{12,28},{16,0},{20,4},{24,8},{28,12},{1,17},{... | collective-permute-start | bytes 786440 | tf_op jit(solution)/shard_map/ppermute | solution.py:640
  334.2 23.8 %collective-permute-start.26 = (bf16[256,512]{1,0:T(8,128)(2,1)S(1)}, bf16[256,512]{1,0:T(8,128)(2,1)}, u32[]{:S(2)}, u32[]{:S(2)}) collective-permute-start(bf16[256,512]{1,0:T(8,128)(2,1)S(1)} %pad_maximum_fusion.4.refs_0_), channel_id=1, source_target_pairs={{0,24},{4,28},{8,0},{12,4},{16,8},{20,12},{24,16},{28,20},{1,25},{... | collective-permute-start | bytes 786440 | tf_op jit(solution)/shard_map/ppermute | solution.py:640
  337.8 49.9 %collective-permute-start.32 = (bf16[512,1024]{1,0:T(8,128)(2,1)S(1)}, bf16[512,1024]{1,0:T(8,128)(2,1)S(1)}, u32[]{:S(2)}, u32[]{:S(2)}) collective-permute-start(bf16[512,1024]{1,0:T(8,128)(2,1)S(1)} %add_convert_fusion.own_ref), channel_id=1, source_target_pairs={{0,1},{1,0},{2,3},{3,2},{4,5},{5,4},{6,7},{7,6},{8,9},{9,8},{10,11... | collective-permute-start | bytes 3145736 | tf_op jit(solution)/shard_map/ppermute | solution.py:651
  362.2 30.3 %collective-permute-start.31 = (bf16[512,1024]{1,0:T(8,128)(2,1)S(1)}, bf16[512,1024]{1,0:T(8,128)(2,1)S(1)}, u32[]{:S(2)}, u32[]{:S(2)}) collective-permute-start(bf16[512,1024]{1,0:T(8,128)(2,1)S(1)} %get-tuple-element.149.own_ref), channel_id=1, source_target_pairs={{0,1},{1,0},{2,3},{3,2},{4,5},{5,4},{6,7},{7,6},{8,9},{9,8},{10,11... | collective-permute-start | bytes 3145736 | tf_op jit(solution)/shard_map/ppermute | solution.py:651
  387.8 18.4 %collective-permute-start.36 = (bf16[256,512]{1,0:T(8,128)(2,1)S(1)}, bf16[256,512]{1,0:T(8,128)(2,1)S(1)}, u32[]{:S(2)}, u32[]{:S(2)}) collective-permute-start(bf16[256,512]{1,0:T(8,128)(2,1)S(1)} %collective-permute-done.25.refs_4_), channel_id=1, source_target_pairs={{0,4},{4,0},{8,12},{12,8},{16,20},{20,16},{24,28},{28,24},{1,5},{5... | collective-permute-start | bytes 786440 | tf_op jit(solution)/shard_map/ppermute | solution.py:645
  391.0 19.2 %collective-permute-start.37 = (bf16[256,512]{1,0:T(8,128)(2,1)}, bf16[256,512]{1,0:T(8,128)(2,1)S(1)}, u32[]{:S(2)}, u32[]{:S(2)}) collective-permute-start(bf16[256,512]{1,0:T(8,128)(2,1)} %collective-permute-done.26.refs_6_), channel_id=1, source_target_pairs={{0,4},{4,0},{8,12},{12,8},{16,20},{20,16},{24,28},{28,24},{1,5},{5... | collective-permute-start | bytes 786440 | tf_op jit(solution)/shard_map/ppermute | solution.py:645
  394.0 19.8 %collective-permute-start.33 = (f32[12,1024]{1,0:T(8,128)S(1)}, f32[12,1024]{1,0:T(8,128)S(1)}, u32[]{:S(2)}, u32[]{:S(2)}) collective-permute-start(f32[12,1024]{1,0:T(8,128)S(1)} %add.191), channel_id=1, source_target_pairs={{0,16},{4,20},{8,24},{12,28},{16,0},{20,4},{24,8},{28,12},{1,17},{... | collective-permute-start | bytes 147464 | tf_op jit(solution)/shard_map/ppermute | solution.py:849
  (68 other events, 720.3 us)
Sparse Core Ops, SparseCore 0:
  107.2 54.9 all-gather.5
Sparse Core Ops, SparseCore 1:
  142.7 102.7 reduce-scatter.1
  310.2 92.2 all-gather.3
